TPU v7x, 256 devices: a whole 4x4x8 slice. The times are simulated.
256 devices in a mesh: frame: 8 (over z_lo, core), row: 32 (over y, x, z_hi).
Axes of the slice: x: 4, y: 4, z: 8 (z_hi: 2, z_lo: 4; z = z_hi * 4 + z_lo), core: 2. Of those that a mesh axis runs over, the one named last changes fastest.
Arguments:
- latent: bfloat16 [32, 32, 40, 1152], P('frame', 'row'), may hold values from -6 to 6
- mod_spatial: float32 [3, 1152], replicated, may hold values from -3 to 3
- mod_temporal: float32 [3, 1152], replicated, may hold values from -3 to 3
- qk_gain: float32 [4, 72], replicated, may hold values from 0.7 to 6, as said below
- w_qkv_spatial: bfloat16 [1152, 3456], P('row'), may hold values from -0.1875 to 0.1875
- w_out_spatial: bfloat16 [1152, 1152], P('row'), may hold values from -0.1875 to 0.1875
- w_qkv_temporal: bfloat16 [1152, 3456], P('row'), may hold values from -0.1875 to 0.1875
- w_out_temporal: bfloat16 [1152, 1152], P('row'), may hold values from -0.1875 to 0.1875
Outputs:
- mixed: bfloat16 [32, 32, 40, 1152], P('frame', 'row')
Inputs may be any that keep to these rules, and one draw needn't show every extreme that they name: `qk_gain`: gains of the per-head query and key norms.
All inputs are finite; a program needn't handle non-finite values.
Results may differ from a plain program's by a relative error of at most 0.028.
Values may be sent and summed in bfloat16 or wider, within the bound.
No kernel may reach another device: no remote copies, remote signals or barrier semaphores. Data moves between devices by JAX's collectives and lax.ppermute only.
A program may use at most 128 MiB of HBM per device.

v0:
```python
import jax
import jax.numpy as jnp
from jax import lax
from jax.sharding import PartitionSpec as P

HEADS = 16
HDIM = 72


def modulate(tokens_in, modulation):
    values = tokens_in.astype(jnp.float32)
    center = values - jnp.mean(values, -1, keepdims=True)
    variance = jnp.mean(center * center, -1, keepdims=True)
    normed = center * lax.rsqrt(variance + 1e-06)
    return (normed * (1.0 + modulation[1]) + modulation[0]).astype(jnp.bfloat16)


def head_norm(heads_in, gain):
    square = jnp.mean(heads_in * heads_in, -1, keepdims=True)
    return (heads_in * lax.rsqrt(square + 1e-06) * gain).astype(jnp.bfloat16)


def project(flat_in, weight_shard):
    return jnp.dot(
        flat_in,
        lax.all_gather(weight_shard, "row", axis=0, tiled=True),
        preferred_element_type=jnp.float32,
    )


def make_heads(flat_in, weight_shard, gain_query, gain_key):
    qkv = project(flat_in, weight_shard).reshape(flat_in.shape[0], 3, HEADS, HDIM)
    queries = head_norm(qkv[:, 0], gain_query)
    keyset = head_norm(qkv[:, 1], gain_key)
    values = qkv[:, 2].astype(jnp.bfloat16)
    return (queries, keyset, values)


def add_branch(tokens_in, attended_flat, weight_shard, modulation):
    projected = project(attended_flat, weight_shard).reshape(tokens_in.shape)
    return (tokens_in.astype(jnp.float32) + modulation[2] * projected).astype(jnp.bfloat16)


def attend_item(items):
    queries, keyset, values = items
    score_scale = 1.0 / jnp.sqrt(jnp.float32(HDIM))
    scores = (
        jnp.einsum("qd,kd->qk", queries, keyset, preferred_element_type=jnp.float32) * score_scale
    )
    highest = jnp.max(scores, -1, keepdims=True)
    expo = jnp.exp(scores - highest)
    probabilities = (expo / jnp.sum(expo, -1, keepdims=True)).astype(jnp.bfloat16)
    return jnp.dot(probabilities, values, preferred_element_type=jnp.float32).astype(jnp.bfloat16)


def spatial_attend(triple):
    queries, keyset, values = triple
    return lax.map(attend_item, (queries[0], keyset[0], values[0]))[None]


def temporal_attend(triple):
    queries, keyset, values = triple
    score_scale = 1.0 / jnp.sqrt(jnp.float32(HDIM))
    scores = (
        jnp.einsum("fphd,gphd->phfg", queries, keyset, preferred_element_type=jnp.float32)
        * score_scale
    )
    highest = jnp.max(scores, -1, keepdims=True)
    expo = jnp.exp(scores - highest)
    probabilities = (expo / jnp.sum(expo, -1, keepdims=True)).astype(jnp.bfloat16)
    return jnp.einsum(
        "phfg,gphd->fphd", probabilities, values, preferred_element_type=jnp.float32
    ).astype(jnp.bfloat16)


def per_device(
    latent,
    mod_spatial,
    mod_temporal,
    qk_gain,
    w_qkv_spatial,
    w_out_spatial,
    w_qkv_temporal,
    w_out_temporal,
):
    frames_dev, rows_dev, columns_dev, model_width = latent.shape
    row_tokens = rows_dev * columns_dev
    tokens = frames_dev * row_tokens
    n_row = lax.axis_size("row")
    modulated = modulate(latent, mod_spatial).reshape(tokens, model_width)
    queries, keyset, values = make_heads(modulated, w_qkv_spatial, qk_gain[0], qk_gain[1])

    def to_spatial(heads_in):
        grouped = heads_in.reshape(frames_dev, row_tokens, HEADS, HDIM).transpose(0, 2, 1, 3)
        return grouped.reshape(n_row, frames_dev * HEADS // n_row, row_tokens, HDIM)

    attended = spatial_attend(
        (
            lax.all_to_all(to_spatial(queries), "row", split_axis=0, concat_axis=2, tiled=True),
            lax.all_to_all(to_spatial(keyset), "row", split_axis=0, concat_axis=2, tiled=True),
            lax.all_to_all(to_spatial(values), "row", split_axis=0, concat_axis=2, tiled=True),
        )
    )
    returned = lax.all_to_all(attended, "row", split_axis=2, concat_axis=0, tiled=True)
    returned = (
        returned.reshape(frames_dev, HEADS, row_tokens, HDIM)
        .transpose(0, 2, 1, 3)
        .reshape(tokens, model_width)
    )
    hidden = add_branch(latent, returned, w_out_spatial, mod_spatial)
    modulated = modulate(hidden, mod_temporal).reshape(tokens, model_width)
    queries, keyset, values = make_heads(modulated, w_qkv_temporal, qk_gain[2], qk_gain[3])
    clip_shape = (frames_dev, row_tokens, HEADS, HDIM)
    attended = temporal_attend(
        (
            lax.all_to_all(
                queries.reshape(clip_shape), "frame", split_axis=2, concat_axis=0, tiled=True
            ),
            lax.all_to_all(
                keyset.reshape(clip_shape), "frame", split_axis=2, concat_axis=0, tiled=True
            ),
            lax.all_to_all(
                values.reshape(clip_shape), "frame", split_axis=2, concat_axis=0, tiled=True
            ),
        )
    )
    returned = lax.all_to_all(attended, "frame", split_axis=0, concat_axis=2, tiled=True)
    return add_branch(hidden, returned.reshape(tokens, model_width), w_out_temporal, mod_temporal)


def solution(mesh):
    in_specs = (
        P("frame", "row", None, None),
        P(),
        P(),
        P(),
        P("row", None),
        P("row", None),
        P("row", None),
        P("row", None),
    )
    out_specs = P("frame", "row", None, None)
    return jax.shard_map(
        per_device, mesh=mesh, in_specs=in_specs, out_specs=out_specs, check_vma=False
    )
```

profile of v0, /device:TPU:1, one launch (start us, length us, event | category | flops | bytes accessed | tf_op | source)
XLA Modules:
  0.0 611.7 jit_solution(17563455642418169414)
XLA Ops:
  11.3 162.1 %all-gather.9.cloned.1.call-done = bf16[32,36,3456]{2,1,0:T(8,128)(2,1)} async-done(((bf16[1,36,3456]{2,1,0:T(8,128)(2,1)}), bf16[32,36,3456]{2,1,0:T(8,128)(2,1)}) %all-gather.9.cloned.1.call-update) | async-done | bytes 7962640 | tf_op jit(solution)/shard_map/all_gather | solution.py:26
  173.4 12.5 %reshape.210 = bf16[1152,3456]{1,0:T(8,128)(2,1)} reshape(bf16[32,36,3456]{2,1,0:T(8,128)(2,1)} %all-gather.9.cloned.1.call-done) | data formatting | bytes 15925248
  185.9 11.5 %copy.64 = bf16[3456,1152]{1,0:T(8,128)(2,1)} copy(bf16[3456,1152]{0,1:T(8,128)(2,1)} %bitcast.147) | data formatting | bytes 15925248 | tf_op jit(solution)/shard_map/dot_general | solution.py:24
  197.4 5.8 fusion.39
  209.1 5.3 all-to-all-start.1
  216.7 17.1 %all-to-all-done.1 = bf16[32,2,40,72]{3,2,1,0:T(8,128)(2,1)S(1)} async-done(((bf16[32,2,40,72]{3,2,1,0:T(8,128)(2,1)}), bf16[32,2,40,72]{3,2,1,0:T(8,128)(2,1)S(1)}, u32[]{:S(2)}, u32[]{:S(2)}) %all-to-all-start.1) | async-done | bytes 368672 | tf_op jit(solution)/shard_map/all_to_all | solution.py:100
  233.7 3.9 all-to-all-start
  240.6 29.0 %all-to-all-done = bf16[32,2,40,72]{3,2,1,0:T(8,128)(2,1)S(1)} async-done(((bf16[32,2,40,72]{3,2,1,0:T(8,128)(2,1)}), bf16[32,2,40,72]{3,2,1,0:T(8,128)(2,1)S(1)}, u32[]{:S(2)}, u32[]{:S(2)}) %all-to-all-start) | async-done | bytes 368672 | tf_op jit(solution)/shard_map/all_to_all | solution.py:99
  269.6 4.8 all-to-all-start.2
  274.6 14.1 %all-to-all-done.2 = bf16[32,2,40,72]{3,2,1,0:T(8,128)(2,1)} async-done(((bf16[32,2,40,72]{3,2,1,0:T(8,128)(2,1)}), bf16[32,2,40,72]{3,2,1,0:T(8,128)(2,1)}, u32[]{:S(2)}, u32[]{:S(2)}) %all-to-all-start.2) | async-done | bytes 368672 | tf_op jit(solution)/shard_map/all_to_all | solution.py:101
  289.8 6.5 %while.10 = (s32[]{:T(128)}, bf16[2,1280,72]{1,2,0:T(8,128)(2,1)S(1)}, bf16[2,1280,72]{2,1,0:T(8,128)(2,1)S(1)}, bf16[2,1280,72]{2,1,0:T(8,128)(2,1)S(1)}, bf16[2,1280,72]{2,1,0:T(8,128)(2,1)S(1)}, /*index=5*/s32[]{:T(128)}) while((s32[]{:T(128)}, bf16[2,1280,72]{1,2,0:T(8,128)(2,1)S(1)}, bf16[2,1280,72]{2,1,0:T(8,128)(2,1)S(1)}, ...), condition=%wide.region_7.8_spmd, body=%wide.region_4.7_spmd.sunk | while | flops 483417600 | bytes 20862020 | solution.py:58
  297.6 3.9 all-to-all-start.3
  305.7 143.4 %all-gather.13.cloned.1.call-done = bf16[32,36,3456]{2,1,0:T(8,128)(2,1)} async-done(((bf16[1,36,3456]{2,1,0:T(8,128)(2,1)}), bf16[32,36,3456]{2,1,0:T(8,128)(2,1)}) %all-gather.13.cloned.1.call-update) | async-done | bytes 7962640 | tf_op jit(solution)/shard_map/all_gather | solution.py:26
  449.1 12.4 %reshape.214 = bf16[1152,3456]{1,0:T(8,128)(2,1)} reshape(bf16[32,36,3456]{2,1,0:T(8,128)(2,1)} %all-gather.13.cloned.1.call-done) | data formatting | bytes 15925248
  461.5 11.5 %copy.80 = bf16[3456,1152]{1,0:T(8,128)(2,1)} copy(bf16[3456,1152]{0,1:T(8,128)(2,1)} %bitcast.148) | data formatting | bytes 15925248 | tf_op jit(solution)/shard_map/dot_general | solution.py:24
  477.1 5.8 fusion.40
  488.6 5.2 all-to-all-start.6
  496.1 15.1 %all-to-all-done.6 = bf16[4,40,16,72]{3,1,0,2:T(8,128)(2,1)} async-done(((bf16[4,40,16,72]{3,1,0,2:T(8,128)(2,1)}), bf16[4,40,16,72]{3,1,0,2:T(8,128)(2,1)}, u32[]{:S(2)}, u32[]{:S(2)}) %all-to-all-start.6) | async-done | bytes 368672 | tf_op jit(solution)/shard_map/all_to_all | solution.py:119
  511.2 4.3 all-to-all-start.5
  518.0 30.9 %all-to-all-done.5 = bf16[4,40,16,72]{3,1,0,2:T(8,128)(2,1)S(1)} async-done(((bf16[4,40,16,72]{3,1,0,2:T(8,128)(2,1)}), bf16[4,40,16,72]{3,1,0,2:T(8,128)(2,1)S(1)}, u32[]{:S(2)}, u32[]{:S(2)}) %all-to-all-start.5) | async-done | bytes 368672 | tf_op jit(solution)/shard_map/all_to_all | solution.py:116
  548.9 3.9 all-to-all-start.4
  554.6 15.5 %all-to-all-done.4 = bf16[4,40,16,72]{3,1,0,2:T(8,128)(2,1)S(1)} async-done(((bf16[4,40,16,72]{3,1,0,2:T(8,128)(2,1)}), bf16[4,40,16,72]{3,1,0,2:T(8,128)(2,1)S(1)}, u32[]{:S(2)}, u32[]{:S(2)}) %all-to-all-start.4) | async-done | bytes 368672 | tf_op jit(solution)/shard_map/all_to_all | solution.py:122
  575.4 4.9 all-to-all-start.7
  584.0 13.8 %all-to-all-done.7 = bf16[32,40,2,72]{3,2,1,0:T(2,128)(2,1)} async-done(((bf16[32,40,2,72]{3,2,1,0:T(2,128)(2,1)}), bf16[32,40,2,72]{3,2,1,0:T(2,128)(2,1)}, u32[]{:S(2)}, u32[]{:S(2)}) %all-to-all-start.7) | async-done | bytes 368672 | tf_op jit(solution)/shard_map/all_to_all | solution.py:127
  (87 shorter events, 61.5 us)
Async XLA Ops:
  6.5 4.2 copy-start
  6.5 4.5 copy-start.4
  6.5 166.9 %all-gather.9.cloned.1.call-start = ((), (), s32[]{:S(2)}) async-start(), calls=%async_computation.8 | async-start | bytes 9123840 | tf_op jit(solution)/shard_map/all_gather | solution.py:26
  7.3 294.9 %all-gather.11.cloned.1.call-start = ((), (), s32[]{:S(2)}) async-start(), calls=%async_computation.9 | async-start | bytes 3041280 | tf_op jit(solution)/shard_map/all_gather | solution.py:26
  8.0 441.1 %all-gather.13.cloned.1.call-start = ((), (), s32[]{:S(2)}) async-start(), calls=%async_computation.10 | async-start | bytes 9123840 | tf_op jit(solution)/shard_map/all_gather | solution.py:26
  203.2 2.2 copy-start.1
  209.1 24.7 %all-to-all-start.1 = ((bf16[32,2,40,72]{3,2,1,0:T(8,128)(2,1)}), bf16[32,2,40,72]{3,2,1,0:T(8,128)(2,1)S(1)}, u32[]{:S(2)}, u32[]{:S(2)}) async-start(bf16[32,2,40,72]{3,2,1,0:T(8,128)(2,1)} %bitcast.23), calls=%async_computation.1 | async-start | bytes 1310720 | tf_op jit(solution)/shard_map/all_to_all | solution.py:100
  233.7 35.9 %all-to-all-start = ((bf16[32,2,40,72]{3,2,1,0:T(8,128)(2,1)}), bf16[32,2,40,72]{3,2,1,0:T(8,128)(2,1)S(1)}, u32[]{:S(2)}, u32[]{:S(2)}) async-start(bf16[32,2,40,72]{3,2,1,0:T(8,128)(2,1)} %bitcast.15), calls=%async_computation | async-start | bytes 1310720 | tf_op jit(solution)/shard_map/all_to_all | solution.py:99
  269.6 19.0 %all-to-all-start.2 = ((bf16[32,2,40,72]{3,2,1,0:T(8,128)(2,1)}), bf16[32,2,40,72]{3,2,1,0:T(8,128)(2,1)}, u32[]{:S(2)}, u32[]{:S(2)}) async-start(bf16[32,2,40,72]{3,2,1,0:T(8,128)(2,1)} %bitcast.29), calls=%async_computation.2 | async-start | bytes 1310720 | tf_op jit(solution)/shard_map/all_to_all | solution.py:101
  296.3 5.7 copy-start.3
  297.6 175.5 %all-to-all-start.3 = ((bf16[1,2,1280,72]{3,1,0,2:T(2,128)(2,1)}), bf16[1,2,1280,72]{3,1,0,2:T(2,128)(2,1)S(1)}, u32[]{:S(2)}, u32[]{:S(2)}) async-start(bf16[1,2,1280,72]{3,1,0,2:T(2,128)(2,1)} %bitcast.33), calls=%async_computation.3 | async-start | bytes 1310720 | tf_op jit(solution)/shard_map/all_to_all | solution.py:104
  301.5 278.9 %all-gather.15.cloned.1.call-start = ((), (), s32[]{:S(2)}) async-start(), calls=%async_computation.11 | async-start | bytes 3041280 | tf_op jit(solution)/shard_map/all_gather | solution.py:26
  482.9 2.1 copy-start.2
  488.6 22.6 %all-to-all-start.6 = ((bf16[4,40,16,72]{3,1,0,2:T(8,128)(2,1)}), bf16[4,40,16,72]{3,1,0,2:T(8,128)(2,1)}, u32[]{:S(2)}, u32[]{:S(2)}) async-start(bf16[4,40,16,72]{3,1,0,2:T(8,128)(2,1)} %copy.90), calls=%async_computation.6 | async-start | bytes 1310720 | tf_op jit(solution)/shard_map/all_to_all | solution.py:119
  511.2 37.7 %all-to-all-start.5 = ((bf16[4,40,16,72]{3,1,0,2:T(8,128)(2,1)}), bf16[4,40,16,72]{3,1,0,2:T(8,128)(2,1)S(1)}, u32[]{:S(2)}, u32[]{:S(2)}) async-start(bf16[4,40,16,72]{3,1,0,2:T(8,128)(2,1)} %copy.86), calls=%async_computation.5 | async-start | bytes 1310720 | tf_op jit(solution)/shard_map/all_to_all | solution.py:116
  548.9 21.2 %all-to-all-start.4 = ((bf16[4,40,16,72]{3,1,0,2:T(8,128)(2,1)}), bf16[4,40,16,72]{3,1,0,2:T(8,128)(2,1)S(1)}, u32[]{:S(2)}, u32[]{:S(2)}) async-start(bf16[4,40,16,72]{3,1,0,2:T(8,128)(2,1)} %bitcast.47), calls=%async_computation.4 | async-start | bytes 1310720 | tf_op jit(solution)/shard_map/all_to_all | solution.py:122
  575.4 22.4 %all-to-all-start.7 = ((bf16[32,40,2,72]{3,2,1,0:T(2,128)(2,1)}), bf16[32,40,2,72]{3,2,1,0:T(2,128)(2,1)}, u32[]{:S(2)}, u32[]{:S(2)}) async-start(bf16[32,40,2,72]{3,2,1,0:T(2,128)(2,1)} %copy.93), calls=%async_computation.7 | async-start | bytes 1310720 | tf_op jit(solution)/shard_map/all_to_all | solution.py:127
Sparse Core Ops, SparseCore 0:
  10.9 162.5 all-gather.8
  176.9 111.0 all-gather.10
  291.6 157.4 all-gather.12
  452.5 103.9 all-gather.14
where the time goes:
time: 614 us; the launch traced here: 612 us
  waiting for transfers between devices  444 us (72%)
  local copies, waits for them, and re-layouts  85.4 us (14%)
  starting transfers between devices  36.3 us (6%)
  matrix products  23.3 us (4%)
  between operations  13.5 us (2%)
  other arithmetic  9.61 us (2%)
    all_gather x4, waiting for transfers between devices, project(): lax.all_gather(weight_shard, 'row', axis=0, tiled=True)  305 us
    unnamed x14, local copies, waits for them, and re-layouts  33.4 us
    all_to_all x1, waiting for transfers between devices, per_device(): lax.all_to_all(queries.reshape(clip_shape), 'frame', split_axis=2, concat...  30.9 us
    all_to_all x1, waiting for transfers between devices, per_device(): lax.all_to_all(to_spatial(queries), 'row', split_axis=0, concat_axis=2, t...  29 us
    dot_general x4, local copies, waits for them, and re-layouts, project(): jnp.dot(flat_in, lax.all_gather(weight_shard, 'row', axis=0, tiled=True),...  27 us
    all_to_all x1, waiting for transfers between devices, per_device(): lax.all_to_all(to_spatial(keyset), 'row', split_axis=0, concat_axis=2, ti...  17.1 us
    dot_general x4, matrix products, project(): jnp.dot(flat_in, lax.all_gather(weight_shard, 'row', axis=0, tiled=True),...  15.9 us
    all_to_all x1, waiting for transfers between devices, per_device(): lax.all_to_all(values.reshape(clip_shape), 'frame', split_axis=2, concat_...  15.5 us
  transfers between devices with their start and end apart: 12, of which 9 were waited for; matrix products, arithmetic and copies ran while one was open for 18% of the time, Pallas kernels for 0%

commit v1 on v0

v1 whole, which is shorter than its diff:
```python
import jax
import jax.numpy as jnp
from jax import lax
from jax.sharding import Mesh
from jax.sharding import PartitionSpec as P

HEADS = 16
HDIM = 72
D = 1152


def modulate(tokens_in, modulation):
    values = tokens_in.astype(jnp.float32)
    center = values - jnp.mean(values, -1, keepdims=True)
    variance = jnp.mean(center * center, -1, keepdims=True)
    normed = center * lax.rsqrt(variance + 1e-06)
    return (normed * (1.0 + modulation[1]) + modulation[0]).astype(jnp.bfloat16)


def head_norm(heads_in, gain):
    square = jnp.mean(heads_in * heads_in, -1, keepdims=True)
    return (heads_in * lax.rsqrt(square + 1e-06) * gain).astype(jnp.bfloat16)


def softmax(scores):
    highest = jnp.max(scores, -1, keepdims=True)
    expo = jnp.exp(scores - highest)
    return (expo / jnp.sum(expo, -1, keepdims=True)).astype(jnp.bfloat16)


def dot32(a, b):
    return jnp.dot(a, b, preferred_element_type=jnp.float32)


def spatial_attend(tokens, weight, gain_q, gain_k):
    qkv = dot32(tokens, weight).reshape(tokens.shape[0], 3, 2, HDIM)
    scale = 1.0 / jnp.sqrt(jnp.float32(HDIM))
    outs = []
    for head in range(2):
        q = head_norm(qkv[:, 0, head], gain_q)
        k = head_norm(qkv[:, 1, head], gain_k)
        v = qkv[:, 2, head].astype(jnp.bfloat16)
        probs = softmax(jnp.einsum("qd,kd->qk", q, k, preferred_element_type=jnp.float32) * scale)
        outs.append(dot32(probs, v).astype(jnp.bfloat16))
    return jnp.concatenate(outs, -1)


def temporal_attend(qkv, gain_q, gain_k):
    q = head_norm(qkv[:, :, 0], gain_q)
    k = head_norm(qkv[:, :, 1], gain_k)
    v = qkv[:, :, 2].astype(jnp.bfloat16)
    scale = 1.0 / jnp.sqrt(jnp.float32(HDIM))
    scores = jnp.einsum("fphd,gphd->phfg", q, k, preferred_element_type=jnp.float32) * scale
    probs = softmax(scores)
    return jnp.einsum("phfg,gphd->fphd", probs, v, preferred_element_type=jnp.float32).astype(
        jnp.bfloat16
    )


def per_device(latent, mod_s, mod_t, gain, wqkv_s, wout_s, wqkv_t, wout_t):
    core = lax.axis_index("core")
    zh = lax.axis_index("zh")
    by_pair = wqkv_s.reshape(36, 3, 4, 2, 2 * HDIM)
    half_s = lax.dynamic_index_in_dim(by_pair, core, 3, keepdims=False)
    half_s = half_s.transpose(0, 2, 1, 3).reshape(36, 4 * 432)
    rest = jnp.concatenate([wout_s, wqkv_t, wout_t, jnp.zeros((36, 128), jnp.bfloat16)], 1)
    half_r = lax.dynamic_slice_in_dim(rest, core * 2944, 2944, 1)

    modulated = modulate(latent, mod_s).reshape(4, 40, D)
    y = lax.axis_index("y")
    swap = [(c * 2 + z, z * 2 + c) for c in range(2) for z in range(2)]
    swapped = lax.ppermute(modulated, ("core", "zh"), swap)
    frame_rows = lax.all_to_all(swapped, "y", split_axis=0, concat_axis=0, tiled=True)

    mine = jnp.concatenate([half_s, half_r], 1)
    other = lax.ppermute(mine, "zh", [(0, 1), (1, 0)])
    low = jnp.where(zh == 0, mine, other)
    high = jnp.where(zh == 0, other, mine)
    both = jnp.concatenate([low, high], 0)
    both_s = both[:, :1728].reshape(72, 4, 432).transpose(1, 0, 2)
    both_s = jnp.broadcast_to(both_s[None], (4, 4, 72, 432)).reshape(16, 72, 432)
    w_s = lax.all_to_all(both_s, ("y", "x"), split_axis=0, concat_axis=0, tiled=True)
    w_s = w_s.reshape(D, 432)

    gathered = lax.all_gather(both[:, 1728:], ("y", "x"), axis=0, tiled=True)
    pair = lax.ppermute(gathered, "core", [(0, 1), (1, 0)])
    w0 = jnp.where(core == 0, gathered, pair)
    w1 = jnp.where(core == 0, pair, gathered)
    wo_s = w0[:, :D]

    frame_rows = frame_rows.reshape(160, D)
    in_x = lax.all_to_all(
        jnp.broadcast_to(frame_rows[None], (4, 160, D)), "x", split_axis=0, concat_axis=0, tiled=True
    )
    in_core = lax.ppermute(in_x, "core", [(0, 1), (1, 0)])
    tok = jnp.concatenate([in_x, in_core], 0).reshape(1280, D)

    attended = spatial_attend(tok, w_s, gain[0], gain[1])
    att = attended.reshape(2, 4, 4, 4, 2, 5, 2 * HDIM)
    att = jnp.where(core == 0, att, att[::-1])
    att = att.transpose(3, 0, 2, 1, 4, 5, 6).reshape(256, 5, 2 * HDIM)
    everyone = ("zl", "zh", "y", "x", "core")
    back = lax.all_to_all(att, everyone, split_axis=0, concat_axis=0, tiled=True)
    back = back.reshape(32, 8, 5, 2 * HDIM).transpose(0, 2, 1, 3).reshape(160, D)

    home = lax.all_to_all(
        latent.reshape(4, 40, D), ("zl", "core"), split_axis=1, concat_axis=0, tiled=True
    )
    residual = home.reshape(160, D).astype(jnp.float32)
    hidden = (residual + mod_s[2] * dot32(back, wo_s)).astype(jnp.bfloat16)

    modulated = modulate(hidden, mod_t)
    qkv = jnp.concatenate(
        [dot32(modulated, w0[:, D:]), dot32(modulated, w1[:, : 3 * D - 1792])], 1
    ).reshape(32, 5, 3, HEADS, HDIM)
    att_t = temporal_attend(qkv, gain[2], gain[3]).reshape(160, D)
    wo_t = w1[:, 3 * D - 1792 : 4 * D - 1792]
    mixed = (hidden.astype(jnp.float32) + mod_t[2] * dot32(att_t, wo_t)).astype(jnp.bfloat16)
    mixed = lax.all_to_all(
        mixed.reshape(32, 5, D), ("zl", "core"), split_axis=0, concat_axis=1, tiled=True
    )
    return mixed.reshape(4, 1, 40, D)


def solution(mesh):
    fine = Mesh(mesh.devices.reshape(4, 2, 4, 4, 2), ("zl", "core", "y", "x", "zh"))
    frame, row = ("zl", "core"), ("y", "x", "zh")
    in_specs = (
        P(frame, row, None, None),
        P(),
        P(),
        P(),
        P(row, None),
        P(row, None),
        P(row, None),
        P(row, None),
    )
    return jax.shard_map(
        per_device,
        mesh=fine,
        in_specs=in_specs,
        out_specs=P(frame, row, None, None),
        check_vma=False,
    )
```

time: 614 us -> 226 us (0.37)
  waiting for transfers between devices: 444 us -> 69.7 us
  local copies, waits for them, and re-layouts: 85.4 us -> 22.7 us
  blocking collectives: 0 us -> 47.2 us
  matrix products: 23.3 us -> 16.4 us
  starting transfers between devices: 36.3 us -> 42.5 us
    all_gather x4 -> x1, waiting for transfers between devices: 305 us -> 37.1 us  [per_device(): gathered = lax.all_gather(both[:, 1728:], ('y', 'x'), axis=0, tiled=True)]
    all_to_all x8 -> x3, waiting for transfers between devices: 135 us -> 18.3 us  [the longest x1 18.2 us: per_device(): lax.all_to_all(att, everyone, split_axis=0, concat_axis=0, tiled=True)]
    all_to_all x0 -> x3, blocking collectives: none -> 47.2 us  [the longest x1 18.9 us: per_device(): lax.all_to_all(mixed.reshape(32, 5, D), ('zl', 'core'), split_axis=0, con...]
    unnamed x14 -> x21, local copies, waits for them, and re-layouts: 33.4 us -> 4.27 us
    dot_general x4 -> x1, local copies, waits for them, and re-layouts: 27 us -> 1.5 us  [dot32(): return jnp.dot(a, b, preferred_element_type=jnp.float32)]
    ppermute x0 -> x4, starting transfers between devices: none -> 23.9 us  [the longest x1 15.4 us: per_device(): swapped = lax.ppermute(modulated, ('core', 'zh'), swap)]
    all_to_all x8 -> x3, starting transfers between devices: 36.2 us -> 18.6 us  [the longest x1 9.95 us: per_device(): lax.all_to_all(att, everyone, split_axis=0, concat_axis=0, tiled=True)]
    ppermute x0 -> x4, waiting for transfers between devices: none -> 14.3 us  [the longest x1 9.01 us: per_device(): other = lax.ppermute(mine, 'zh', [(0, 1), (1, 0)])]
  transfers between devices with their start and end apart: 12 -> 8, of which waited for: 9 -> 4; matrix products, arithmetic and copies ran while one was open for 18% -> 9% of each run, Pallas kernels for 0% -> 0%
where the time goes in v1:
time: 226 us
  waiting for transfers between devices  69.7 us (31%)
  blocking collectives  47.2 us (21%)
  starting transfers between devices  42.5 us (19%)
  local copies, waits for them, and re-layouts  22.7 us (10%)
  matrix products  16.4 us (7%)
  between operations  13.9 us (6%)
  other arithmetic  13.6 us (6%)
    all_gather x1, waiting for transfers between devices, per_device(): gathered = lax.all_gather(both[:, 1728:], ('y', 'x'), axis=0, tiled=True)  37.1 us
    all_to_all x1, blocking collectives, per_device(): lax.all_to_all(mixed.reshape(32, 5, D), ('zl', 'core'), split_axis=0, con...  18.9 us
    all_to_all x1, waiting for transfers between devices, per_device(): lax.all_to_all(att, everyone, split_axis=0, concat_axis=0, tiled=True)  18.2 us
    all_to_all x1, blocking collectives, per_device(): lax.all_to_all(jnp.broadcast_to(frame_rows[None], (4, 160, D)), 'x', spli...  17.9 us
    ppermute x1, starting transfers between devices, per_device(): swapped = lax.ppermute(modulated, ('core', 'zh'), swap)  15.4 us
    all_to_all x1, blocking collectives, per_device(): lax.all_to_all(swapped, 'y', split_axis=0, concat_axis=0, tiled=True)  10.4 us
    all_to_all x1, starting transfers between devices, per_device(): lax.all_to_all(att, everyone, split_axis=0, concat_axis=0, tiled=True)  9.95 us
    dot_general x7, matrix products, dot32(): return jnp.dot(a, b, preferred_element_type=jnp.float32)  9.36 us
  transfers between devices with their start and end apart: 8, of which 4 were waited for; matrix products, arithmetic and copies ran while one was open for 9% of the time, Pallas kernels for 0%

profile of v1, /device:TPU:1, one launch (start us, length us, event | category | flops | bytes accessed | tf_op | source)
XLA Modules:
  0.0 225.9 jit_solution(15467189855522036032)
XLA Ops:
  6.5 1.6 reshape.223
  9.6 7.8 %collective-permute-start.2 = (bf16[36,4672]{1,0:T(8,128)(2,1)S(1)}, bf16[36,4672]{1,0:T(8,128)(2,1)S(1)}, u32[]{:S(2)}, u32[]{:S(2)}) collective-permute-start(bf16[36,4672]{1,0:T(8,128)(2,1)S(1)} %pad_maximum_fusion.3), channel_id=1, source_target_pairs={{0,1},{1,0},{2,3},{3,2},{4,5},{5,4},{6,7},{7,6},{8,9},{9,8},{10,11... | collective-permute-start | bytes 1009160 | tf_op jit(solution)/shard_map/ppermute | solution.py:76
  17.5 9.0 %collective-permute-done.2 = bf16[36,4672]{1,0:T(8,128)(2,1)S(1)} collective-permute-done((bf16[36,4672]{1,0:T(8,128)(2,1)S(1)}, bf16[36,4672]{1,0:T(8,128)(2,1)S(1)}, u32[]{:S(2)}, u32[]{:S(2)}) %collective-permute-start.2) | collective-permute-done | bytes 336416 | tf_op jit(solution)/shard_map/ppermute | solution.py:76
  28.5 15.4 %collective-permute-start = (bf16[4,40,1152]{2,1,0:T(8,128)(2,1)S(1)}, bf16[4,40,1152]{2,1,0:T(8,128)(2,1)S(1)}, u32[]{:S(2)}, u32[]{:S(2)}) collective-permute-start(bf16[4,40,1152]{2,1,0:T(8,128)(2,1)S(1)} %fusion.53), channel_id=1, source_target_pairs={{0,0},{1,32},{32,1},{33,33},{2,2},{3,34},{34,3},{35,35},{4,4},{5,3... | collective-permute-start | bytes 1105928 | tf_op jit(solution)/shard_map/ppermute | solution.py:72
  43.8 5.3 %collective-permute-done = bf16[4,40,1152]{2,1,0:T(8,128)(2,1)S(1)} collective-permute-done((bf16[4,40,1152]{2,1,0:T(8,128)(2,1)S(1)}, bf16[4,40,1152]{2,1,0:T(8,128)(2,1)S(1)}, u32[]{:S(2)}, u32[]{:S(2)}) %collective-permute-start) | collective-permute-done | bytes 368672 | tf_op jit(solution)/shard_map/ppermute | solution.py:72
  49.1 10.4 %all_to_all.44 = bf16[4,40,1152]{2,1,0:T(8,128)(2,1)S(1)} all-to-all(bf16[4,40,1152]{2,1,0:T(8,128)(2,1)S(1)} %collective-permute-done), channel_id=1, replica_groups=mesh['zl'=4,'core'=2,'y'=4,'x'=4,'zh'=2] {'y'}, dimensions={0} | all-to-all | bytes 737280 | tf_op jit(solution)/shard_map/all_to_all | solution.py:73
  59.7 17.9 %all_to_all.45 = bf16[4,160,1152]{2,1,0:T(8,128)(2,1)S(1)} all-to-all(bf16[4,160,1152]{2,1,0:T(8,128)(2,1)S(1)} %broadcast_in_dim.9), channel_id=1, replica_groups=mesh['zl'=4,'core'=2,'y'=4,'x'=4,'zh'=2] {'x'}, dimensions={0} | all-to-all | bytes 2949120 | tf_op jit(solution)/shard_map/all_to_all | solution.py:92
  79.3 3.7 %all-to-all-start.3 = ((bf16[16,72,432]{2,1,0:T(8,128)(2,1)}), bf16[16,72,432]{2,1,0:T(8,128)(2,1)S(1)}, u32[]{:S(2)}, u32[]{:S(2)}) async-start(bf16[16,72,432]{2,1,0:T(8,128)(2,1)} %bitcast.103), calls=%async_computation.3 | async-start | bytes 2359296 | tf_op jit(solution)/shard_map/all_to_all | solution.py:82
  83.0 37.1 %all-gather.2.cloned.1.call-done = bf16[1152,2944]{1,0:T(8,128)(2,1)} async-done(((bf16[72,2944]{1,0:T(8,128)(2,1)}), bf16[1152,2944]{1,0:T(8,128)(2,1)}) %all-gather.2.cloned.1.call-update) | async-done | bytes 6782992 | tf_op jit(solution)/shard_map/all_gather | solution.py:85
  121.6 4.9 %all-to-all-start = ((bf16[4,40,1152]{2,0,1:T(4,128)(2,1)}), bf16[4,40,1152]{2,0,1:T(4,128)(2,1)S(1)}, u32[]{:S(2)}, u32[]{:S(2)}) async-start(bf16[4,40,1152]{2,0,1:T(4,128)(2,1)} %bitcast.111), calls=%async_computation | async-start | bytes 737280 | tf_op jit(solution)/shard_map/all_to_all | solution.py:106
  126.6 1.5 copy.36
  128.1 1.8 pad_maximum_fusion
  129.8 1.7 fusion.75
  139.3 1.7 reshape.245
  141.1 10.0 %all-to-all-start.4 = ((bf16[256,2,360]{2,1,0:T(2,128)(2,1)}), bf16[256,2,360]{2,1,0:T(2,128)(2,1)S(1)}, u32[]{:S(2)}, u32[]{:S(2)}) async-start(bf16[256,2,360]{2,1,0:T(2,128)(2,1)} %reshape.245), calls=%async_computation.4 | async-start | bytes 786432 | tf_op jit(solution)/shard_map/all_to_all | solution.py:103
  151.5 18.2 %all-to-all-done.4 = bf16[256,2,360]{2,1,0:T(2,128)(2,1)S(1)} async-done(((bf16[256,2,360]{2,1,0:T(2,128)(2,1)}), bf16[256,2,360]{2,1,0:T(2,128)(2,1)S(1)}, u32[]{:S(2)}, u32[]{:S(2)}) %all-to-all-start.4) | async-done | bytes 368672 | tf_op jit(solution)/shard_map/all_to_all | solution.py:103
  171.4 5.7 %broadcast_select_fusion = (bf16[1152,2944]{1,0:T(8,128)(2,1)S(1)}, bf16[1152,2944]{1,0:T(8,128)(2,1)S(1)}) fusion(bf16[1152,2944]{1,0:T(8,128)(2,1)} %collective-permute-done.3, bf16[1152,2944]{1,0:T(8,128)(2,1)} %all-gather.2.cloned.1.call-done, pred[]{:T(512)S(6)} %eq.4), kind=kLoop, calls=%fused_computation.3 | loop fusion | flops 6782976 | bytes 27131904 | tf_op jit(solution)/shard_map/jit(_where)/select_n | solution.py:88
  181.1 4.6 %reshape.232 = f32[32,5,3,16,72]{4,3,2,1,0:T(8,128)} reshape(f32[160,3456]{1,0:T(8,128)S(1)} %pad_maximum_fusion.1) | data formatting | bytes 4423680 | tf_op jit(solution)/shard_map/reshape | solution.py:115
  185.6 1.9 fusion.73
  187.6 2.3 %slice.118 = bf16[32,5,1,16,72]{4,3,2,1,0:T(8,128)(2,1)} slice(f32[32,5,3,16,72]{4,3,2,1,0:T(8,128)} %reshape.232), slice={[0:32], [0:5], [2:3], [0:16], [0:72]} | slice | bytes 737280 | tf_op jit(solution)/shard_map/slice | solution.py:51
  190.9 2.8 %fusion.78 = (f32[5,16,32]{2,1,0:T(8,128)S(1)}, f32[5,16,32,32]{2,3,1,0:T(8,128)}) fusion(f32[32,5,1,16,72]{4,3,2,1,0:T(8,128)S(1)} %get-tuple-element.18, f32[32,5,1,16,72]{4,3,2,1,0:T(8,128)S(1)} %get-tuple-element.17, f32[72]{0:T(128)S(1)} %get-tuple-element.24, f32[32,5,16]{0,2,1:T(8,128)S(1)} %add_rsqrt_fusion, f32[72]{0:T(128)S(1)} %get-tuple-element.21, ...), kind=kOutput, calls=%fused_computation.129 | convolution fusion | flops 13148191 | bytes 1833536 | tf_op jit(solution)/shard_map/sub | solution.py:27
  193.7 1.9 fusion.38
  196.6 2.5 %fusion.25 = bf16[160,1152]{1,0:T(8,128)(2,1)S(1)} fusion(f32[160,1152]{1,0:T(8,128)S(1)} %get-tuple-element.32, bf16[160,1152]{1,0:T(8,128)(2,1)S(1)} %reshape.233, bf16[1152,2944]{1,0:T(8,128)(2,1)} %copy-done, f32[1152]{0:T(1024)S(1)} %get-tuple-element.9), kind=kOutput, calls=%fused_computation.26 | convolution fusion | flops 425226240 | bytes 4133376 | tf_op jit(solution)/shard_map/dot_general | solution.py:32
  199.2 18.9 %all_to_all.46 = bf16[32,5,1152]{2,1,0:T(8,128)(2,1)S(1)} all-to-all(bf16[32,5,1152]{2,1,0:T(8,128)(2,1)S(1)} %reshape.234), channel_id=1, replica_groups=mesh['zl'=4,'core'=2,'y'=4,'x'=4,'zh'=2] {'zl','core'}, dimensions={0} | all-to-all | bytes 737280 | tf_op jit(solution)/shard_map/all_to_all | solution.py:119
  (85 shorter events, 23.5 us)
Async XLA Ops:
  6.5 2.7 %copy-start.4 = (bf16[36,1152]{1,0:T(8,128)(2,1)S(1)}, bf16[36,1152]{1,0:T(8,128)(2,1)}, u32[]{:S(2)}) copy-start(bf16[36,1152]{1,0:T(8,128)(2,1)} %param.13) | copy-start | bytes 248836
  6.5 2.7 %copy-start.3 = (bf16[36,3456]{1,0:T(8,128)(2,1)S(1)}, bf16[36,3456]{1,0:T(8,128)(2,1)}, u32[]{:S(2)}) copy-start(bf16[36,3456]{1,0:T(8,128)(2,1)} %param.14) | copy-start | bytes 746500
  6.5 2.7 %copy-start.5 = (bf16[36,1152]{1,0:T(8,128)(2,1)S(1)}, bf16[36,1152]{1,0:T(8,128)(2,1)}, u32[]{:S(2)}) copy-start(bf16[36,1152]{1,0:T(8,128)(2,1)} %param.15) | copy-start | bytes 248836
  6.5 113.5 %all-gather.2.cloned.1.call-start = ((), (), s32[]{:S(2)}) async-start(), calls=%async_computation.6 | async-start | bytes 7206912 | tf_op jit(solution)/shard_map/all_gather | solution.py:85
  9.2 18.5 %copy-start.6 = (f32[3,1152]{1,0:T(4,128)S(1)}, f32[3,1152]{1,0:T(4,128)}, u32[]{:S(2)}) copy-start(f32[3,1152]{1,0:T(4,128)} %param.9) | copy-start | bytes 41476
  9.3 18.5 %copy-start.1 = (bf16[4,1,40,1152]{3,2,1,0:T(8,128)(2,1)S(1)}, bf16[4,1,40,1152]{3,2,1,0:T(8,128)(2,1)}, u32[]{:S(2)}) copy-start(bf16[4,1,40,1152]{3,2,1,0:T(8,128)(2,1)} %param.8) | copy-start | bytes 1105924
  9.6 16.8 %collective-permute-start.2 = (bf16[36,4672]{1,0:T(8,128)(2,1)S(1)}, bf16[36,4672]{1,0:T(8,128)(2,1)S(1)}, u32[]{:S(2)}, u32[]{:S(2)}) collective-permute-start(bf16[36,4672]{1,0:T(8,128)(2,1)S(1)} %pad_maximum_fusion.3), channel_id=1, source_target_pairs={{0,1},{1,0},{2,3},{3,2},{4,5},{5,4},{6,7},{7,6},{8,9},{9,8},{10,11... | collective-permute-start | bytes 1009160 | tf_op jit(solution)/shard_map/ppermute | solution.py:76
  28.5 20.7 %collective-permute-start = (bf16[4,40,1152]{2,1,0:T(8,128)(2,1)S(1)}, bf16[4,40,1152]{2,1,0:T(8,128)(2,1)S(1)}, u32[]{:S(2)}, u32[]{:S(2)}) collective-permute-start(bf16[4,40,1152]{2,1,0:T(8,128)(2,1)S(1)} %fusion.53), channel_id=1, source_target_pairs={{0,0},{1,32},{32,1},{33,33},{2,2},{3,34},{34,3},{35,35},{4,4},{5,3... | collective-permute-start | bytes 1105928 | tf_op jit(solution)/shard_map/ppermute | solution.py:72
  77.6 50.5 %collective-permute-start.1 = (bf16[4,160,1152]{2,1,0:T(8,128)(2,1)S(1)}, bf16[4,160,1152]{2,1,0:T(8,128)(2,1)}, u32[]{:S(2)}, u32[]{:S(2)}) collective-permute-start(bf16[4,160,1152]{2,1,0:T(8,128)(2,1)S(1)} %all_to_all.45), channel_id=1, source_target_pairs={{0,32},{32,0},{1,33},{33,1},{2,34},{34,2},{3,35},{35,3},{4,36},{36... | collective-permute-start | bytes 4423688 | tf_op jit(solution)/shard_map/ppermute | solution.py:95
  78.1 43.5 %copy-start.8 = (f32[4,72]{1,0:T(4,128)S(1)}, f32[4,72]{1,0:T(4,128)}, u32[]{:S(2)}) copy-start(f32[4,72]{1,0:T(4,128)} %param.11) | copy-start | bytes 3460
  79.3 42.4 %all-to-all-start.3 = ((bf16[16,72,432]{2,1,0:T(8,128)(2,1)}), bf16[16,72,432]{2,1,0:T(8,128)(2,1)S(1)}, u32[]{:S(2)}, u32[]{:S(2)}) async-start(bf16[16,72,432]{2,1,0:T(8,128)(2,1)} %bitcast.103), calls=%async_computation.3 | async-start | bytes 2359296 | tf_op jit(solution)/shard_map/all_to_all | solution.py:82
  120.1 51.4 %collective-permute-start.3 = (bf16[1152,2944]{1,0:T(8,128)(2,1)}, bf16[1152,2944]{1,0:T(8,128)(2,1)}, u32[]{:S(2)}, u32[]{:S(2)}) collective-permute-start(bf16[1152,2944]{1,0:T(8,128)(2,1)} %all-gather.2.cloned.1.call-done), channel_id=1, source_target_pairs={{0,32},{32,0},{1,33},{33,1},{2,34},{34,2},{3,35},{35,3},{4,36},{36... | collective-permute-start | bytes 20348936 | tf_op jit(solution)/shard_map/ppermute | solution.py:86
  121.6 19.4 %all-to-all-start = ((bf16[4,40,1152]{2,0,1:T(4,128)(2,1)}), bf16[4,40,1152]{2,0,1:T(4,128)(2,1)S(1)}, u32[]{:S(2)}, u32[]{:S(2)}) async-start(bf16[4,40,1152]{2,0,1:T(4,128)(2,1)} %bitcast.111), calls=%async_computation | async-start | bytes 737280 | tf_op jit(solution)/shard_map/all_to_all | solution.py:106
  128.1 1.8 copy-start.2
  139.2 11.9 %copy-start.7 = (f32[3,1152]{1,0:T(4,128)S(1)}, f32[3,1152]{1,0:T(4,128)}, u32[]{:S(2)}) copy-start(f32[3,1152]{1,0:T(4,128)} %param.10) | copy-start | bytes 41476
  141.1 28.6 %all-to-all-start.4 = ((bf16[256,2,360]{2,1,0:T(2,128)(2,1)}), bf16[256,2,360]{2,1,0:T(2,128)(2,1)S(1)}, u32[]{:S(2)}, u32[]{:S(2)}) async-start(bf16[256,2,360]{2,1,0:T(2,128)(2,1)} %reshape.245), calls=%async_computation.4 | async-start | bytes 786432 | tf_op jit(solution)/shard_map/all_to_all | solution.py:103
  177.1 2.8 %copy-start = (bf16[1152,2944]{1,0:T(8,128)(2,1)}, bf16[1152,2944]{1,0:T(8,128)(2,1)S(1)}, u32[]{:S(2)}) copy-start(bf16[1152,2944]{1,0:T(8,128)(2,1)S(1)} %get-tuple-element.15) | copy-start | bytes 20348932
Sparse Core Ops, SparseCore 0:
  27.8 92.2 all-gather.1

commit v2 on v1

v2 whole, which is shorter than its diff:
```python
import jax
import jax.numpy as jnp
from jax import lax
from jax.experimental import pallas as pl
from jax.experimental.pallas import tpu as pltpu
from jax.sharding import Mesh
from jax.sharding import PartitionSpec as P

HEADS = 16
HDIM = 72
D = 1152
PAIR = 2 * HDIM
CUT = 2944
REST = 3 * D - CUT
SCALE = HDIM**-0.5
EXP2 = 1.4426950408889634
F32 = jnp.float32
BF16 = jnp.bfloat16
VMEM = pl.BlockSpec(memory_space=pltpu.VMEM)
SMEM = pl.BlockSpec(memory_space=pltpu.SMEM)
ANY = pl.BlockSpec(memory_space=pl.ANY)


def dot32(a, b):
    return jnp.dot(a, b, preferred_element_type=F32)


def dot_t(a, b):
    return lax.dot_general(a, b, (((1,), (1,)), ((), ())), preferred_element_type=F32)


def modulate(values, shift, scale):
    center = values - jnp.mean(values, -1, keepdims=True)
    variance = jnp.mean(center * center, -1, keepdims=True)
    return (center * lax.rsqrt(variance + 1e-06) * (1.0 + scale) + shift).astype(BF16)


def merge_kernel(place, mod, a0, a1, a2, a3, out):
    for k, piece in enumerate((a0, a1, a2, a3)):
        rows = modulate(piece[...].astype(F32), mod[0:1], mod[1:2])
        for copy in range(4):
            out[copy, lax.rem(place[0] + k, 4)] = rows


def merge(place, mod, pieces):
    return pl.pallas_call(
        merge_kernel,
        out_shape=jax.ShapeDtypeStruct((4, 4, 40, D), BF16),
        in_specs=[SMEM] + [VMEM] * 5,
        out_specs=VMEM,
        cost_estimate=pl.CostEstimate(
            flops=4_000_000, bytes_accessed=2_000_000, transcendentals=0
        ),
    )(place, mod, *pieces)


def softmax(scores):
    highest = jnp.max(scores, -1, keepdims=True)
    expo = jnp.exp2((scores - highest) * (SCALE * EXP2))
    return (expo * (1.0 / jnp.sum(expo, -1, keepdims=True))).astype(BF16)


def spatial_kernel(place, gain, tok_ours, tok_theirs, wts, out, wall, q0, q1, k0, v0):
    core = place[1]
    wall[...] = jnp.zeros_like(wall)
    for part in range(3):
        wall[:, 256 * part : 256 * part + PAIR] = wts[:, PAIR * part : PAIR * (part + 1)]
    lane = lax.broadcasted_iota(jnp.int32, (1, 256), 1)
    first = lane < HDIM
    second = (lane >= HDIM) & (lane < PAIR)

    def head_norm(heads, g):
        square = heads * heads
        s0 = jnp.sum(jnp.where(first, square, 0.0), -1, keepdims=True)
        s1 = jnp.sum(jnp.where(first, 0.0, square), -1, keepdims=True)
        r0 = lax.rsqrt(s0 * (1.0 / HDIM) + 1e-06)
        r1 = lax.rsqrt(s1 * (1.0 / HDIM) + 1e-06)
        return heads * jnp.where(first, r0, r1) * g

    for i in range(4):
        at = slice(320 * i, 320 * (i + 1))
        tok = (tok_ours, tok_theirs)[i // 2]
        qkv = dot32(tok[320 * (i % 2) : 320 * (i % 2 + 1)], wall[...])
        q = head_norm(qkv[:, :256], gain[0:1])
        q0[at] = jnp.where(first, q, 0.0).astype(BF16)
        q1[at] = jnp.where(second, q, 0.0).astype(BF16)
        k0[at] = head_norm(qkv[:, 256:512], gain[1:2]).astype(BF16)
        v0[at] = qkv[:, 512:].astype(BF16)

    for i in range(4):
        at = slice(320 * i, 320 * (i + 1))
        a = dot32(softmax(dot_t(q0[at], k0[...])), v0[...])
        b = dot32(softmax(dot_t(q1[at], k0[...])), v0[...])
        att = jnp.where(first, a, b)[:, :PAIR]
        from_zh = core if i < 2 else 1 - core
        for j in range(8):
            out[from_zh * 16 + (i % 2) * 8 + j] = att[40 * j : 40 * (j + 1)].astype(BF16)


def spatial(place, gain, *operands):
    return pl.pallas_call(
        spatial_kernel,
        out_shape=jax.ShapeDtypeStruct((32, 40, PAIR), BF16),
        in_specs=[SMEM] + [VMEM] * 4,
        out_specs=VMEM,
        scratch_shapes=[pltpu.VMEM((D, 768), BF16)] + [pltpu.VMEM((1280, 256), BF16)] * 4,
        compiler_params=pltpu.CompilerParams(vmem_limit_bytes=48 * 2**20),
        cost_estimate=pl.CostEstimate(
            flops=5_000_000_000, bytes_accessed=5_000_000, transcendentals=3_300_000
        ),
    )(place, gain, *operands)


def temporal_kernel(mods, gain, seg, back, res, wts, out, wos, wa, wb, wot, sem):
    parts = [
        (pl.ds(D, D), slice(REST, REST + D), wos),
        (pl.ds(0, D), slice(0, CUT), wa),
        (pl.ds(D, D), slice(0, REST), wb),
        (pl.ds(D, D), slice(REST + D, REST + 2 * D), wot),
    ]
    waits = [
        pltpu.make_async_copy(wts.at[rows, cols], to, sem.at[i])
        for i, (rows, cols, to) in enumerate(parts)
    ]
    for copy in waits:
        copy.start()
    waits[0].wait()
    hidden = res[...].astype(F32) + mods[2:3] * dot32(back[...], wos[...])
    hidden = hidden.astype(BF16).astype(F32)
    modulated = modulate(hidden, mods[3:4], mods[4:5])
    waits[1].wait()
    qkv_a = dot32(modulated, wa[...])
    waits[2].wait()
    qkv_b = dot32(modulated, wb[...])
    q, k = qkv_a[:, :D], qkv_a[:, D : 2 * D]
    v = jnp.concatenate([qkv_a[:, 2 * D :], qkv_b], 1).astype(BF16)

    def head_norm(heads, g):
        square = heads * heads
        high = square.astype(BF16)
        low = (square - high.astype(F32)).astype(BF16)
        mean = (dot32(high, seg[...]) + dot32(low, seg[...])) * (1.0 / HDIM)
        r = lax.rsqrt(mean + 1e-06)
        r_high = r.astype(BF16)
        r_mid = (r - r_high.astype(F32)).astype(BF16)
        r_low = (r - r_high.astype(F32) - r_mid.astype(F32)).astype(BF16)
        wide = dot_t(r_high, seg[...]) + dot_t(r_mid, seg[...]) + dot_t(r_low, seg[...])
        return heads * wide * g

    q = head_norm(q, gain[0:1])
    k = head_norm(k, gain[1:2]).astype(BF16)
    row = lax.broadcasted_iota(jnp.int32, (160, 160), 0)
    col = lax.broadcasted_iota(jnp.int32, (160, 160), 1)
    apart = lax.rem(row, 5) != lax.rem(col, 5)
    tiles = [None] * (D // 128)
    for h in range(HEADS):
        lo, hi = HDIM * h, HDIM * (h + 1)
        t0, t1 = lo // 128, -(-hi // 128)
        lane = lax.broadcasted_iota(jnp.int32, (1, 128 * (t1 - t0)), 1) + 128 * t0
        inside = (lane >= lo) & (lane < hi)
        window = slice(128 * t0, 128 * t1)
        qh = jnp.where(inside, q[:, window], 0.0).astype(BF16)
        scores = jnp.where(apart, -1e30, dot_t(qh, k[:, window]))
        att = dot32(softmax(scores), v[:, window])
        att = jnp.where(inside, att, 0.0)
        for t in range(t0, t1):
            part = att[:, 128 * (t - t0) : 128 * (t - t0 + 1)]
            tiles[t] = part if tiles[t] is None else tiles[t] + part
    attended = jnp.concatenate(tiles, 1).astype(BF16)
    waits[3].wait()
    out[...] = (hidden + mods[5:6] * dot32(attended, wot[...])).astype(BF16)


def temporal(mods, gain, seg, back, res, wts):
    return pl.pallas_call(
        temporal_kernel,
        out_shape=jax.ShapeDtypeStruct((160, D), BF16),
        in_specs=[VMEM] * 5 + [ANY],
        out_specs=VMEM,
        scratch_shapes=[
            pltpu.VMEM((D, D), BF16),
            pltpu.VMEM((D, CUT), BF16),
            pltpu.VMEM((D, REST), BF16),
            pltpu.VMEM((D, D), BF16),
            pltpu.SemaphoreType.DMA((4,)),
        ],
        compiler_params=pltpu.CompilerParams(vmem_limit_bytes=40 * 2**20),
        cost_estimate=pl.CostEstimate(
            flops=1_800_000_000, bytes_accessed=15_000_000, transcendentals=500_000
        ),
    )(mods, gain, seg, back, res, wts)


def in_order(zh, mine, far):
    return jnp.concatenate([jnp.where(zh == 0, mine, far), jnp.where(zh == 0, far, mine)], 0)


def per_device(latent, mod_s, mod_t, gain, wqkv_s, wout_s, wqkv_t, wout_t):
    core = lax.axis_index("core")
    zh = lax.axis_index("zh")
    y = lax.axis_index("y")
    place = jnp.stack([y, core]).astype(jnp.int32)
    other = [(0, 1), (1, 0)]
    latent = latent.reshape(4, 40, D)

    pad = jnp.zeros((36, 2 * CUT - 5 * D), BF16)
    tail = jnp.concatenate([wqkv_t[:, CUT:], wout_s, wout_t, pad], 1)
    half_r = jnp.where(core == 0, wqkv_t[:, :CUT], tail)
    far_r = lax.ppermute(half_r, "zh", other)

    pieces = []
    for k in range(4):
        piece = lax.dynamic_index_in_dim(latent, (y + 4 - k) % 4, 0, keepdims=False)
        route = [
            ((c * 4 + (t + k) % 4) * 2 + z, (z * 4 + t) * 2 + c)
            for c in range(2)
            for t in range(4)
            for z in range(2)
        ]
        pieces.append(lax.ppermute(piece, ("core", "y", "zh"), route))

    by_pair = wqkv_s.reshape(36, 3, 4, 2, PAIR)
    half_s = lax.dynamic_index_in_dim(by_pair, core, 3, keepdims=False)
    half_s = half_s.transpose(2, 0, 1, 3).reshape(4, 36, 3 * PAIR)
    w_x = lax.all_to_all(half_s, "x", split_axis=0, concat_axis=0, tiled=True)
    w_far = lax.ppermute(w_x, "zh", other)
    far_r, w_far, pieces = lax.optimization_barrier((far_r, w_far, pieces))
    w_x = jnp.stack([jnp.where(zh == 0, w_x, w_far), jnp.where(zh == 0, w_far, w_x)], 1)
    w_x = jnp.broadcast_to(w_x.reshape(1, D // 4, 3 * PAIR), (4, D // 4, 3 * PAIR))
    w_y = lax.all_to_all(w_x, "y", split_axis=0, concat_axis=0, tiled=True)
    w_y = w_y.reshape(D, 3 * PAIR)

    both_r = in_order(zh, half_r, far_r)
    weights = lax.all_gather(both_r, ("core", "y", "x"), axis=0, tiled=True)

    copies = merge(place, mod_s, pieces).reshape(4, 160, D)
    ours = lax.all_to_all(copies, "x", split_axis=0, concat_axis=0, tiled=True).reshape(640, D)
    ours, w_y = lax.optimization_barrier((ours, w_y))
    theirs = lax.ppermute(ours, "core", other)
    home_in, ours = lax.optimization_barrier((latent, ours))
    home = lax.all_to_all(home_in, ("zl", "core"), split_axis=1, concat_axis=0, tiled=True)
    home = home.reshape(160, D)
    gain_s = jnp.pad(jnp.tile(gain[:2], (1, 2)), ((0, 0), (0, 256 - PAIR)))
    att = spatial(place, gain_s, ours, theirs, w_y)

    att = att.reshape(2, 4, 4, 4, 2, 5, PAIR).transpose(3, 0, 2, 1, 4, 5, 6)
    att = att.reshape(256, 5, PAIR)
    everyone = ("zl", "zh", "y", "x", "core")
    back = lax.all_to_all(att, everyone, split_axis=0, concat_axis=0, tiled=True)
    back = back.reshape(32, 8, 5, PAIR).transpose(0, 2, 1, 3).reshape(160, D)

    seg = (jnp.arange(D)[:, None] // HDIM == jnp.arange(128)[None]).astype(BF16)
    mods = jnp.concatenate([mod_s, mod_t], 0)
    mixed = temporal(mods, jnp.tile(gain[2:], (1, HEADS)), seg, back, home, weights)
    mixed = lax.all_to_all(
        mixed.reshape(32, 5, D), ("zl", "core"), split_axis=0, concat_axis=1, tiled=True
    )
    return mixed.reshape(4, 1, 40, D)


def solution(mesh):
    fine = Mesh(mesh.devices.reshape(4, 2, 4, 4, 2), ("zl", "core", "y", "x", "zh"))
    frame, row = ("zl", "core"), ("y", "x", "zh")
    in_specs = (
        P(frame, row, None, None),
        P(),
        P(),
        P(),
        P(row, None),
        P(row, None),
        P(row, None),
        P(row, None),
    )
    return jax.shard_map(
        per_device,
        mesh=fine,
        in_specs=in_specs,
        out_specs=P(frame, row, None, None),
        check_vma=False,
    )
```

time: 226 us -> 173 us (0.77)
  waiting for transfers between devices: 69.7 us -> 36.9 us
  Pallas kernels: 0 us -> 21 us
  matrix products: 16.4 us -> 0 us
  other arithmetic: 13.6 us -> 1.83 us
  local copies, waits for them, and re-layouts: 22.7 us -> 11 us
  blocking collectives: 47.2 us -> 42.4 us
  starting transfers between devices: 42.5 us -> 46 us
    all_gather x1, waiting for transfers between devices: 37.1 us -> 0.02 us  [per_device(): weights = lax.all_gather(both_r, ('core', 'y', 'x'), axis=0, tiled=True)]
    pallas_call x0 -> x3, Pallas kernels: none -> 21 us  [the longest x1 9.27 us: spatial(): pl.pallas_call(spatial_kernel, out_shape=jax.ShapeDtypeStruct((32, 40, PA...]
    dot_general x10 -> x0, matrix products: 13.6 us -> none  [the longest x7 9.36 us: dot32(): return jnp.dot(a, b, preferred_element_type=jnp.float32)]
    all_to_all x2 -> x3, waiting for transfers between devices: 0.01 us -> 7.36 us  [the longest x1 7.36 us: per_device(): w_y = lax.all_to_all(w_x, 'y', split_axis=0, concat_axis=0, tiled=True)]
    all_to_all x2 -> x3, starting transfers between devices: 8.63 us -> 15.3 us  [the longest x1 6.94 us: per_device(): lax.all_to_all(home_in, ('zl', 'core'), split_axis=1, concat_axis=0, tile...]
    select_n x2 -> x3, other arithmetic: 5.87 us -> 0.13 us  [the longest x1 0.08 us: per_device(): half_r = jnp.where(core == 0, wqkv_t[:, :CUT], tail)]
    reshape x9 -> x6, local copies, waits for them, and re-layouts: 8.84 us -> 3.82 us  [the longest x1 1.62 us: per_device(): by_pair = wqkv_s.reshape(36, 3, 4, 2, PAIR)]
    all_to_all x2 -> x1, blocking collectives: 28.3 us -> 23.6 us  [per_device(): lax.all_to_all(copies, 'x', split_axis=0, concat_axis=0, tiled=True)]
  transfers between devices with their start and end apart: 8 -> 12, of which waited for: 4 -> 5; matrix products, arithmetic and copies ran while one was open for 9% -> 4% of each run, Pallas kernels for 0% -> 7%
where the time goes in v2:
time: 173 us
  starting transfers between devices  46 us (27%)
  blocking collectives  42.4 us (25%)
  waiting for transfers between devices  36.9 us (21%)
  Pallas kernels  21 us (12%)
  between operations  13.8 us (8%)
  local copies, waits for them, and re-layouts  11 us (6%)
  other arithmetic  1.83 us (1%)
    all_to_all x1, blocking collectives, per_device(): lax.all_to_all(copies, 'x', split_axis=0, concat_axis=0, tiled=True)  23.6 us
    all_to_all x1, blocking collectives, per_device(): lax.all_to_all(mixed.reshape(32, 5, D), ('zl', 'core'), split_axis=0, con...  18.8 us
    all_to_all x1, waiting for transfers between devices, per_device(): lax.all_to_all(att, everyone, split_axis=0, concat_axis=0, tiled=True)  18 us
    ppermute x4, starting transfers between devices, per_device(): pieces.append(lax.ppermute(piece, ('core', 'y', 'zh'), route))  14.5 us
    ppermute x4, waiting for transfers between devices, per_device(): pieces.append(lax.ppermute(piece, ('core', 'y', 'zh'), route))  11.4 us
    pallas_call x1, Pallas kernels, spatial(): pl.pallas_call(spatial_kernel, out_shape=jax.ShapeDtypeStruct((32, 40, PA...  9.27 us
    pallas_call x1, Pallas kernels, temporal(): pl.pallas_call(temporal_kernel, out_shape=jax.ShapeDtypeStruct((160, D),...  9.24 us
    all_to_all x1, waiting for transfers between devices, per_device(): w_y = lax.all_to_all(w_x, 'y', split_axis=0, concat_axis=0, tiled=True)  7.36 us
  transfers between devices with their start and end apart: 12, of which 5 were waited for; matrix products, arithmetic and copies ran while one was open for 4% of the time, Pallas kernels for 7%

profile of v2, /device:TPU:1, one launch (start us, length us, event | category | flops | bytes accessed | tf_op | source)
XLA Modules:
  0.0 172.9 jit_solution(8107198429436496506)
XLA Ops:
  6.5 1.6 reshape.83
  9.7 4.8 %all-to-all-start = ((bf16[4,36,432]{2,1,0:T(8,128)(2,1)}), bf16[4,36,432]{2,1,0:T(8,128)(2,1)S(1)}, u32[]{:S(2)}, u32[]{:S(2)}) async-start(bf16[4,36,432]{2,1,0:T(8,128)(2,1)} %reshape.95), calls=%async_computation | async-start | bytes 327680 | tf_op jit(solution)/shard_map/all_to_all | solution.py:225
  14.7 7.0 %collective-permute-start = (bf16[36,2944]{1,0:T(8,128)(2,1)S(1)}, bf16[36,2944]{1,0:T(8,128)(2,1)S(1)}, u32[]{:S(2)}, u32[]{:S(2)}) collective-permute-start(bf16[36,2944]{1,0:T(8,128)(2,1)S(1)} %maximum_select_fusion), channel_id=1, source_target_pairs={{0,1},{1,0},{2,3},{3,2},{4,5},{5,4},{6,7},{7,6},{8,9},{9,8},{10,11... | collective-permute-start | bytes 635912 | tf_op jit(solution)/shard_map/ppermute | solution.py:209
  21.7 2.8 %collective-permute-start.2 = (bf16[40,1152]{1,0:T(8,128)(2,1)S(1)}, bf16[40,1152]{1,0:T(8,128)(2,1)S(1)}, u32[]{:S(2)}, u32[]{:S(2)}) collective-permute-start(bf16[40,1152]{1,0:T(8,128)(2,1)S(1)} %get-tuple-element.29), channel_id=1, source_target_pairs={{0,0},{1,32},{8,8},{9,40},{16,16},{17,48},{24,24},{25,56},{32,1},{... | collective-permute-start | bytes 276488 | tf_op jit(solution)/shard_map/ppermute | solution.py:220
  24.6 1.9 %collective-permute-start.1 = (bf16[4,36,432]{2,1,0:T(8,128)(2,1)S(1)}, bf16[4,36,432]{2,1,0:T(8,128)(2,1)S(1)}, u32[]{:S(2)}, u32[]{:S(2)}) collective-permute-start(bf16[4,36,432]{2,1,0:T(8,128)(2,1)S(1)} %all-to-all-done), channel_id=1, source_target_pairs={{0,1},{1,0},{2,3},{3,2},{4,5},{5,4},{6,7},{7,6},{8,9},{9,8},{10,11... | collective-permute-start | bytes 373256 | tf_op jit(solution)/shard_map/ppermute | solution.py:226
  26.4 5.5 %collective-permute-start.3 = (bf16[40,1152]{1,0:T(8,128)(2,1)S(1)}, bf16[40,1152]{1,0:T(8,128)(2,1)S(1)}, u32[]{:S(2)}, u32[]{:S(2)}) collective-permute-start(bf16[40,1152]{1,0:T(8,128)(2,1)S(1)} %get-tuple-element.28), channel_id=1, source_target_pairs={{8,0},{9,32},{16,8},{17,40},{24,16},{25,48},{0,24},{1,56},{40,1},{... | collective-permute-start | bytes 276488 | tf_op jit(solution)/shard_map/ppermute | solution.py:220
  31.9 2.7 %collective-permute-start.4 = (bf16[40,1152]{1,0:T(8,128)(2,1)S(1)}, bf16[40,1152]{1,0:T(8,128)(2,1)S(1)}, u32[]{:S(2)}, u32[]{:S(2)}) collective-permute-start(bf16[40,1152]{1,0:T(8,128)(2,1)S(1)} %get-tuple-element.30), channel_id=1, source_target_pairs={{16,0},{17,32},{24,8},{25,40},{0,16},{1,48},{8,24},{9,56},{48,1},{... | collective-permute-start | bytes 276488 | tf_op jit(solution)/shard_map/ppermute | solution.py:220
  34.6 3.5 %collective-permute-start.5 = (bf16[40,1152]{1,0:T(8,128)(2,1)S(1)}, bf16[40,1152]{1,0:T(8,128)(2,1)S(1)}, u32[]{:S(2)}, u32[]{:S(2)}) collective-permute-start(bf16[40,1152]{1,0:T(8,128)(2,1)S(1)} %get-tuple-element.27), channel_id=1, source_target_pairs={{24,0},{25,32},{0,8},{1,40},{8,16},{9,48},{16,24},{17,56},{56,1},{... | collective-permute-start | bytes 276488 | tf_op jit(solution)/shard_map/ppermute | solution.py:220
  38.1 4.9 %collective-permute-done.3.a1 = bf16[40,1152]{1,0:T(8,128)(2,1)S(1)} collective-permute-done((bf16[40,1152]{1,0:T(8,128)(2,1)S(1)}, bf16[40,1152]{1,0:T(8,128)(2,1)S(1)}, u32[]{:S(2)}, u32[]{:S(2)}) %collective-permute-start.3) | collective-permute-done | bytes 92192 | tf_op jit(solution)/shard_map/ppermute | solution.py:220
  43.0 4.0 %collective-permute-done.4.a2 = bf16[40,1152]{1,0:T(8,128)(2,1)S(1)} collective-permute-done((bf16[40,1152]{1,0:T(8,128)(2,1)S(1)}, bf16[40,1152]{1,0:T(8,128)(2,1)S(1)}, u32[]{:S(2)}, u32[]{:S(2)}) %collective-permute-start.4) | collective-permute-done | bytes 92192 | tf_op jit(solution)/shard_map/ppermute | solution.py:220
  47.0 2.5 %collective-permute-done.5.a3 = bf16[40,1152]{1,0:T(8,128)(2,1)S(1)} collective-permute-done((bf16[40,1152]{1,0:T(8,128)(2,1)S(1)}, bf16[40,1152]{1,0:T(8,128)(2,1)S(1)}, u32[]{:S(2)}, u32[]{:S(2)}) %collective-permute-start.5) | collective-permute-done | bytes 92192 | tf_op jit(solution)/shard_map/ppermute | solution.py:220
  50.7 1.1 broadcast_in_dim.14
  51.8 3.5 %all-to-all-start.2 = ((bf16[4,288,432]{2,1,0:T(8,128)(2,1)}), bf16[4,288,432]{2,1,0:T(8,128)(2,1)S(1)}, u32[]{:S(2)}, u32[]{:S(2)}) async-start(bf16[4,288,432]{2,1,0:T(8,128)(2,1)} %broadcast_in_dim.14), calls=%async_computation.2 | async-start | bytes 2359296 | tf_op jit(solution)/shard_map/all_to_all | solution.py:230
  55.9 2.5 %shard_map.82 = bf16[4,4,40,1152]{3,2,1,0:T(8,128)(2,1)} custom-call(s32[2]{0:T(128)} %pad_add_fusion.place, f32[3,1152]{1,0:T(4,128)} %mod.1, bf16[40,1152]{1,0:T(8,128)(2,1)} %copy-done.3, bf16[40,1152]{1,0:T(8,128)(2,1)} %copy-done.4, bf16[40,1152]{1,0:T(8,128)(2,1)} %copy-done.5, bf16[40,1152]{1,0:T(8,128)(2,1)} %copy-done.6), custom_call_target="tpu_custom_call" | custom-call | flops 4000000 | bytes 2000000 | tf_op jit(solution)/shard_map/pallas_call | solution.py:46
  58.4 7.4 %all-to-all-done.2 = bf16[4,288,432]{2,1,0:T(8,128)(2,1)S(1)} async-done(((bf16[4,288,432]{2,1,0:T(8,128)(2,1)}), bf16[4,288,432]{2,1,0:T(8,128)(2,1)S(1)}, u32[]{:S(2)}, u32[]{:S(2)}) %all-to-all-start.2) | async-done | bytes 995360 | tf_op jit(solution)/shard_map/all_to_all | solution.py:230
  65.8 23.6 %all_to_all.50 = bf16[4,160,1152]{2,1,0:T(8,128)(2,1)S(1)} all-to-all(bf16[4,160,1152]{2,1,0:T(8,128)(2,1)} %bitcast.45), channel_id=1, replica_groups=mesh['zl'=4,'core'=2,'y'=4,'x'=4,'zh'=2] {'x'}, dimensions={0} | all-to-all | bytes 2949120 | tf_op jit(solution)/shard_map/all_to_all | solution.py:237
  90.2 6.9 %all-to-all-start.4 = ((bf16[4,40,1152]{2,0,1:T(4,128)(2,1)}), bf16[4,40,1152]{2,0,1:T(4,128)(2,1)S(1)}, u32[]{:S(2)}, u32[]{:S(2)}) async-start(bf16[4,40,1152]{2,0,1:T(4,128)(2,1)} %bitcast.40), calls=%async_computation.4 | async-start | bytes 737280 | tf_op jit(solution)/shard_map/all_to_all | solution.py:241
  97.3 9.3 %shard_map.83 = bf16[32,40,144]{2,1,0:T(8,128)(2,1)S(1)} custom-call(s32[2]{0:T(128)S(1)} %copy-done, f32[2,256]{1,0:T(2,128)S(1)} %pad.4.gain, bf16[640,1152]{1,0:T(8,128)(2,1)S(1)} %bitcast.43, bf16[640,1152]{1,0:T(8,128)(2,1)} %collective-permute-done.6.tok_theirs, bf16[1152,432]{1,0:T(8,128)(2,1)S(1)} %bitcast.44), custom_call_target="tpu_custom_call" | custom-call | flops 5000000000 | bytes 5000000 | tf_op jit(solution)/shard_map/pallas_call | solution.py:101
  107.4 1.7 %reshape.96 = bf16[256,2,360]{2,1,0:T(2,128)(2,1)} reshape(bf16[256,5,144]{2,1,0:T(8,128)(2,1)S(1)} %bitcast.46) | data formatting | bytes 737280
  109.1 7.3 %all-to-all-start.3 = ((bf16[256,2,360]{2,1,0:T(2,128)(2,1)}), bf16[256,2,360]{2,1,0:T(2,128)(2,1)S(1)}, u32[]{:S(2)}, u32[]{:S(2)}) async-start(bf16[256,2,360]{2,1,0:T(2,128)(2,1)} %reshape.96), calls=%async_computation.3 | async-start | bytes 786432 | tf_op jit(solution)/shard_map/all_to_all | solution.py:249
  117.1 18.0 %all-to-all-done.3 = bf16[256,2,360]{2,1,0:T(2,128)(2,1)S(1)} async-done(((bf16[256,2,360]{2,1,0:T(2,128)(2,1)}), bf16[256,2,360]{2,1,0:T(2,128)(2,1)S(1)}, u32[]{:S(2)}, u32[]{:S(2)}) %all-to-all-start.3) | async-done | bytes 368672 | tf_op jit(solution)/shard_map/all_to_all | solution.py:249
  135.1 0.9 reshape.97
  136.8 9.2 %shard_map.84 = bf16[160,1152]{1,0:T(8,128)(2,1)S(1)} custom-call(f32[6,1152]{1,0:T(8,128)S(1)} %pad_maximum_fusion.2.mods, f32[2,1152]{1,0:T(2,128)S(1)} %tile.9.gain, bf16[1152,128]{1,0:T(8,128)(2,1)S(1)} %fusion.seg, bf16[160,1152]{1,0:T(8,128)(2,1)S(1)} %reshape.91.back, bf16[160,1152]{1,0:T(8,128)(2,1)S(1)} %reshape.92.res, ...), custom_call_target="tpu_custom_call" | custom-call | flops 1800000000 | bytes 15000000 | tf_op jit(solution)/shard_map/pallas_call | solution.py:175
  146.2 18.8 %all_to_all.51 = bf16[32,5,1152]{2,1,0:T(8,128)(2,1)S(1)} all-to-all(bf16[32,5,1152]{2,1,0:T(8,128)(2,1)S(1)} %reshape.93), channel_id=1, replica_groups=mesh['zl'=4,'core'=2,'y'=4,'x'=4,'zh'=2] {'zl','core'}, dimensions={0} | all-to-all | bytes 737280 | tf_op jit(solution)/shard_map/all_to_all | solution.py:255
  (70 shorter events, 7.5 us)
Async XLA Ops:
  6.5 8.0 %copy-start.2 = (bf16[36,3456]{1,0:T(8,128)(2,1)S(1)}, bf16[36,3456]{1,0:T(8,128)(2,1)}, u32[]{:S(2)}) copy-start(bf16[36,3456]{1,0:T(8,128)(2,1)} %param.14) | copy-start | bytes 746500
  6.5 8.0 %slice-start = ((bf16[36,3456]{1,0:T(8,128)(2,1)}), bf16[36,512]{1,0:T(8,128)(2,1)S(1)}, s32[]{:S(2)}) async-start(bf16[36,3456]{1,0:T(8,128)(2,1)} %param.14), calls=%async_computation.7 | async-start | bytes 81920 | tf_op jit(solution)/shard_map/slice | solution.py:207
  6.5 8.0 %copy-start.7 = (bf16[36,1152]{1,0:T(8,128)(2,1)S(1)}, bf16[36,1152]{1,0:T(8,128)(2,1)}, u32[]{:S(2)}) copy-start(bf16[36,1152]{1,0:T(8,128)(2,1)} %param.15) | copy-start | bytes 248836
  6.5 8.0 %copy-start.8 = (bf16[36,1152]{1,0:T(8,128)(2,1)S(1)}, bf16[36,1152]{1,0:T(8,128)(2,1)}, u32[]{:S(2)}) copy-start(bf16[36,1152]{1,0:T(8,128)(2,1)} %param.13) | copy-start | bytes 248836
  8.2 13.5 %copy-start.1 = (bf16[4,1,40,1152]{3,2,1,0:T(8,128)(2,1)S(1)}, bf16[4,1,40,1152]{3,2,1,0:T(8,128)(2,1)}, u32[]{:S(2)}) copy-start(bf16[4,1,40,1152]{3,2,1,0:T(8,128)(2,1)} %param.8) | copy-start | bytes 1105924
  9.7 14.9 %all-to-all-start = ((bf16[4,36,432]{2,1,0:T(8,128)(2,1)}), bf16[4,36,432]{2,1,0:T(8,128)(2,1)S(1)}, u32[]{:S(2)}, u32[]{:S(2)}) async-start(bf16[4,36,432]{2,1,0:T(8,128)(2,1)} %reshape.95), calls=%async_computation | async-start | bytes 327680 | tf_op jit(solution)/shard_map/all_to_all | solution.py:225
  14.5 122.3 %all-gather.2.cloned.1.call-start = ((), (), s32[]{:S(2)}) async-start(), calls=%async_computation.6 | async-start | bytes 13989888 | tf_op jit(solution)/shard_map/all_gather | solution.py:234
  14.7 34.8 %collective-permute-start = (bf16[36,2944]{1,0:T(8,128)(2,1)S(1)}, bf16[36,2944]{1,0:T(8,128)(2,1)S(1)}, u32[]{:S(2)}, u32[]{:S(2)}) collective-permute-start(bf16[36,2944]{1,0:T(8,128)(2,1)S(1)} %maximum_select_fusion), channel_id=1, source_target_pairs={{0,1},{1,0},{2,3},{3,2},{4,5},{5,4},{6,7},{7,6},{8,9},{9,8},{10,11... | collective-permute-start | bytes 635912 | tf_op jit(solution)/shard_map/ppermute | solution.py:209
  21.7 12.9 %collective-permute-start.2 = (bf16[40,1152]{1,0:T(8,128)(2,1)S(1)}, bf16[40,1152]{1,0:T(8,128)(2,1)S(1)}, u32[]{:S(2)}, u32[]{:S(2)}) collective-permute-start(bf16[40,1152]{1,0:T(8,128)(2,1)S(1)} %get-tuple-element.29), channel_id=1, source_target_pairs={{0,0},{1,32},{8,8},{9,40},{16,16},{17,48},{24,24},{25,56},{32,1},{... | collective-permute-start | bytes 276488 | tf_op jit(solution)/shard_map/ppermute | solution.py:220
  24.6 25.0 %collective-permute-start.1 = (bf16[4,36,432]{2,1,0:T(8,128)(2,1)S(1)}, bf16[4,36,432]{2,1,0:T(8,128)(2,1)S(1)}, u32[]{:S(2)}, u32[]{:S(2)}) collective-permute-start(bf16[4,36,432]{2,1,0:T(8,128)(2,1)S(1)} %all-to-all-done), channel_id=1, source_target_pairs={{0,1},{1,0},{2,3},{3,2},{4,5},{5,4},{6,7},{7,6},{8,9},{9,8},{10,11... | collective-permute-start | bytes 373256 | tf_op jit(solution)/shard_map/ppermute | solution.py:226
  26.4 16.6 %collective-permute-start.3 = (bf16[40,1152]{1,0:T(8,128)(2,1)S(1)}, bf16[40,1152]{1,0:T(8,128)(2,1)S(1)}, u32[]{:S(2)}, u32[]{:S(2)}) collective-permute-start(bf16[40,1152]{1,0:T(8,128)(2,1)S(1)} %get-tuple-element.28), channel_id=1, source_target_pairs={{8,0},{9,32},{16,8},{17,40},{24,16},{25,48},{0,24},{1,56},{40,1},{... | collective-permute-start | bytes 276488 | tf_op jit(solution)/shard_map/ppermute | solution.py:220
  31.9 15.1 %collective-permute-start.4 = (bf16[40,1152]{1,0:T(8,128)(2,1)S(1)}, bf16[40,1152]{1,0:T(8,128)(2,1)S(1)}, u32[]{:S(2)}, u32[]{:S(2)}) collective-permute-start(bf16[40,1152]{1,0:T(8,128)(2,1)S(1)} %get-tuple-element.30), channel_id=1, source_target_pairs={{16,0},{17,32},{24,8},{25,40},{0,16},{1,48},{8,24},{9,56},{48,1},{... | collective-permute-start | bytes 276488 | tf_op jit(solution)/shard_map/ppermute | solution.py:220
  34.6 15.9 %copy-start.3 = (bf16[40,1152]{1,0:T(8,128)(2,1)}, bf16[40,1152]{1,0:T(8,128)(2,1)S(1)}, u32[]{:S(2)}) copy-start(bf16[40,1152]{1,0:T(8,128)(2,1)S(1)} %collective-permute-done.2.a0) | copy-start | bytes 276484
  34.6 14.9 %collective-permute-start.5 = (bf16[40,1152]{1,0:T(8,128)(2,1)S(1)}, bf16[40,1152]{1,0:T(8,128)(2,1)S(1)}, u32[]{:S(2)}, u32[]{:S(2)}) collective-permute-start(bf16[40,1152]{1,0:T(8,128)(2,1)S(1)} %get-tuple-element.27), channel_id=1, source_target_pairs={{24,0},{25,32},{0,8},{1,40},{8,16},{9,48},{16,24},{17,56},{56,1},{... | collective-permute-start | bytes 276488 | tf_op jit(solution)/shard_map/ppermute | solution.py:220
  43.0 7.5 %copy-start.4 = (bf16[40,1152]{1,0:T(8,128)(2,1)}, bf16[40,1152]{1,0:T(8,128)(2,1)S(1)}, u32[]{:S(2)}) copy-start(bf16[40,1152]{1,0:T(8,128)(2,1)S(1)} %collective-permute-done.3.a1) | copy-start | bytes 276484
  47.0 3.6 %copy-start.5 = (bf16[40,1152]{1,0:T(8,128)(2,1)}, bf16[40,1152]{1,0:T(8,128)(2,1)S(1)}, u32[]{:S(2)}) copy-start(bf16[40,1152]{1,0:T(8,128)(2,1)S(1)} %collective-permute-done.4.a2) | copy-start | bytes 276484
  51.8 13.9 %all-to-all-start.2 = ((bf16[4,288,432]{2,1,0:T(8,128)(2,1)}), bf16[4,288,432]{2,1,0:T(8,128)(2,1)S(1)}, u32[]{:S(2)}, u32[]{:S(2)}) async-start(bf16[4,288,432]{2,1,0:T(8,128)(2,1)} %broadcast_in_dim.14), calls=%async_computation.2 | async-start | bytes 2359296 | tf_op jit(solution)/shard_map/all_to_all | solution.py:230
  89.3 7.8 %copy-start.11 = (f32[4,72]{1,0:T(4,128)S(1)}, f32[4,72]{1,0:T(4,128)}, u32[]{:S(2)}) copy-start(f32[4,72]{1,0:T(4,128)} %param.11) | copy-start | bytes 3460
  89.3 7.9 %copy-start = (s32[2]{0:T(128)S(1)}, s32[2]{0:T(128)}, u32[]{:S(2)}) copy-start(s32[2]{0:T(128)} %pad_add_fusion.place) | copy-start | bytes 28
  89.3 7.9 %collective-permute-start.6 = (bf16[640,1152]{1,0:T(8,128)(2,1)S(1)}, bf16[640,1152]{1,0:T(8,128)(2,1)}, u32[]{:S(2)}, u32[]{:S(2)}) collective-permute-start(bf16[640,1152]{1,0:T(8,128)(2,1)S(1)} %bitcast.42), channel_id=1, source_target_pairs={{0,32},{32,0},{1,33},{33,1},{2,34},{34,2},{3,35},{35,3},{4,36},{36... | collective-permute-start | bytes 4423688 | tf_op jit(solution)/shard_map/ppermute | solution.py:239
  90.2 18.9 %all-to-all-start.4 = ((bf16[4,40,1152]{2,0,1:T(4,128)(2,1)}), bf16[4,40,1152]{2,0,1:T(4,128)(2,1)S(1)}, u32[]{:S(2)}, u32[]{:S(2)}) async-start(bf16[4,40,1152]{2,0,1:T(4,128)(2,1)} %bitcast.40), calls=%async_computation.4 | async-start | bytes 737280 | tf_op jit(solution)/shard_map/all_to_all | solution.py:241
  107.3 9.2 %copy-start.9 = (f32[3,1152]{1,0:T(4,128)S(1)}, f32[3,1152]{1,0:T(4,128)}, u32[]{:S(2)}) copy-start(f32[3,1152]{1,0:T(4,128)} %mod.1) | copy-start | bytes 41476
  107.3 9.2 %copy-start.10 = (f32[3,1152]{1,0:T(4,128)S(1)}, f32[3,1152]{1,0:T(4,128)}, u32[]{:S(2)}) copy-start(f32[3,1152]{1,0:T(4,128)} %param.10) | copy-start | bytes 41476
  109.1 26.0 %all-to-all-start.3 = ((bf16[256,2,360]{2,1,0:T(2,128)(2,1)}), bf16[256,2,360]{2,1,0:T(2,128)(2,1)S(1)}, u32[]{:S(2)}, u32[]{:S(2)}) async-start(bf16[256,2,360]{2,1,0:T(2,128)(2,1)} %reshape.96), calls=%async_computation.3 | async-start | bytes 786432 | tf_op jit(solution)/shard_map/all_to_all | solution.py:249
  (1 other events, 1.0 us)
Sparse Core Ops, SparseCore 0:
  50.6 75.3 all-gather.1

commit v3 on v2

--- a/solution.py
+++ b/solution.py
@@ -35,23 +35,20 @@
     return (center * lax.rsqrt(variance + 1e-06) * (1.0 + scale) + shift).astype(BF16)
 
 
-def merge_kernel(place, mod, a0, a1, a2, a3, out):
-    for k, piece in enumerate((a0, a1, a2, a3)):
-        rows = modulate(piece[...].astype(F32), mod[0:1], mod[1:2])
-        for copy in range(4):
-            out[copy, lax.rem(place[0] + k, 4)] = rows
-
-
-def merge(place, mod, pieces):
+def norm_kernel(mod, rows, out):
+    normed = modulate(rows[...].astype(F32), mod[0:1], mod[1:2])
+    for copy in range(4):
+        out[copy] = normed
+
+
+def norm_copies(mod, rows):
     return pl.pallas_call(
-        merge_kernel,
+        norm_kernel,
         out_shape=jax.ShapeDtypeStruct((4, 4, 40, D), BF16),
-        in_specs=[SMEM] + [VMEM] * 5,
+        in_specs=[VMEM] * 2,
         out_specs=VMEM,
-        cost_estimate=pl.CostEstimate(
-            flops=4_000_000, bytes_accessed=2_000_000, transcendentals=0
-        ),
-    )(place, mod, *pieces)
+        cost_estimate=pl.CostEstimate(flops=4_000_000, bytes_accessed=2_000_000, transcendentals=0),
+    )(mod, rows)
 
 
 def softmax(scores):
@@ -60,11 +57,14 @@
     return (expo * (1.0 / jnp.sum(expo, -1, keepdims=True))).astype(BF16)
 
 
-def spatial_kernel(place, gain, tok_ours, tok_theirs, wts, out, wall, q0, q1, k0, v0):
-    core = place[1]
+def spatial_kernel(place, gain, tok_ours, tok_theirs, w0, w1, w2, w3, out, wall, q0, q1, k0, v0):
+    y, own_zh = place[0], place[1]
+    quarter = D // 4
     wall[...] = jnp.zeros_like(wall)
-    for part in range(3):
-        wall[:, 256 * part : 256 * part + PAIR] = wts[:, PAIR * part : PAIR * (part + 1)]
+    for k, w in enumerate((w0, w1, w2, w3)):
+        rows = pl.ds(pl.multiple_of(lax.rem(y + k, 4) * quarter, quarter), quarter)
+        for part in range(3):
+            wall[rows, 256 * part : 256 * part + PAIR] = w[:, PAIR * part : PAIR * (part + 1)]
     lane = lax.broadcasted_iota(jnp.int32, (1, 256), 1)
     first = lane < HDIM
     second = (lane >= HDIM) & (lane < PAIR)
@@ -92,7 +92,7 @@
         a = dot32(softmax(dot_t(q0[at], k0[...])), v0[...])
         b = dot32(softmax(dot_t(q1[at], k0[...])), v0[...])
         att = jnp.where(first, a, b)[:, :PAIR]
-        from_zh = core if i < 2 else 1 - core
+        from_zh = own_zh if i < 2 else 1 - own_zh
         for j in range(8):
             out[from_zh * 16 + (i % 2) * 8 + j] = att[40 * j : 40 * (j + 1)].astype(BF16)
 
@@ -101,7 +101,7 @@
     return pl.pallas_call(
         spatial_kernel,
         out_shape=jax.ShapeDtypeStruct((32, 40, PAIR), BF16),
-        in_specs=[SMEM] + [VMEM] * 4,
+        in_specs=[SMEM] + [VMEM] * 7,
         out_specs=VMEM,
         scratch_shapes=[pltpu.VMEM((D, 768), BF16)] + [pltpu.VMEM((1280, 256), BF16)] * 4,
         compiler_params=pltpu.CompilerParams(vmem_limit_bytes=48 * 2**20),
@@ -199,41 +199,40 @@
     core = lax.axis_index("core")
     zh = lax.axis_index("zh")
     y = lax.axis_index("y")
-    place = jnp.stack([y, core]).astype(jnp.int32)
+    own_zh = lax.rem(zh + core + y // 2, 2)
+    place = jnp.stack([y, own_zh]).astype(jnp.int32)
     other = [(0, 1), (1, 0)]
     latent = latent.reshape(4, 40, D)
+
+    stay = lax.dynamic_slice_in_dim(latent, 2 * zh, 2, 0)
+    leave = lax.dynamic_slice_in_dim(latent, 2 - 2 * zh, 2, 0)
+    moved = lax.ppermute(leave, ("core", "zh"), [(i, 3 - i) for i in range(4)])
 
     pad = jnp.zeros((36, 2 * CUT - 5 * D), BF16)
     tail = jnp.concatenate([wqkv_t[:, CUT:], wout_s, wout_t, pad], 1)
     half_r = jnp.where(core == 0, wqkv_t[:, :CUT], tail)
     far_r = lax.ppermute(half_r, "zh", other)
 
-    pieces = []
-    for k in range(4):
-        piece = lax.dynamic_index_in_dim(latent, (y + 4 - k) % 4, 0, keepdims=False)
-        route = [
-            ((c * 4 + (t + k) % 4) * 2 + z, (z * 4 + t) * 2 + c)
-            for c in range(2)
-            for t in range(4)
-            for z in range(2)
-        ]
-        pieces.append(lax.ppermute(piece, ("core", "y", "zh"), route))
-
     by_pair = wqkv_s.reshape(36, 3, 4, 2, PAIR)
     half_s = lax.dynamic_index_in_dim(by_pair, core, 3, keepdims=False)
     half_s = half_s.transpose(2, 0, 1, 3).reshape(4, 36, 3 * PAIR)
     w_x = lax.all_to_all(half_s, "x", split_axis=0, concat_axis=0, tiled=True)
+    moved, w_x, far_r = lax.optimization_barrier((moved, w_x, far_r))
     w_far = lax.ppermute(w_x, "zh", other)
-    far_r, w_far, pieces = lax.optimization_barrier((far_r, w_far, pieces))
-    w_x = jnp.stack([jnp.where(zh == 0, w_x, w_far), jnp.where(zh == 0, w_far, w_x)], 1)
-    w_x = jnp.broadcast_to(w_x.reshape(1, D // 4, 3 * PAIR), (4, D // 4, 3 * PAIR))
-    w_y = lax.all_to_all(w_x, "y", split_axis=0, concat_axis=0, tiled=True)
-    w_y = w_y.reshape(D, 3 * PAIR)
-
-    both_r = in_order(zh, half_r, far_r)
-    weights = lax.all_gather(both_r, ("core", "y", "x"), axis=0, tiled=True)
-
-    copies = merge(place, mod_s, pieces).reshape(4, 160, D)
+    frames = jnp.concatenate(
+        [jnp.where(core == 0, stay, moved), jnp.where(core == 0, moved, stay)], 0
+    )
+    rows = lax.all_to_all(frames, "y", split_axis=0, concat_axis=0, tiled=True)
+    w_far, rows = lax.optimization_barrier((w_far, rows))
+    weights = lax.all_gather(in_order(zh, half_r, far_r), ("core", "y", "x"), axis=0, tiled=True)
+
+    w_z = jnp.stack([jnp.where(zh == 0, w_x, w_far), jnp.where(zh == 0, w_far, w_x)], 1)
+    w_z = w_z.reshape(D // 4, 3 * PAIR)
+    w_y = [w_z] + [
+        lax.ppermute(w_z, "y", [((i + k) % 4, i) for i in range(4)]) for k in (1, 2, 3)
+    ]
+
+    copies = norm_copies(mod_s, rows).reshape(4, 160, D)
     ours = lax.all_to_all(copies, "x", split_axis=0, concat_axis=0, tiled=True).reshape(640, D)
     ours, w_y = lax.optimization_barrier((ours, w_y))
     theirs = lax.ppermute(ours, "core", other)
@@ -241,13 +240,13 @@
     home = lax.all_to_all(home_in, ("zl", "core"), split_axis=1, concat_axis=0, tiled=True)
     home = home.reshape(160, D)
     gain_s = jnp.pad(jnp.tile(gain[:2], (1, 2)), ((0, 0), (0, 256 - PAIR)))
-    att = spatial(place, gain_s, ours, theirs, w_y)
+    att = spatial(place, gain_s, ours, theirs, *w_y)
 
     att = att.reshape(2, 4, 4, 4, 2, 5, PAIR).transpose(3, 0, 2, 1, 4, 5, 6)
     att = att.reshape(256, 5, PAIR)
     everyone = ("zl", "zh", "y", "x", "core")
     back = lax.all_to_all(att, everyone, split_axis=0, concat_axis=0, tiled=True)
-    back = back.reshape(32, 8, 5, PAIR).transpose(0, 2, 1, 3).reshape(160, D)
+    back = back.reshape(4, 2, 2, 2, 8, 5, PAIR).transpose(0, 2, 1, 3, 5, 4, 6).reshape(160, D)
 
     seg = (jnp.arange(D)[:, None] // HDIM == jnp.arange(128)[None]).astype(BF16)
     mods = jnp.concatenate([mod_s, mod_t], 0)

time: 173 us -> 169 us (0.977)
  blocking collectives: 42.4 us -> 18.9 us
  waiting for transfers between devices: 36.9 us -> 52.6 us
  local copies, waits for them, and re-layouts: 11 us -> 17.5 us
  starting transfers between devices: 46 us -> 42 us
    all_to_all x1 -> x0, blocking collectives: 23.6 us -> none  [per_device(): lax.all_to_all(copies, 'x', split_axis=0, concat_axis=0, tiled=True)]
    ppermute x1, waiting for transfers between devices: 0.01 us -> 9.81 us  [per_device(): w_far = lax.ppermute(w_x, 'zh', other)]
    all_to_all x1 -> x2, waiting for transfers between devices: 7.36 us -> 0.01 us  [the longest x1 0.01 us: per_device(): rows = lax.all_to_all(frames, 'y', split_axis=0, concat_axis=0, tiled=True)]
    ppermute x1, starting transfers between devices: 7 us -> 0.29 us  [per_device(): far_r = lax.ppermute(half_r, 'zh', other)]
    all_to_all x1 -> x2, starting transfers between devices: 3.53 us -> 9.22 us  [the longest x1 5.66 us: per_device(): rows = lax.all_to_all(frames, 'y', split_axis=0, concat_axis=0, tiled=True)]
    ppermute x1, waiting for transfers between devices: 0.01 us -> 5.52 us  [per_device(): far_r = lax.ppermute(half_r, 'zh', other)]
    all_to_all x1, waiting for transfers between devices: 0.01 us -> 5.29 us  [per_device(): w_x = lax.all_to_all(half_s, 'x', split_axis=0, concat_axis=0, tiled=True)]
    unnamed x27 -> x21, local copies, waits for them, and re-layouts: 3.6 us -> 8.64 us
  transfers between devices with their start and end apart: 12 -> 13, of which waited for: 5 -> 7; matrix products, arithmetic and copies ran while one was open for 4% -> 8% of each run, Pallas kernels for 7% -> 7%
where the time goes in v3:
time: 169 us; the launch traced here: 168 us
  waiting for transfers between devices  52.6 us (31%)
  starting transfers between devices  42 us (25%)
  Pallas kernels  20.2 us (12%)
  blocking collectives  18.9 us (11%)
  local copies, waits for them, and re-layouts  17.5 us (10%)
  between operations  13.7 us (8%)
  other arithmetic  3.22 us (2%)
    all_to_all x1, blocking collectives, per_device(): lax.all_to_all(mixed.reshape(32, 5, D), ('zl', 'core'), split_axis=0, con...  18.9 us
    all_to_all x1, waiting for transfers between devices, per_device(): lax.all_to_all(att, everyone, split_axis=0, concat_axis=0, tiled=True)  17.1 us
    ppermute x3, waiting for transfers between devices, per_device(): lax.ppermute(w_z, 'y', [((i + k) % 4, i) for i in range(4)])  14.9 us
    ppermute x1, waiting for transfers between devices, per_device(): w_far = lax.ppermute(w_x, 'zh', other)  9.81 us
    pallas_call x1, Pallas kernels, temporal(): pl.pallas_call(temporal_kernel, out_shape=jax.ShapeDtypeStruct((160, D),...  9.24 us
    unnamed x21, local copies, waits for them, and re-layouts  8.64 us
    pallas_call x1, Pallas kernels, spatial(): pl.pallas_call(spatial_kernel, out_shape=jax.ShapeDtypeStruct((32, 40, PA...  8.52 us
    all_to_all x1, starting transfers between devices, per_device(): lax.all_to_all(att, everyone, split_axis=0, concat_axis=0, tiled=True)  8.41 us
  transfers between devices with their start and end apart: 13, of which 7 were waited for; matrix products, arithmetic and copies ran while one was open for 8% of the time, Pallas kernels for 7%

profile of v3, /device:TPU:1, one launch (start us, length us, event | category | flops | bytes accessed | tf_op | source)
XLA Modules:
  0.0 168.2 jit_solution(14448474561000519549)
XLA Ops:
  7.5 8.4 %collective-permute-start = (bf16[2,40,1152]{2,1,0:T(8,128)(2,1)S(1)}, bf16[2,40,1152]{2,1,0:T(8,128)(2,1)S(1)}, u32[]{:S(2)}, u32[]{:S(2)}) collective-permute-start(bf16[2,40,1152]{2,1,0:T(8,128)(2,1)S(1)} %dynamic-slice_bitcast_fusion), channel_id=1, source_target_pairs={{0,33},{1,32},{32,1},{33,0},{2,35},{3,34},{34,3},{35,2},{4,37},{5,... | collective-permute-start | bytes 552968 | tf_op jit(solution)/shard_map/ppermute | solution.py:209
  16.7 1.1 maximum_select_fusion
  18.1 1.6 reshape.75
  21.1 3.8 %all-to-all-start = ((bf16[4,36,432]{2,1,0:T(8,128)(2,1)}), bf16[4,36,432]{2,1,0:T(8,128)(2,1)S(1)}, u32[]{:S(2)}, u32[]{:S(2)}) async-start(bf16[4,36,432]{2,1,0:T(8,128)(2,1)} %reshape.87), calls=%async_computation | async-start | bytes 327680 | tf_op jit(solution)/shard_map/all_to_all | solution.py:219
  25.0 5.3 %all-to-all-done = bf16[4,36,432]{2,1,0:T(8,128)(2,1)S(1)} async-done(((bf16[4,36,432]{2,1,0:T(8,128)(2,1)}), bf16[4,36,432]{2,1,0:T(8,128)(2,1)S(1)}, u32[]{:S(2)}, u32[]{:S(2)}) %all-to-all-start) | async-done | bytes 124448 | tf_op jit(solution)/shard_map/all_to_all | solution.py:219
  30.3 5.5 %collective-permute-done.1 = bf16[36,2944]{1,0:T(8,128)(2,1)S(1)} collective-permute-done((bf16[36,2944]{1,0:T(8,128)(2,1)S(1)}, bf16[36,2944]{1,0:T(8,128)(2,1)S(1)}, u32[]{:S(2)}, u32[]{:S(2)}) %collective-permute-start.1) | collective-permute-done | bytes 212000 | tf_op jit(solution)/shard_map/ppermute | solution.py:214
  37.6 5.7 %all-to-all-start.1 = ((bf16[4,40,1152]{2,1,0:T(8,128)(2,1)}), bf16[4,40,1152]{2,1,0:T(8,128)(2,1)S(1)}, u32[]{:S(2)}, u32[]{:S(2)}) async-start(bf16[4,40,1152]{2,1,0:T(8,128)(2,1)} %pad_maximum_fusion.1), calls=%async_computation.1 | async-start | bytes 737280 | tf_op jit(solution)/shard_map/all_to_all | solution.py:225
  43.2 3.1 %collective-permute-start.2 = (bf16[4,36,432]{2,1,0:T(8,128)(2,1)S(1)}, bf16[4,36,432]{2,1,0:T(8,128)(2,1)S(1)}, u32[]{:S(2)}, u32[]{:S(2)}) collective-permute-start(bf16[4,36,432]{2,1,0:T(8,128)(2,1)S(1)} %all-to-all-done), channel_id=1, source_target_pairs={{0,1},{1,0},{2,3},{3,2},{4,5},{5,4},{6,7},{7,6},{8,9},{9,8},{10,11... | collective-permute-start | bytes 373256 | tf_op jit(solution)/shard_map/ppermute | solution.py:221
  46.3 9.8 %collective-permute-done.2 = bf16[4,36,432]{2,1,0:T(8,128)(2,1)S(1)} collective-permute-done((bf16[4,36,432]{2,1,0:T(8,128)(2,1)S(1)}, bf16[4,36,432]{2,1,0:T(8,128)(2,1)S(1)}, u32[]{:S(2)}, u32[]{:S(2)}) %collective-permute-start.2) | collective-permute-done | bytes 124448 | tf_op jit(solution)/shard_map/ppermute | solution.py:221
  56.9 2.5 %shard_map.82 = bf16[4,4,40,1152]{3,2,1,0:T(8,128)(2,1)} custom-call(f32[3,1152]{1,0:T(4,128)} %mod.1, bf16[4,40,1152]{2,1,0:T(8,128)(2,1)} %copy-done.5), custom_call_target="tpu_custom_call" | custom-call | flops 4000000 | bytes 2000000 | tf_op jit(solution)/shard_map/pallas_call | solution.py:45
  59.3 3.6 %all-to-all-start.2 = ((bf16[4,160,1152]{2,1,0:T(8,128)(2,1)}), bf16[4,160,1152]{2,1,0:T(8,128)(2,1)S(1)}, u32[]{:S(2)}, u32[]{:S(2)}) async-start(bf16[4,160,1152]{2,1,0:T(8,128)(2,1)} %bitcast.40), calls=%async_computation.2 | async-start | bytes 2949120 | tf_op jit(solution)/shard_map/all_to_all | solution.py:236
  63.1 2.9 %collective-permute-start.3 = (bf16[288,432]{1,0:T(8,128)(2,1)S(1)}, bf16[288,432]{1,0:T(8,128)(2,1)S(1)}, u32[]{:S(2)}, u32[]{:S(2)}) collective-permute-start(bf16[288,432]{1,0:T(8,128)(2,1)S(1)} %reshape.79.w0), channel_id=1, source_target_pairs={{8,0},{16,8},{24,16},{0,24},{9,1},{17,9},{25,17},{1,25},{10,2},{18... | collective-permute-start | bytes 746504 | tf_op jit(solution)/shard_map/ppermute | solution.py:232
  67.2 5.2 %collective-permute-done.3.w1 = bf16[288,432]{1,0:T(8,128)(2,1)S(1)} collective-permute-done((bf16[288,432]{1,0:T(8,128)(2,1)S(1)}, bf16[288,432]{1,0:T(8,128)(2,1)S(1)}, u32[]{:S(2)}, u32[]{:S(2)}) %collective-permute-start.3) | collective-permute-done | bytes 248864 | tf_op jit(solution)/shard_map/ppermute | solution.py:232
  72.4 2.5 %collective-permute-done.4.w2 = bf16[288,432]{1,0:T(8,128)(2,1)S(1)} collective-permute-done((bf16[288,432]{1,0:T(8,128)(2,1)S(1)}, bf16[288,432]{1,0:T(8,128)(2,1)S(1)}, u32[]{:S(2)}, u32[]{:S(2)}) %collective-permute-start.4) | collective-permute-done | bytes 248864 | tf_op jit(solution)/shard_map/ppermute | solution.py:232
  75.6 7.2 %collective-permute-done.5.w3 = bf16[288,432]{1,0:T(8,128)(2,1)S(1)} collective-permute-done((bf16[288,432]{1,0:T(8,128)(2,1)S(1)}, bf16[288,432]{1,0:T(8,128)(2,1)S(1)}, u32[]{:S(2)}, u32[]{:S(2)}) %collective-permute-start.5) | collective-permute-done | bytes 248864 | tf_op jit(solution)/shard_map/ppermute | solution.py:232
  84.0 1.9 %copy.44 = bf16[4,1,40,1152]{3,0,2,1:T(4,128)(2,1)} copy(bf16[4,1,40,1152]{3,2,1,0:T(8,128)(2,1)} %param.8) | data formatting | bytes 737280 | tf_op args[0]
  85.8 4.2 %all-to-all-start.4 = ((bf16[4,40,1152]{2,0,1:T(4,128)(2,1)}), bf16[4,40,1152]{2,0,1:T(4,128)(2,1)}, u32[]{:S(2)}, u32[]{:S(2)}) async-start(bf16[4,40,1152]{2,0,1:T(4,128)(2,1)} %bitcast.45), calls=%async_computation.4 | async-start | bytes 737280 | tf_op jit(solution)/shard_map/all_to_all | solution.py:240
  92.2 8.5 %shard_map.83 = bf16[32,40,144]{2,1,0:T(8,128)(2,1)S(1)} custom-call(s32[2]{0:T(128)S(1)} %pad_add_fusion.place, f32[2,256]{1,0:T(2,128)S(1)} %pad.4.gain, bf16[640,1152]{1,0:T(8,128)(2,1)S(1)} %bitcast.39, bf16[640,1152]{1,0:T(8,128)(2,1)S(1)} %collective-permute-done.6.tok_theirs, bf16[288,432]{1,0:T(8,128)(2,1)S(1)} %reshape.79.w0, ...), custom_call_target="tpu_custom_call" | custom-call | flops 5000000000 | bytes 5000000 | tf_op jit(solution)/shard_map/pallas_call | solution.py:101
  101.5 1.7 %reshape.88 = bf16[256,2,360]{2,1,0:T(2,128)(2,1)} reshape(bf16[256,5,144]{2,1,0:T(8,128)(2,1)S(1)} %bitcast.41) | data formatting | bytes 737280
  103.3 8.4 %all-to-all-start.3 = ((bf16[256,2,360]{2,1,0:T(2,128)(2,1)}), bf16[256,2,360]{2,1,0:T(2,128)(2,1)S(1)}, u32[]{:S(2)}, u32[]{:S(2)}) async-start(bf16[256,2,360]{2,1,0:T(2,128)(2,1)} %reshape.88), calls=%async_computation.3 | async-start | bytes 786432 | tf_op jit(solution)/shard_map/all_to_all | solution.py:248
  112.1 1.1 copy.32
  113.3 17.1 %all-to-all-done.3 = bf16[256,2,360]{2,1,0:T(2,128)(2,1)S(1)} async-done(((bf16[256,2,360]{2,1,0:T(2,128)(2,1)}), bf16[256,2,360]{2,1,0:T(2,128)(2,1)S(1)}, u32[]{:S(2)}, u32[]{:S(2)}) %all-to-all-start.3) | async-done | bytes 368672 | tf_op jit(solution)/shard_map/all_to_all | solution.py:248
  132.1 9.2 %shard_map.84 = bf16[160,1152]{1,0:T(8,128)(2,1)S(1)} custom-call(f32[6,1152]{1,0:T(8,128)S(1)} %pad_maximum_fusion.3.mods, f32[2,1152]{1,0:T(2,128)S(1)} %tile.9.gain, bf16[1152,128]{1,0:T(8,128)(2,1)S(1)} %fusion.seg, bf16[160,1152]{1,0:T(8,128)(2,1)S(1)} %reshape.83.back, bf16[160,1152]{1,0:T(8,128)(2,1)S(1)} %reshape.84.res, ...), custom_call_target="tpu_custom_call" | custom-call | flops 1800000000 | bytes 15000000 | tf_op jit(solution)/shard_map/pallas_call | solution.py:175
  141.5 18.9 %all_to_all.50 = bf16[32,5,1152]{2,1,0:T(8,128)(2,1)S(1)} all-to-all(bf16[32,5,1152]{2,1,0:T(8,128)(2,1)S(1)} %reshape.85), channel_id=1, replica_groups=mesh['zl'=4,'core'=2,'y'=4,'x'=4,'zh'=2] {'zl','core'}, dimensions={0} | all-to-all | bytes 737280 | tf_op jit(solution)/shard_map/all_to_all | solution.py:254
  (65 shorter events, 15.4 us)
Async XLA Ops:
  7.5 22.8 %collective-permute-start = (bf16[2,40,1152]{2,1,0:T(8,128)(2,1)S(1)}, bf16[2,40,1152]{2,1,0:T(8,128)(2,1)S(1)}, u32[]{:S(2)}, u32[]{:S(2)}) collective-permute-start(bf16[2,40,1152]{2,1,0:T(8,128)(2,1)S(1)} %dynamic-slice_bitcast_fusion), channel_id=1, source_target_pairs={{0,33},{1,32},{32,1},{33,0},{2,35},{3,34},{34,3},{35,2},{4,37},{5,... | collective-permute-start | bytes 552968 | tf_op jit(solution)/shard_map/ppermute | solution.py:209
  17.8 18.0 %collective-permute-start.1 = (bf16[36,2944]{1,0:T(8,128)(2,1)S(1)}, bf16[36,2944]{1,0:T(8,128)(2,1)S(1)}, u32[]{:S(2)}, u32[]{:S(2)}) collective-permute-start(bf16[36,2944]{1,0:T(8,128)(2,1)S(1)} %maximum_select_fusion), channel_id=1, source_target_pairs={{0,1},{1,0},{2,3},{3,2},{4,5},{5,4},{6,7},{7,6},{8,9},{9,8},{10,11... | collective-permute-start | bytes 635912 | tf_op jit(solution)/shard_map/ppermute | solution.py:214
  20.3 16.5 %copy-start.4 = (bf16[4,1,40,1152]{3,2,1,0:T(8,128)(2,1)S(1)}, bf16[4,1,40,1152]{3,2,1,0:T(8,128)(2,1)}, u32[]{:S(2)}) copy-start(bf16[4,1,40,1152]{3,2,1,0:T(8,128)(2,1)} %param.8) | copy-start | bytes 1105924
  21.1 9.1 %all-to-all-start = ((bf16[4,36,432]{2,1,0:T(8,128)(2,1)}), bf16[4,36,432]{2,1,0:T(8,128)(2,1)S(1)}, u32[]{:S(2)}, u32[]{:S(2)}) async-start(bf16[4,36,432]{2,1,0:T(8,128)(2,1)} %reshape.87), calls=%async_computation | async-start | bytes 327680 | tf_op jit(solution)/shard_map/all_to_all | solution.py:219
  25.0 107.1 %all-gather.2.cloned.1.call-start = ((), (), s32[]{:S(2)}) async-start(), calls=%async_computation.6 | async-start | bytes 13989888 | tf_op jit(solution)/shard_map/all_gather | solution.py:227
  37.6 18.6 %all-to-all-start.1 = ((bf16[4,40,1152]{2,1,0:T(8,128)(2,1)}), bf16[4,40,1152]{2,1,0:T(8,128)(2,1)S(1)}, u32[]{:S(2)}, u32[]{:S(2)}) async-start(bf16[4,40,1152]{2,1,0:T(8,128)(2,1)} %pad_maximum_fusion.1), calls=%async_computation.1 | async-start | bytes 737280 | tf_op jit(solution)/shard_map/all_to_all | solution.py:225
  43.2 12.9 %collective-permute-start.2 = (bf16[4,36,432]{2,1,0:T(8,128)(2,1)S(1)}, bf16[4,36,432]{2,1,0:T(8,128)(2,1)S(1)}, u32[]{:S(2)}, u32[]{:S(2)}) collective-permute-start(bf16[4,36,432]{2,1,0:T(8,128)(2,1)S(1)} %all-to-all-done), channel_id=1, source_target_pairs={{0,1},{1,0},{2,3},{3,2},{4,5},{5,4},{6,7},{7,6},{8,9},{9,8},{10,11... | collective-permute-start | bytes 373256 | tf_op jit(solution)/shard_map/ppermute | solution.py:221
  56.2 0.7 copy-start.5
  59.3 24.1 %all-to-all-start.2 = ((bf16[4,160,1152]{2,1,0:T(8,128)(2,1)}), bf16[4,160,1152]{2,1,0:T(8,128)(2,1)S(1)}, u32[]{:S(2)}, u32[]{:S(2)}) async-start(bf16[4,160,1152]{2,1,0:T(8,128)(2,1)} %bitcast.40), calls=%async_computation.2 | async-start | bytes 2949120 | tf_op jit(solution)/shard_map/all_to_all | solution.py:236
  63.0 27.1 %copy-start.8 = (f32[4,72]{1,0:T(4,128)S(1)}, f32[4,72]{1,0:T(4,128)}, u32[]{:S(2)}) copy-start(f32[4,72]{1,0:T(4,128)} %param.11) | copy-start | bytes 3460
  63.1 9.3 %collective-permute-start.3 = (bf16[288,432]{1,0:T(8,128)(2,1)S(1)}, bf16[288,432]{1,0:T(8,128)(2,1)S(1)}, u32[]{:S(2)}, u32[]{:S(2)}) collective-permute-start(bf16[288,432]{1,0:T(8,128)(2,1)S(1)} %reshape.79.w0), channel_id=1, source_target_pairs={{8,0},{16,8},{24,16},{0,24},{9,1},{17,9},{25,17},{1,25},{10,2},{18... | collective-permute-start | bytes 746504 | tf_op jit(solution)/shard_map/ppermute | solution.py:232
  66.0 8.8 %collective-permute-start.4 = (bf16[288,432]{1,0:T(8,128)(2,1)S(1)}, bf16[288,432]{1,0:T(8,128)(2,1)S(1)}, u32[]{:S(2)}, u32[]{:S(2)}) collective-permute-start(bf16[288,432]{1,0:T(8,128)(2,1)S(1)} %reshape.79.w0), channel_id=1, source_target_pairs={{16,0},{24,8},{0,16},{8,24},{17,1},{25,9},{1,17},{9,25},{18,2},{26... | collective-permute-start | bytes 746504 | tf_op jit(solution)/shard_map/ppermute | solution.py:232
  66.6 16.2 %collective-permute-start.5 = (bf16[288,432]{1,0:T(8,128)(2,1)S(1)}, bf16[288,432]{1,0:T(8,128)(2,1)S(1)}, u32[]{:S(2)}, u32[]{:S(2)}) collective-permute-start(bf16[288,432]{1,0:T(8,128)(2,1)S(1)} %reshape.79.w0), channel_id=1, source_target_pairs={{24,0},{0,8},{8,16},{16,24},{25,1},{1,9},{9,17},{17,25},{26,2},{2,... | collective-permute-start | bytes 746504 | tf_op jit(solution)/shard_map/ppermute | solution.py:232
  74.8 0.7 copy-start
  82.8 0.7 copy-start.2
  83.5 6.8 %collective-permute-start.6 = (bf16[640,1152]{1,0:T(8,128)(2,1)S(1)}, bf16[640,1152]{1,0:T(8,128)(2,1)S(1)}, u32[]{:S(2)}, u32[]{:S(2)}) collective-permute-start(bf16[640,1152]{1,0:T(8,128)(2,1)S(1)} %bitcast.38), channel_id=1, source_target_pairs={{0,32},{32,0},{1,33},{33,1},{2,34},{34,2},{3,35},{35,3},{4,36},{36... | collective-permute-start | bytes 4423688 | tf_op jit(solution)/shard_map/ppermute | solution.py:238
  85.8 17.5 %all-to-all-start.4 = ((bf16[4,40,1152]{2,0,1:T(4,128)(2,1)}), bf16[4,40,1152]{2,0,1:T(4,128)(2,1)}, u32[]{:S(2)}, u32[]{:S(2)}) async-start(bf16[4,40,1152]{2,0,1:T(4,128)(2,1)} %bitcast.45), calls=%async_computation.4 | async-start | bytes 737280 | tf_op jit(solution)/shard_map/all_to_all | solution.py:240
  90.3 1.0 copy-start.1
  91.2 1.0 copy-start.3
  101.5 10.3 %copy-start.6 = (f32[3,1152]{1,0:T(4,128)S(1)}, f32[3,1152]{1,0:T(4,128)}, u32[]{:S(2)}) copy-start(f32[3,1152]{1,0:T(4,128)} %mod.1) | copy-start | bytes 41476
  101.5 10.3 %copy-start.7 = (f32[3,1152]{1,0:T(4,128)S(1)}, f32[3,1152]{1,0:T(4,128)}, u32[]{:S(2)}) copy-start(f32[3,1152]{1,0:T(4,128)} %param.10) | copy-start | bytes 41476
  103.3 27.1 %all-to-all-start.3 = ((bf16[256,2,360]{2,1,0:T(2,128)(2,1)}), bf16[256,2,360]{2,1,0:T(2,128)(2,1)S(1)}, u32[]{:S(2)}, u32[]{:S(2)}) async-start(bf16[256,2,360]{2,1,0:T(2,128)(2,1)} %reshape.88), calls=%async_computation.3 | async-start | bytes 786432 | tf_op jit(solution)/shard_map/all_to_all | solution.py:248
Sparse Core Ops, SparseCore 0:
  36.8 78.4 all-gather.1

commit v4 on v3

--- a/solution.py
+++ b/solution.py
@@ -85,13 +85,18 @@
         q0[at] = jnp.where(first, q, 0.0).astype(BF16)
         q1[at] = jnp.where(second, q, 0.0).astype(BF16)
         k0[at] = head_norm(qkv[:, 256:512], gain[1:2]).astype(BF16)
-        v0[at] = qkv[:, 512:].astype(BF16)
+        v0[at] = jnp.where(lane == PAIR, 1.0, qkv[:, 512:]).astype(BF16)
+
+    def attend(queries):
+        scores = dot_t(queries, k0[...])
+        highest = jnp.max(scores, -1, keepdims=True)
+        expo = jnp.exp2((scores - highest) * (SCALE * EXP2)).astype(BF16)
+        both = dot32(expo, v0[...])
+        return both * (1.0 / both[:, PAIR : PAIR + 1])
 
     for i in range(4):
         at = slice(320 * i, 320 * (i + 1))
-        a = dot32(softmax(dot_t(q0[at], k0[...])), v0[...])
-        b = dot32(softmax(dot_t(q1[at], k0[...])), v0[...])
-        att = jnp.where(first, a, b)[:, :PAIR]
+        att = jnp.where(first, attend(q0[at]), attend(q1[at]))[:, :PAIR]
         from_zh = own_zh if i < 2 else 1 - own_zh
         for j in range(8):
             out[from_zh * 16 + (i % 2) * 8 + j] = att[40 * j : 40 * (j + 1)].astype(BF16)
@@ -111,11 +116,13 @@
     )(place, gain, *operands)
 
 
-def temporal_kernel(mods, gain, seg, back, res, wts, out, wos, wa, wb, wot, sem):
+def temporal_kernel(mods, gain, seg, back, res, wts, out, wos, wq, wk, wv, wot, sem):
     parts = [
         (pl.ds(D, D), slice(REST, REST + D), wos),
-        (pl.ds(0, D), slice(0, CUT), wa),
-        (pl.ds(D, D), slice(0, REST), wb),
+        (pl.ds(0, D), slice(0, D), wq),
+        (pl.ds(0, D), slice(D, 2 * D), wk),
+        (pl.ds(0, D), slice(2 * D, CUT), wv.at[:, : CUT - 2 * D]),
+        (pl.ds(D, D), slice(0, REST), wv.at[:, CUT - 2 * D :]),
         (pl.ds(D, D), slice(REST + D, REST + 2 * D), wot),
     ]
     waits = [
@@ -128,12 +135,6 @@
     hidden = res[...].astype(F32) + mods[2:3] * dot32(back[...], wos[...])
     hidden = hidden.astype(BF16).astype(F32)
     modulated = modulate(hidden, mods[3:4], mods[4:5])
-    waits[1].wait()
-    qkv_a = dot32(modulated, wa[...])
-    waits[2].wait()
-    qkv_b = dot32(modulated, wb[...])
-    q, k = qkv_a[:, :D], qkv_a[:, D : 2 * D]
-    v = jnp.concatenate([qkv_a[:, 2 * D :], qkv_b], 1).astype(BF16)
 
     def head_norm(heads, g):
         square = heads * heads
@@ -147,11 +148,16 @@
         wide = dot_t(r_high, seg[...]) + dot_t(r_mid, seg[...]) + dot_t(r_low, seg[...])
         return heads * wide * g
 
-    q = head_norm(q, gain[0:1])
-    k = head_norm(k, gain[1:2]).astype(BF16)
+    waits[1].wait()
+    q = head_norm(dot32(modulated, wq[...]), gain[0:1])
+    waits[2].wait()
+    k = head_norm(dot32(modulated, wk[...]), gain[1:2]).astype(BF16)
+    waits[3].wait()
+    waits[4].wait()
+    v = dot32(modulated, wv[...]).astype(BF16)
     row = lax.broadcasted_iota(jnp.int32, (160, 160), 0)
     col = lax.broadcasted_iota(jnp.int32, (160, 160), 1)
-    apart = lax.rem(row, 5) != lax.rem(col, 5)
+    apart = row // 32 != col // 32
     tiles = [None] * (D // 128)
     for h in range(HEADS):
         lo, hi = HDIM * h, HDIM * (h + 1)
@@ -167,22 +173,27 @@
             part = att[:, 128 * (t - t0) : 128 * (t - t0 + 1)]
             tiles[t] = part if tiles[t] is None else tiles[t] + part
     attended = jnp.concatenate(tiles, 1).astype(BF16)
-    waits[3].wait()
-    out[...] = (hidden + mods[5:6] * dot32(attended, wot[...])).astype(BF16)
+    waits[5].wait()
+    mixed = hidden + mods[5:6] * dot32(attended, wot[...])
+    for p in range(5):
+        for f in range(8):
+            lo = 32 * p + 4 * f
+            out[f, p] = mixed[lo : lo + 4].astype(BF16)
 
 
 def temporal(mods, gain, seg, back, res, wts):
     return pl.pallas_call(
         temporal_kernel,
-        out_shape=jax.ShapeDtypeStruct((160, D), BF16),
+        out_shape=jax.ShapeDtypeStruct((8, 5, 4, D), BF16),
         in_specs=[VMEM] * 5 + [ANY],
         out_specs=VMEM,
         scratch_shapes=[
             pltpu.VMEM((D, D), BF16),
-            pltpu.VMEM((D, CUT), BF16),
-            pltpu.VMEM((D, REST), BF16),
-            pltpu.VMEM((D, D), BF16),
-            pltpu.SemaphoreType.DMA((4,)),
+            pltpu.VMEM((D, D), BF16),
+            pltpu.VMEM((D, D), BF16),
+            pltpu.VMEM((D, D), BF16),
+            pltpu.VMEM((D, D), BF16),
+            pltpu.SemaphoreType.DMA((6,)),
         ],
         compiler_params=pltpu.CompilerParams(vmem_limit_bytes=40 * 2**20),
         cost_estimate=pl.CostEstimate(
@@ -223,7 +234,8 @@
         [jnp.where(core == 0, stay, moved), jnp.where(core == 0, moved, stay)], 0
     )
     rows = lax.all_to_all(frames, "y", split_axis=0, concat_axis=0, tiled=True)
-    w_far, rows = lax.optimization_barrier((w_far, rows))
+    by_home = latent.reshape(4, 8, 5, D).transpose(1, 2, 0, 3)
+    w_far, rows, by_home = lax.optimization_barrier((w_far, rows, by_home))
     weights = lax.all_gather(in_order(zh, half_r, far_r), ("core", "y", "x"), axis=0, tiled=True)
 
     w_z = jnp.stack([jnp.where(zh == 0, w_x, w_far), jnp.where(zh == 0, w_far, w_x)], 1)
@@ -236,9 +248,9 @@
     ours = lax.all_to_all(copies, "x", split_axis=0, concat_axis=0, tiled=True).reshape(640, D)
     ours, w_y = lax.optimization_barrier((ours, w_y))
     theirs = lax.ppermute(ours, "core", other)
-    home_in, ours = lax.optimization_barrier((latent, ours))
-    home = lax.all_to_all(home_in, ("zl", "core"), split_axis=1, concat_axis=0, tiled=True)
-    home = home.reshape(160, D)
+    by_home, ours = lax.optimization_barrier((by_home, ours))
+    home = lax.all_to_all(by_home, ("zl", "core"), split_axis=0, concat_axis=0, tiled=True)
+    home = home.transpose(1, 0, 2, 3).reshape(160, D)
     gain_s = jnp.pad(jnp.tile(gain[:2], (1, 2)), ((0, 0), (0, 256 - PAIR)))
     att = spatial(place, gain_s, ours, theirs, *w_y)
 
@@ -246,15 +258,13 @@
     att = att.reshape(256, 5, PAIR)
     everyone = ("zl", "zh", "y", "x", "core")
     back = lax.all_to_all(att, everyone, split_axis=0, concat_axis=0, tiled=True)
-    back = back.reshape(4, 2, 2, 2, 8, 5, PAIR).transpose(0, 2, 1, 3, 5, 4, 6).reshape(160, D)
+    back = back.reshape(4, 2, 2, 2, 8, 5, PAIR).transpose(5, 0, 2, 1, 3, 4, 6).reshape(160, D)
 
     seg = (jnp.arange(D)[:, None] // HDIM == jnp.arange(128)[None]).astype(BF16)
     mods = jnp.concatenate([mod_s, mod_t], 0)
     mixed = temporal(mods, jnp.tile(gain[2:], (1, HEADS)), seg, back, home, weights)
-    mixed = lax.all_to_all(
-        mixed.reshape(32, 5, D), ("zl", "core"), split_axis=0, concat_axis=1, tiled=True
-    )
-    return mixed.reshape(4, 1, 40, D)
+    mixed = lax.all_to_all(mixed, ("zl", "core"), split_axis=0, concat_axis=0, tiled=True)
+    return mixed.transpose(2, 0, 1, 3).reshape(4, 1, 40, D)
 
 
 def solution(mesh):

time: 169 us -> 161 us (0.953)
  blocking collectives: 18.9 us -> 14 us
    all_to_all x1, blocking collectives: 18.9 us -> 14 us  [per_device(): lax.all_to_all(mixed, ('zl', 'core'), split_axis=0, concat_axis=0, tiled=...]
  transfers between devices with their start and end apart: 13 -> 13, of which waited for: 7 -> 7; matrix products, arithmetic and copies ran while one was open for 8% -> 8% of each run, Pallas kernels for 7% -> 6%
where the time goes in v4:
time: 161 us; the launch traced here: 160 us
  waiting for transfers between devices  51.8 us (32%)
  starting transfers between devices  42 us (26%)
  Pallas kernels  19 us (12%)
  local copies, waits for them, and re-layouts  16.2 us (10%)
  blocking collectives  14 us (9%)
  between operations  13.7 us (9%)
  other arithmetic  3.22 us (2%)
    all_to_all x1, waiting for transfers between devices, per_device(): lax.all_to_all(att, everyone, split_axis=0, concat_axis=0, tiled=True)  17.1 us
    ppermute x3, waiting for transfers between devices, per_device(): lax.ppermute(w_z, 'y', [((i + k) % 4, i) for i in range(4)])  14.9 us
    all_to_all x1, blocking collectives, per_device(): lax.all_to_all(mixed, ('zl', 'core'), split_axis=0, concat_axis=0, tiled=...  14 us
    ppermute x1, waiting for transfers between devices, per_device(): w_far = lax.ppermute(w_x, 'zh', other)  8.92 us
    pallas_call x1, Pallas kernels, temporal(): pl.pallas_call(temporal_kernel, out_shape=jax.ShapeDtypeStruct((8, 5, 4,...  8.67 us
    all_to_all x1, starting transfers between devices, per_device(): lax.all_to_all(att, everyone, split_axis=0, concat_axis=0, tiled=True)  8.4 us
    ppermute x1, starting transfers between devices, per_device(): moved = lax.ppermute(leave, ('core', 'zh'), [(i, 3 - i) for i in range(4)])  8.39 us
    pallas_call x1, Pallas kernels, spatial(): pl.pallas_call(spatial_kernel, out_shape=jax.ShapeDtypeStruct((32, 40, PA...  7.9 us
  transfers between devices with their start and end apart: 13, of which 7 were waited for; matrix products, arithmetic and copies ran while one was open for 8% of the time, Pallas kernels for 6%

profile of v4, /device:TPU:1, one launch (start us, length us, event | category | flops | bytes accessed | tf_op | source)
XLA Modules:
  0.0 159.9 jit_solution(12903238617496020342)
XLA Ops:
  7.5 8.4 %collective-permute-start = (bf16[2,40,1152]{2,1,0:T(8,128)(2,1)S(1)}, bf16[2,40,1152]{2,1,0:T(8,128)(2,1)S(1)}, u32[]{:S(2)}, u32[]{:S(2)}) collective-permute-start(bf16[2,40,1152]{2,1,0:T(8,128)(2,1)S(1)} %dynamic-slice_bitcast_fusion), channel_id=1, source_target_pairs={{0,33},{1,32},{32,1},{33,0},{2,35},{3,34},{34,3},{35,2},{4,37},{5,... | collective-permute-start | bytes 552968 | tf_op jit(solution)/shard_map/ppermute | solution.py:220
  16.7 1.1 maximum_select_fusion
  18.1 1.6 reshape.67
  21.1 3.8 %all-to-all-start = ((bf16[4,36,432]{2,1,0:T(8,128)(2,1)}), bf16[4,36,432]{2,1,0:T(8,128)(2,1)S(1)}, u32[]{:S(2)}, u32[]{:S(2)}) async-start(bf16[4,36,432]{2,1,0:T(8,128)(2,1)} %reshape.78), calls=%async_computation | async-start | bytes 327680 | tf_op jit(solution)/shard_map/all_to_all | solution.py:230
  25.0 5.3 %all-to-all-done = bf16[4,36,432]{2,1,0:T(8,128)(2,1)S(1)} async-done(((bf16[4,36,432]{2,1,0:T(8,128)(2,1)}), bf16[4,36,432]{2,1,0:T(8,128)(2,1)S(1)}, u32[]{:S(2)}, u32[]{:S(2)}) %all-to-all-start) | async-done | bytes 124448 | tf_op jit(solution)/shard_map/all_to_all | solution.py:230
  30.3 5.5 %collective-permute-done.1 = bf16[36,2944]{1,0:T(8,128)(2,1)S(1)} collective-permute-done((bf16[36,2944]{1,0:T(8,128)(2,1)S(1)}, bf16[36,2944]{1,0:T(8,128)(2,1)S(1)}, u32[]{:S(2)}, u32[]{:S(2)}) %collective-permute-start.1) | collective-permute-done | bytes 212000 | tf_op jit(solution)/shard_map/ppermute | solution.py:225
  37.6 5.7 %all-to-all-start.1 = ((bf16[4,40,1152]{2,1,0:T(8,128)(2,1)}), bf16[4,40,1152]{2,1,0:T(8,128)(2,1)S(1)}, u32[]{:S(2)}, u32[]{:S(2)}) async-start(bf16[4,40,1152]{2,1,0:T(8,128)(2,1)} %pad_maximum_fusion.1), calls=%async_computation.1 | async-start | bytes 737280 | tf_op jit(solution)/shard_map/all_to_all | solution.py:236
  43.2 3.1 %collective-permute-start.2 = (bf16[4,36,432]{2,1,0:T(8,128)(2,1)S(1)}, bf16[4,36,432]{2,1,0:T(8,128)(2,1)S(1)}, u32[]{:S(2)}, u32[]{:S(2)}) collective-permute-start(bf16[4,36,432]{2,1,0:T(8,128)(2,1)S(1)} %all-to-all-done), channel_id=1, source_target_pairs={{0,1},{1,0},{2,3},{3,2},{4,5},{5,4},{6,7},{7,6},{8,9},{9,8},{10,11... | collective-permute-start | bytes 373256 | tf_op jit(solution)/shard_map/ppermute | solution.py:232
  47.2 8.9 %collective-permute-done.2 = bf16[4,36,432]{2,1,0:T(8,128)(2,1)S(1)} collective-permute-done((bf16[4,36,432]{2,1,0:T(8,128)(2,1)S(1)}, bf16[4,36,432]{2,1,0:T(8,128)(2,1)S(1)}, u32[]{:S(2)}, u32[]{:S(2)}) %collective-permute-start.2) | collective-permute-done | bytes 124448 | tf_op jit(solution)/shard_map/ppermute | solution.py:232
  56.9 2.5 %shard_map.82 = bf16[4,4,40,1152]{3,2,1,0:T(8,128)(2,1)} custom-call(f32[3,1152]{1,0:T(4,128)} %mod.1, bf16[4,40,1152]{2,1,0:T(8,128)(2,1)} %copy-done.5), custom_call_target="tpu_custom_call" | custom-call | flops 4000000 | bytes 2000000 | tf_op jit(solution)/shard_map/pallas_call | solution.py:45
  59.3 3.6 %all-to-all-start.2 = ((bf16[4,160,1152]{2,1,0:T(8,128)(2,1)}), bf16[4,160,1152]{2,1,0:T(8,128)(2,1)S(1)}, u32[]{:S(2)}, u32[]{:S(2)}) async-start(bf16[4,160,1152]{2,1,0:T(8,128)(2,1)} %bitcast.37), calls=%async_computation.2 | async-start | bytes 2949120 | tf_op jit(solution)/shard_map/all_to_all | solution.py:248
  63.1 2.9 %collective-permute-start.3 = (bf16[288,432]{1,0:T(8,128)(2,1)S(1)}, bf16[288,432]{1,0:T(8,128)(2,1)S(1)}, u32[]{:S(2)}, u32[]{:S(2)}) collective-permute-start(bf16[288,432]{1,0:T(8,128)(2,1)S(1)} %reshape.71.w0), channel_id=1, source_target_pairs={{8,0},{16,8},{24,16},{0,24},{9,1},{17,9},{25,17},{1,25},{10,2},{18... | collective-permute-start | bytes 746504 | tf_op jit(solution)/shard_map/ppermute | solution.py:244
  67.2 5.2 %collective-permute-done.3.w1 = bf16[288,432]{1,0:T(8,128)(2,1)S(1)} collective-permute-done((bf16[288,432]{1,0:T(8,128)(2,1)S(1)}, bf16[288,432]{1,0:T(8,128)(2,1)S(1)}, u32[]{:S(2)}, u32[]{:S(2)}) %collective-permute-start.3) | collective-permute-done | bytes 248864 | tf_op jit(solution)/shard_map/ppermute | solution.py:244
  72.4 2.5 %collective-permute-done.4.w2 = bf16[288,432]{1,0:T(8,128)(2,1)S(1)} collective-permute-done((bf16[288,432]{1,0:T(8,128)(2,1)S(1)}, bf16[288,432]{1,0:T(8,128)(2,1)S(1)}, u32[]{:S(2)}, u32[]{:S(2)}) %collective-permute-start.4) | collective-permute-done | bytes 248864 | tf_op jit(solution)/shard_map/ppermute | solution.py:244
  75.6 7.2 %collective-permute-done.5.w3 = bf16[288,432]{1,0:T(8,128)(2,1)S(1)} collective-permute-done((bf16[288,432]{1,0:T(8,128)(2,1)S(1)}, bf16[288,432]{1,0:T(8,128)(2,1)S(1)}, u32[]{:S(2)}, u32[]{:S(2)}) %collective-permute-start.5) | collective-permute-done | bytes 248864 | tf_op jit(solution)/shard_map/ppermute | solution.py:244
  84.0 4.2 %all-to-all-start.4 = ((bf16[8,5,4,1152]{3,2,1,0:T(4,128)(2,1)}), bf16[8,5,4,1152]{3,2,1,0:T(4,128)(2,1)}, u32[]{:S(2)}, u32[]{:S(2)}) async-start(bf16[8,5,4,1152]{3,2,1,0:T(4,128)(2,1)} %bitcast.41), calls=%async_computation.4 | async-start | bytes 737280 | tf_op jit(solution)/shard_map/all_to_all | solution.py:252
  88.4 1.0 copy-done.1
  90.4 7.9 %shard_map.83 = bf16[32,40,144]{2,1,0:T(8,128)(2,1)S(1)} custom-call(s32[2]{0:T(128)S(1)} %pad_add_fusion.place, f32[2,256]{1,0:T(2,128)S(1)} %pad.4.gain, bf16[640,1152]{1,0:T(8,128)(2,1)S(1)} %bitcast.36, bf16[640,1152]{1,0:T(8,128)(2,1)S(1)} %collective-permute-done.6.tok_theirs, bf16[288,432]{1,0:T(8,128)(2,1)S(1)} %reshape.71.w0, ...), custom_call_target="tpu_custom_call" | custom-call | flops 5000000000 | bytes 5000000 | tf_op jit(solution)/shard_map/pallas_call | solution.py:106
  99.1 1.7 %reshape.79 = bf16[256,2,360]{2,1,0:T(2,128)(2,1)} reshape(bf16[256,5,144]{2,1,0:T(8,128)(2,1)S(1)} %bitcast.38) | data formatting | bytes 737280
  100.8 8.4 %all-to-all-start.3 = ((bf16[256,2,360]{2,1,0:T(2,128)(2,1)}), bf16[256,2,360]{2,1,0:T(2,128)(2,1)S(1)}, u32[]{:S(2)}, u32[]{:S(2)}) async-start(bf16[256,2,360]{2,1,0:T(2,128)(2,1)} %reshape.79), calls=%async_computation.3 | async-start | bytes 786432 | tf_op jit(solution)/shard_map/all_to_all | solution.py:260
  109.6 1.1 copy.31
  110.8 17.1 %all-to-all-done.3 = bf16[256,2,360]{2,1,0:T(2,128)(2,1)S(1)} async-done(((bf16[256,2,360]{2,1,0:T(2,128)(2,1)}), bf16[256,2,360]{2,1,0:T(2,128)(2,1)S(1)}, u32[]{:S(2)}, u32[]{:S(2)}) %all-to-all-start.3) | async-done | bytes 368672 | tf_op jit(solution)/shard_map/all_to_all | solution.py:260
  129.6 8.7 %shard_map.84 = bf16[8,5,4,1152]{3,2,1,0:T(4,128)(2,1)S(1)} custom-call(f32[6,1152]{1,0:T(8,128)S(1)} %pad_maximum_fusion.3.mods, f32[2,1152]{1,0:T(2,128)S(1)} %tile.9.gain, bf16[1152,128]{1,0:T(8,128)(2,1)S(1)} %fusion.seg, bf16[160,1152]{1,0:T(8,128)(2,1)S(1)} %reshape.75.back, bf16[160,1152]{1,0:T(8,128)(2,1)S(1)} %reshape.76.res, ...), custom_call_target="tpu_custom_call" | custom-call | flops 1800000000 | bytes 15000000 | tf_op jit(solution)/shard_map/pallas_call | solution.py:185
  138.3 14.0 %all_to_all.30 = bf16[8,5,4,1152]{3,2,1,0:T(4,128)(2,1)S(1)} all-to-all(bf16[8,5,4,1152]{3,2,1,0:T(4,128)(2,1)S(1)} %shard_map.84), channel_id=1, replica_groups=mesh['zl'=4,'core'=2,'y'=4,'x'=4,'zh'=2] {'zl','core'}, dimensions={0} | all-to-all | bytes 737280 | tf_op jit(solution)/shard_map/all_to_all | solution.py:266
  (63 shorter events, 14.9 us)
Async XLA Ops:
  7.5 22.8 %collective-permute-start = (bf16[2,40,1152]{2,1,0:T(8,128)(2,1)S(1)}, bf16[2,40,1152]{2,1,0:T(8,128)(2,1)S(1)}, u32[]{:S(2)}, u32[]{:S(2)}) collective-permute-start(bf16[2,40,1152]{2,1,0:T(8,128)(2,1)S(1)} %dynamic-slice_bitcast_fusion), channel_id=1, source_target_pairs={{0,33},{1,32},{32,1},{33,0},{2,35},{3,34},{34,3},{35,2},{4,37},{5,... | collective-permute-start | bytes 552968 | tf_op jit(solution)/shard_map/ppermute | solution.py:220
  17.8 18.0 %collective-permute-start.1 = (bf16[36,2944]{1,0:T(8,128)(2,1)S(1)}, bf16[36,2944]{1,0:T(8,128)(2,1)S(1)}, u32[]{:S(2)}, u32[]{:S(2)}) collective-permute-start(bf16[36,2944]{1,0:T(8,128)(2,1)S(1)} %maximum_select_fusion), channel_id=1, source_target_pairs={{0,1},{1,0},{2,3},{3,2},{4,5},{5,4},{6,7},{7,6},{8,9},{9,8},{10,11... | collective-permute-start | bytes 635912 | tf_op jit(solution)/shard_map/ppermute | solution.py:225
  20.3 16.5 %copy-start.4 = (bf16[4,1,40,1152]{3,2,1,0:T(8,128)(2,1)S(1)}, bf16[4,1,40,1152]{3,2,1,0:T(8,128)(2,1)}, u32[]{:S(2)}) copy-start(bf16[4,1,40,1152]{3,2,1,0:T(8,128)(2,1)} %param.8) | copy-start | bytes 1105924
  21.1 9.1 %all-to-all-start = ((bf16[4,36,432]{2,1,0:T(8,128)(2,1)}), bf16[4,36,432]{2,1,0:T(8,128)(2,1)S(1)}, u32[]{:S(2)}, u32[]{:S(2)}) async-start(bf16[4,36,432]{2,1,0:T(8,128)(2,1)} %reshape.78), calls=%async_computation | async-start | bytes 327680 | tf_op jit(solution)/shard_map/all_to_all | solution.py:230
  25.0 104.6 %all-gather.2.cloned.1.call-start = ((), (), s32[]{:S(2)}) async-start(), calls=%async_computation.6 | async-start | bytes 13989888 | tf_op jit(solution)/shard_map/all_gather | solution.py:239
  37.6 18.6 %all-to-all-start.1 = ((bf16[4,40,1152]{2,1,0:T(8,128)(2,1)}), bf16[4,40,1152]{2,1,0:T(8,128)(2,1)S(1)}, u32[]{:S(2)}, u32[]{:S(2)}) async-start(bf16[4,40,1152]{2,1,0:T(8,128)(2,1)} %pad_maximum_fusion.1), calls=%async_computation.1 | async-start | bytes 737280 | tf_op jit(solution)/shard_map/all_to_all | solution.py:236
  43.2 12.9 %collective-permute-start.2 = (bf16[4,36,432]{2,1,0:T(8,128)(2,1)S(1)}, bf16[4,36,432]{2,1,0:T(8,128)(2,1)S(1)}, u32[]{:S(2)}, u32[]{:S(2)}) collective-permute-start(bf16[4,36,432]{2,1,0:T(8,128)(2,1)S(1)} %all-to-all-done), channel_id=1, source_target_pairs={{0,1},{1,0},{2,3},{3,2},{4,5},{5,4},{6,7},{7,6},{8,9},{9,8},{10,11... | collective-permute-start | bytes 373256 | tf_op jit(solution)/shard_map/ppermute | solution.py:232
  56.2 0.7 copy-start.5
  59.3 24.1 %all-to-all-start.2 = ((bf16[4,160,1152]{2,1,0:T(8,128)(2,1)}), bf16[4,160,1152]{2,1,0:T(8,128)(2,1)S(1)}, u32[]{:S(2)}, u32[]{:S(2)}) async-start(bf16[4,160,1152]{2,1,0:T(8,128)(2,1)} %bitcast.37), calls=%async_computation.2 | async-start | bytes 2949120 | tf_op jit(solution)/shard_map/all_to_all | solution.py:248
  62.9 25.2 %copy-start.8 = (f32[4,72]{1,0:T(4,128)S(1)}, f32[4,72]{1,0:T(4,128)}, u32[]{:S(2)}) copy-start(f32[4,72]{1,0:T(4,128)} %param.11) | copy-start | bytes 3460
  63.1 9.3 %collective-permute-start.3 = (bf16[288,432]{1,0:T(8,128)(2,1)S(1)}, bf16[288,432]{1,0:T(8,128)(2,1)S(1)}, u32[]{:S(2)}, u32[]{:S(2)}) collective-permute-start(bf16[288,432]{1,0:T(8,128)(2,1)S(1)} %reshape.71.w0), channel_id=1, source_target_pairs={{8,0},{16,8},{24,16},{0,24},{9,1},{17,9},{25,17},{1,25},{10,2},{18... | collective-permute-start | bytes 746504 | tf_op jit(solution)/shard_map/ppermute | solution.py:244
  66.0 8.8 %collective-permute-start.4 = (bf16[288,432]{1,0:T(8,128)(2,1)S(1)}, bf16[288,432]{1,0:T(8,128)(2,1)S(1)}, u32[]{:S(2)}, u32[]{:S(2)}) collective-permute-start(bf16[288,432]{1,0:T(8,128)(2,1)S(1)} %reshape.71.w0), channel_id=1, source_target_pairs={{16,0},{24,8},{0,16},{8,24},{17,1},{25,9},{1,17},{9,25},{18,2},{26... | collective-permute-start | bytes 746504 | tf_op jit(solution)/shard_map/ppermute | solution.py:244
  66.6 16.2 %collective-permute-start.5 = (bf16[288,432]{1,0:T(8,128)(2,1)S(1)}, bf16[288,432]{1,0:T(8,128)(2,1)S(1)}, u32[]{:S(2)}, u32[]{:S(2)}) collective-permute-start(bf16[288,432]{1,0:T(8,128)(2,1)S(1)} %reshape.71.w0), channel_id=1, source_target_pairs={{24,0},{0,8},{8,16},{16,24},{25,1},{1,9},{9,17},{17,25},{26,2},{2,... | collective-permute-start | bytes 746504 | tf_op jit(solution)/shard_map/ppermute | solution.py:244
  74.8 0.7 copy-start
  82.8 0.7 copy-start.2
  83.5 4.9 %collective-permute-start.6 = (bf16[640,1152]{1,0:T(8,128)(2,1)S(1)}, bf16[640,1152]{1,0:T(8,128)(2,1)S(1)}, u32[]{:S(2)}, u32[]{:S(2)}) collective-permute-start(bf16[640,1152]{1,0:T(8,128)(2,1)S(1)} %bitcast.35), channel_id=1, source_target_pairs={{0,32},{32,0},{1,33},{33,1},{2,34},{34,2},{3,35},{35,3},{4,36},{36... | collective-permute-start | bytes 4423688 | tf_op jit(solution)/shard_map/ppermute | solution.py:250
  84.0 16.8 %all-to-all-start.4 = ((bf16[8,5,4,1152]{3,2,1,0:T(4,128)(2,1)}), bf16[8,5,4,1152]{3,2,1,0:T(4,128)(2,1)}, u32[]{:S(2)}, u32[]{:S(2)}) async-start(bf16[8,5,4,1152]{3,2,1,0:T(4,128)(2,1)} %bitcast.41), calls=%async_computation.4 | async-start | bytes 737280 | tf_op jit(solution)/shard_map/all_to_all | solution.py:252
  88.4 1.0 copy-start.1
  89.4 1.0 copy-start.3
  99.0 10.3 %copy-start.6 = (f32[3,1152]{1,0:T(4,128)S(1)}, f32[3,1152]{1,0:T(4,128)}, u32[]{:S(2)}) copy-start(f32[3,1152]{1,0:T(4,128)} %mod.1) | copy-start | bytes 41476
  99.1 10.3 %copy-start.7 = (f32[3,1152]{1,0:T(4,128)S(1)}, f32[3,1152]{1,0:T(4,128)}, u32[]{:S(2)}) copy-start(f32[3,1152]{1,0:T(4,128)} %param.10) | copy-start | bytes 41476
  100.8 27.1 %all-to-all-start.3 = ((bf16[256,2,360]{2,1,0:T(2,128)(2,1)}), bf16[256,2,360]{2,1,0:T(2,128)(2,1)S(1)}, u32[]{:S(2)}, u32[]{:S(2)}) async-start(bf16[256,2,360]{2,1,0:T(2,128)(2,1)} %reshape.79), calls=%async_computation.3 | async-start | bytes 786432 | tf_op jit(solution)/shard_map/all_to_all | solution.py:260
Sparse Core Ops, SparseCore 0:
  36.8 78.7 all-gather.1

commit v5 on v4

--- a/solution.py
+++ b/solution.py
@@ -47,6 +47,7 @@
         out_shape=jax.ShapeDtypeStruct((4, 4, 40, D), BF16),
         in_specs=[VMEM] * 2,
         out_specs=VMEM,
+        compiler_params=pltpu.CompilerParams(vmem_limit_bytes=12 * 2**20),
         cost_estimate=pl.CostEstimate(flops=4_000_000, bytes_accessed=2_000_000, transcendentals=0),
     )(mod, rows)
 
@@ -235,7 +236,9 @@
     )
     rows = lax.all_to_all(frames, "y", split_axis=0, concat_axis=0, tiled=True)
     by_home = latent.reshape(4, 8, 5, D).transpose(1, 2, 0, 3)
-    w_far, rows, by_home = lax.optimization_barrier((w_far, rows, by_home))
+    rows, by_home = lax.optimization_barrier((rows, by_home))
+    copies = norm_copies(mod_s, rows).reshape(4, 160, D)
+    copies, w_far = lax.optimization_barrier((copies, w_far))
     weights = lax.all_gather(in_order(zh, half_r, far_r), ("core", "y", "x"), axis=0, tiled=True)
 
     w_z = jnp.stack([jnp.where(zh == 0, w_x, w_far), jnp.where(zh == 0, w_far, w_x)], 1)
@@ -244,7 +247,6 @@
         lax.ppermute(w_z, "y", [((i + k) % 4, i) for i in range(4)]) for k in (1, 2, 3)
     ]
 
-    copies = norm_copies(mod_s, rows).reshape(4, 160, D)
     ours = lax.all_to_all(copies, "x", split_axis=0, concat_axis=0, tiled=True).reshape(640, D)
     ours, w_y = lax.optimization_barrier((ours, w_y))
     theirs = lax.ppermute(ours, "core", other)

time: 161 us -> 160 us (level)
  waiting for transfers between devices: 51.8 us -> 49.6 us
    ppermute x1, waiting for transfers between devices: 8.92 us -> 4.97 us  [per_device(): w_far = lax.ppermute(w_x, 'zh', other)]
    all_to_all x1, waiting for transfers between devices: 0.01 us -> 2.52 us  [per_device(): rows = lax.all_to_all(frames, 'y', split_axis=0, concat_axis=0, tiled=True)]
    unnamed x21 -> x23, local copies, waits for them, and re-layouts: 7.68 us -> 8.63 us
  transfers between devices with their start and end apart: 13 -> 13, of which waited for: 7 -> 8; matrix products, arithmetic and copies ran while one was open for 8% -> 8% of each run, Pallas kernels for 6% -> 6%
where the time goes in v5:
time: 160 us; the launch traced here: 159 us
  waiting for transfers between devices  49.6 us (31%)
  starting transfers between devices  42.9 us (27%)
  Pallas kernels  18.1 us (11%)
  local copies, waits for them, and re-layouts  17.2 us (11%)
  blocking collectives  14.1 us (9%)
  between operations  13.7 us (9%)
  other arithmetic  3.23 us (2%)
    all_to_all x1, waiting for transfers between devices, per_device(): lax.all_to_all(att, everyone, split_axis=0, concat_axis=0, tiled=True)  17.1 us
    ppermute x3, waiting for transfers between devices, per_device(): lax.ppermute(w_z, 'y', [((i + k) % 4, i) for i in range(4)])  14.2 us
    all_to_all x1, blocking collectives, per_device(): lax.all_to_all(mixed, ('zl', 'core'), split_axis=0, concat_axis=0, tiled=...  14.1 us
    all_to_all x1, starting transfers between devices, per_device(): lax.all_to_all(att, everyone, split_axis=0, concat_axis=0, tiled=True)  9.25 us
    pallas_call x1, Pallas kernels, temporal(): pl.pallas_call(temporal_kernel, out_shape=jax.ShapeDtypeStruct((8, 5, 4,...  8.68 us
    unnamed x23, local copies, waits for them, and re-layouts  8.63 us
    ppermute x1, starting transfers between devices, per_device(): moved = lax.ppermute(leave, ('core', 'zh'), [(i, 3 - i) for i in range(4)])  8.39 us
    pallas_call x1, Pallas kernels, spatial(): pl.pallas_call(spatial_kernel, out_shape=jax.ShapeDtypeStruct((32, 40, PA...  7.97 us
  transfers between devices with their start and end apart: 13, of which 8 were waited for; matrix products, arithmetic and copies ran while one was open for 8% of the time, Pallas kernels for 6%

profile of v5, /device:TPU:1, one launch (start us, length us, event | category | flops | bytes accessed | tf_op | source)
XLA Modules:
  0.0 158.7 jit_solution(10001721848385281304)
XLA Ops:
  7.5 8.4 %collective-permute-start = (bf16[2,40,1152]{2,1,0:T(8,128)(2,1)S(1)}, bf16[2,40,1152]{2,1,0:T(8,128)(2,1)S(1)}, u32[]{:S(2)}, u32[]{:S(2)}) collective-permute-start(bf16[2,40,1152]{2,1,0:T(8,128)(2,1)S(1)} %dynamic-slice_bitcast_fusion), channel_id=1, source_target_pairs={{0,33},{1,32},{32,1},{33,0},{2,35},{3,34},{34,3},{35,2},{4,37},{5,... | collective-permute-start | bytes 552968 | tf_op jit(solution)/shard_map/ppermute | solution.py:221
  16.7 1.1 maximum_select_fusion
  18.1 1.6 reshape.67
  21.1 3.8 %all-to-all-start = ((bf16[4,36,432]{2,1,0:T(8,128)(2,1)}), bf16[4,36,432]{2,1,0:T(8,128)(2,1)S(1)}, u32[]{:S(2)}, u32[]{:S(2)}) async-start(bf16[4,36,432]{2,1,0:T(8,128)(2,1)} %reshape.78), calls=%async_computation | async-start | bytes 327680 | tf_op jit(solution)/shard_map/all_to_all | solution.py:231
  25.0 5.3 %all-to-all-done = bf16[4,36,432]{2,1,0:T(8,128)(2,1)S(1)} async-done(((bf16[4,36,432]{2,1,0:T(8,128)(2,1)}), bf16[4,36,432]{2,1,0:T(8,128)(2,1)S(1)}, u32[]{:S(2)}, u32[]{:S(2)}) %all-to-all-start) | async-done | bytes 124448 | tf_op jit(solution)/shard_map/all_to_all | solution.py:231
  30.3 5.5 %collective-permute-done.1 = bf16[36,2944]{1,0:T(8,128)(2,1)S(1)} collective-permute-done((bf16[36,2944]{1,0:T(8,128)(2,1)S(1)}, bf16[36,2944]{1,0:T(8,128)(2,1)S(1)}, u32[]{:S(2)}, u32[]{:S(2)}) %collective-permute-start.1) | collective-permute-done | bytes 212000 | tf_op jit(solution)/shard_map/ppermute | solution.py:226
  37.6 5.7 %all-to-all-start.1 = ((bf16[4,40,1152]{2,1,0:T(8,128)(2,1)}), bf16[4,40,1152]{2,1,0:T(8,128)(2,1)S(1)}, u32[]{:S(2)}, u32[]{:S(2)}) async-start(bf16[4,40,1152]{2,1,0:T(8,128)(2,1)} %pad_maximum_fusion.1), calls=%async_computation.1 | async-start | bytes 737280 | tf_op jit(solution)/shard_map/all_to_all | solution.py:237
  43.2 3.1 %collective-permute-start.2 = (bf16[4,36,432]{2,1,0:T(8,128)(2,1)S(1)}, bf16[4,36,432]{2,1,0:T(8,128)(2,1)S(1)}, u32[]{:S(2)}, u32[]{:S(2)}) collective-permute-start(bf16[4,36,432]{2,1,0:T(8,128)(2,1)S(1)} %all-to-all-done), channel_id=1, source_target_pairs={{0,1},{1,0},{2,3},{3,2},{4,5},{5,4},{6,7},{7,6},{8,9},{9,8},{10,11... | collective-permute-start | bytes 373256 | tf_op jit(solution)/shard_map/ppermute | solution.py:233
  47.2 2.5 %all-to-all-done.1.rows = bf16[4,40,1152]{2,1,0:T(8,128)(2,1)S(1)} async-done(((bf16[4,40,1152]{2,1,0:T(8,128)(2,1)}), bf16[4,40,1152]{2,1,0:T(8,128)(2,1)S(1)}, u32[]{:S(2)}, u32[]{:S(2)}) %all-to-all-start.1) | async-done | bytes 368672 | tf_op jit(solution)/shard_map/all_to_all | solution.py:237
  49.8 1.4 shard_map.82
  51.2 5.0 %collective-permute-done.2 = bf16[4,36,432]{2,1,0:T(8,128)(2,1)S(1)} collective-permute-done((bf16[4,36,432]{2,1,0:T(8,128)(2,1)S(1)}, bf16[4,36,432]{2,1,0:T(8,128)(2,1)S(1)}, u32[]{:S(2)}, u32[]{:S(2)}) %collective-permute-start.2) | collective-permute-done | bytes 124448 | tf_op jit(solution)/shard_map/ppermute | solution.py:233
  56.2 3.6 %all-to-all-start.2 = ((bf16[4,160,1152]{2,1,0:T(8,128)(2,1)}), bf16[4,160,1152]{2,1,0:T(8,128)(2,1)S(1)}, u32[]{:S(2)}, u32[]{:S(2)}) async-start(bf16[4,160,1152]{2,1,0:T(8,128)(2,1)} %bitcast.8), calls=%async_computation.2 | async-start | bytes 2949120 | tf_op jit(solution)/shard_map/all_to_all | solution.py:250
  60.0 2.9 %collective-permute-start.3 = (bf16[288,432]{1,0:T(8,128)(2,1)S(1)}, bf16[288,432]{1,0:T(8,128)(2,1)S(1)}, u32[]{:S(2)}, u32[]{:S(2)}) collective-permute-start(bf16[288,432]{1,0:T(8,128)(2,1)S(1)} %reshape.71.w0), channel_id=1, source_target_pairs={{8,0},{16,8},{24,16},{0,24},{9,1},{17,9},{25,17},{1,25},{10,2},{18... | collective-permute-start | bytes 746504 | tf_op jit(solution)/shard_map/ppermute | solution.py:247
  64.0 5.4 %collective-permute-done.3.w1 = bf16[288,432]{1,0:T(8,128)(2,1)S(1)} collective-permute-done((bf16[288,432]{1,0:T(8,128)(2,1)S(1)}, bf16[288,432]{1,0:T(8,128)(2,1)S(1)}, u32[]{:S(2)}, u32[]{:S(2)}) %collective-permute-start.3) | collective-permute-done | bytes 248864 | tf_op jit(solution)/shard_map/ppermute | solution.py:247
  70.1 1.6 collective-permute-done.4.w2
  72.4 7.2 %collective-permute-done.5.w3 = bf16[288,432]{1,0:T(8,128)(2,1)S(1)} collective-permute-done((bf16[288,432]{1,0:T(8,128)(2,1)S(1)}, bf16[288,432]{1,0:T(8,128)(2,1)S(1)}, u32[]{:S(2)}, u32[]{:S(2)}) %collective-permute-start.5) | collective-permute-done | bytes 248864 | tf_op jit(solution)/shard_map/ppermute | solution.py:247
  80.9 4.2 %all-to-all-start.4 = ((bf16[8,5,4,1152]{3,2,1,0:T(4,128)(2,1)}), bf16[8,5,4,1152]{3,2,1,0:T(4,128)(2,1)}, u32[]{:S(2)}, u32[]{:S(2)}) async-start(bf16[8,5,4,1152]{3,2,1,0:T(4,128)(2,1)} %bitcast.40), calls=%async_computation.4 | async-start | bytes 737280 | tf_op jit(solution)/shard_map/all_to_all | solution.py:254
  88.2 8.0 %shard_map.83 = bf16[32,40,144]{2,1,0:T(8,128)(2,1)S(1)} custom-call(s32[2]{0:T(128)S(1)} %pad_add_fusion.place, f32[2,256]{1,0:T(2,128)S(1)} %pad.4.gain, bf16[640,1152]{1,0:T(8,128)(2,1)S(1)} %bitcast.36, bf16[640,1152]{1,0:T(8,128)(2,1)S(1)} %collective-permute-done.6.tok_theirs, bf16[288,432]{1,0:T(8,128)(2,1)S(1)} %reshape.71.w0, ...), custom_call_target="tpu_custom_call" | custom-call | flops 5000000000 | bytes 5000000 | tf_op jit(solution)/shard_map/pallas_call | solution.py:107
  97.0 1.8 %reshape.79 = bf16[256,2,360]{2,1,0:T(2,128)(2,1)} reshape(bf16[256,5,144]{2,1,0:T(8,128)(2,1)S(1)} %bitcast.37) | data formatting | bytes 737280
  98.7 9.2 %all-to-all-start.3 = ((bf16[256,2,360]{2,1,0:T(2,128)(2,1)}), bf16[256,2,360]{2,1,0:T(2,128)(2,1)S(1)}, u32[]{:S(2)}, u32[]{:S(2)}) async-start(bf16[256,2,360]{2,1,0:T(2,128)(2,1)} %reshape.79), calls=%async_computation.3 | async-start | bytes 786432 | tf_op jit(solution)/shard_map/all_to_all | solution.py:262
  108.4 1.1 copy.31
  109.6 17.1 %all-to-all-done.3 = bf16[256,2,360]{2,1,0:T(2,128)(2,1)S(1)} async-done(((bf16[256,2,360]{2,1,0:T(2,128)(2,1)}), bf16[256,2,360]{2,1,0:T(2,128)(2,1)S(1)}, u32[]{:S(2)}, u32[]{:S(2)}) %all-to-all-start.3) | async-done | bytes 368672 | tf_op jit(solution)/shard_map/all_to_all | solution.py:262
  128.4 8.7 %shard_map.84 = bf16[8,5,4,1152]{3,2,1,0:T(4,128)(2,1)S(1)} custom-call(f32[6,1152]{1,0:T(8,128)S(1)} %pad_maximum_fusion.3.mods, f32[2,1152]{1,0:T(2,128)S(1)} %tile.9.gain, bf16[1152,128]{1,0:T(8,128)(2,1)S(1)} %fusion.seg, bf16[160,1152]{1,0:T(8,128)(2,1)S(1)} %reshape.75.back, bf16[160,1152]{1,0:T(8,128)(2,1)S(1)} %reshape.76.res, ...), custom_call_target="tpu_custom_call" | custom-call | flops 1800000000 | bytes 15000000 | tf_op jit(solution)/shard_map/pallas_call | solution.py:186
  137.0 14.1 %all_to_all.30 = bf16[8,5,4,1152]{3,2,1,0:T(4,128)(2,1)S(1)} all-to-all(bf16[8,5,4,1152]{3,2,1,0:T(4,128)(2,1)S(1)} %shard_map.84), channel_id=1, replica_groups=mesh['zl'=4,'core'=2,'y'=4,'x'=4,'zh'=2] {'zl','core'}, dimensions={0} | all-to-all | bytes 737280 | tf_op jit(solution)/shard_map/all_to_all | solution.py:268
  (65 shorter events, 16.9 us)
Async XLA Ops:
  7.5 22.8 %collective-permute-start = (bf16[2,40,1152]{2,1,0:T(8,128)(2,1)S(1)}, bf16[2,40,1152]{2,1,0:T(8,128)(2,1)S(1)}, u32[]{:S(2)}, u32[]{:S(2)}) collective-permute-start(bf16[2,40,1152]{2,1,0:T(8,128)(2,1)S(1)} %dynamic-slice_bitcast_fusion), channel_id=1, source_target_pairs={{0,33},{1,32},{32,1},{33,0},{2,35},{3,34},{34,3},{35,2},{4,37},{5,... | collective-permute-start | bytes 552968 | tf_op jit(solution)/shard_map/ppermute | solution.py:221
  17.8 18.0 %collective-permute-start.1 = (bf16[36,2944]{1,0:T(8,128)(2,1)S(1)}, bf16[36,2944]{1,0:T(8,128)(2,1)S(1)}, u32[]{:S(2)}, u32[]{:S(2)}) collective-permute-start(bf16[36,2944]{1,0:T(8,128)(2,1)S(1)} %maximum_select_fusion), channel_id=1, source_target_pairs={{0,1},{1,0},{2,3},{3,2},{4,5},{5,4},{6,7},{7,6},{8,9},{9,8},{10,11... | collective-permute-start | bytes 635912 | tf_op jit(solution)/shard_map/ppermute | solution.py:226
  20.3 16.5 %copy-start.7 = (bf16[4,1,40,1152]{3,2,1,0:T(8,128)(2,1)S(1)}, bf16[4,1,40,1152]{3,2,1,0:T(8,128)(2,1)}, u32[]{:S(2)}) copy-start(bf16[4,1,40,1152]{3,2,1,0:T(8,128)(2,1)} %param.8) | copy-start | bytes 1105924
  21.1 9.1 %all-to-all-start = ((bf16[4,36,432]{2,1,0:T(8,128)(2,1)}), bf16[4,36,432]{2,1,0:T(8,128)(2,1)S(1)}, u32[]{:S(2)}, u32[]{:S(2)}) async-start(bf16[4,36,432]{2,1,0:T(8,128)(2,1)} %reshape.78), calls=%async_computation | async-start | bytes 327680 | tf_op jit(solution)/shard_map/all_to_all | solution.py:231
  25.0 103.4 %all-gather.2.cloned.1.call-start = ((), (), s32[]{:S(2)}) async-start(), calls=%async_computation.6 | async-start | bytes 13989888 | tf_op jit(solution)/shard_map/all_gather | solution.py:242
  36.7 13.0 %copy-start = (f32[3,1152]{1,0:T(4,128)S(1)}, f32[3,1152]{1,0:T(4,128)}, u32[]{:S(2)}) copy-start(f32[3,1152]{1,0:T(4,128)} %mod.1) | copy-start | bytes 41476
  37.6 12.2 %all-to-all-start.1 = ((bf16[4,40,1152]{2,1,0:T(8,128)(2,1)}), bf16[4,40,1152]{2,1,0:T(8,128)(2,1)S(1)}, u32[]{:S(2)}, u32[]{:S(2)}) async-start(bf16[4,40,1152]{2,1,0:T(8,128)(2,1)} %pad_maximum_fusion.1), calls=%async_computation.1 | async-start | bytes 737280 | tf_op jit(solution)/shard_map/all_to_all | solution.py:237
  43.2 12.9 %collective-permute-start.2 = (bf16[4,36,432]{2,1,0:T(8,128)(2,1)S(1)}, bf16[4,36,432]{2,1,0:T(8,128)(2,1)S(1)}, u32[]{:S(2)}, u32[]{:S(2)}) collective-permute-start(bf16[4,36,432]{2,1,0:T(8,128)(2,1)S(1)} %all-to-all-done), channel_id=1, source_target_pairs={{0,1},{1,0},{2,3},{3,2},{4,5},{5,4},{6,7},{7,6},{8,9},{9,8},{10,11... | collective-permute-start | bytes 373256 | tf_op jit(solution)/shard_map/ppermute | solution.py:233
  56.2 24.1 %all-to-all-start.2 = ((bf16[4,160,1152]{2,1,0:T(8,128)(2,1)}), bf16[4,160,1152]{2,1,0:T(8,128)(2,1)S(1)}, u32[]{:S(2)}, u32[]{:S(2)}) async-start(bf16[4,160,1152]{2,1,0:T(8,128)(2,1)} %bitcast.8), calls=%async_computation.2 | async-start | bytes 2949120 | tf_op jit(solution)/shard_map/all_to_all | solution.py:250
  59.8 25.3 %copy-start.9 = (f32[4,72]{1,0:T(4,128)S(1)}, f32[4,72]{1,0:T(4,128)}, u32[]{:S(2)}) copy-start(f32[4,72]{1,0:T(4,128)} %param.11) | copy-start | bytes 3460
  60.0 9.4 %collective-permute-start.3 = (bf16[288,432]{1,0:T(8,128)(2,1)S(1)}, bf16[288,432]{1,0:T(8,128)(2,1)S(1)}, u32[]{:S(2)}, u32[]{:S(2)}) collective-permute-start(bf16[288,432]{1,0:T(8,128)(2,1)S(1)} %reshape.71.w0), channel_id=1, source_target_pairs={{8,0},{16,8},{24,16},{0,24},{9,1},{17,9},{25,17},{1,25},{10,2},{18... | collective-permute-start | bytes 746504 | tf_op jit(solution)/shard_map/ppermute | solution.py:247
  62.8 8.8 %collective-permute-start.4 = (bf16[288,432]{1,0:T(8,128)(2,1)S(1)}, bf16[288,432]{1,0:T(8,128)(2,1)S(1)}, u32[]{:S(2)}, u32[]{:S(2)}) collective-permute-start(bf16[288,432]{1,0:T(8,128)(2,1)S(1)} %reshape.71.w0), channel_id=1, source_target_pairs={{16,0},{24,8},{0,16},{8,24},{17,1},{25,9},{1,17},{9,25},{18,2},{26... | collective-permute-start | bytes 746504 | tf_op jit(solution)/shard_map/ppermute | solution.py:247
  63.4 16.2 %collective-permute-start.5 = (bf16[288,432]{1,0:T(8,128)(2,1)S(1)}, bf16[288,432]{1,0:T(8,128)(2,1)S(1)}, u32[]{:S(2)}, u32[]{:S(2)}) collective-permute-start(bf16[288,432]{1,0:T(8,128)(2,1)S(1)} %reshape.71.w0), channel_id=1, source_target_pairs={{24,0},{0,8},{8,16},{16,24},{25,1},{1,9},{9,17},{17,25},{26,2},{2,... | collective-permute-start | bytes 746504 | tf_op jit(solution)/shard_map/ppermute | solution.py:247
  69.4 0.7 copy-start.1
  71.7 0.7 copy-start.3
  79.6 0.7 copy-start.5
  80.3 5.0 %collective-permute-start.6 = (bf16[640,1152]{1,0:T(8,128)(2,1)S(1)}, bf16[640,1152]{1,0:T(8,128)(2,1)S(1)}, u32[]{:S(2)}, u32[]{:S(2)}) collective-permute-start(bf16[640,1152]{1,0:T(8,128)(2,1)S(1)} %bitcast.35), channel_id=1, source_target_pairs={{0,32},{32,0},{1,33},{33,1},{2,34},{34,2},{3,35},{35,3},{4,36},{36... | collective-permute-start | bytes 4423688 | tf_op jit(solution)/shard_map/ppermute | solution.py:252
  80.9 17.9 %all-to-all-start.4 = ((bf16[8,5,4,1152]{3,2,1,0:T(4,128)(2,1)}), bf16[8,5,4,1152]{3,2,1,0:T(4,128)(2,1)}, u32[]{:S(2)}, u32[]{:S(2)}) async-start(bf16[8,5,4,1152]{3,2,1,0:T(4,128)(2,1)} %bitcast.40), calls=%async_computation.4 | async-start | bytes 737280 | tf_op jit(solution)/shard_map/all_to_all | solution.py:254
  85.3 1.0 copy-start.2
  86.3 1.0 copy-start.4
  87.3 1.0 copy-start.6
  97.0 11.1 %copy-start.8 = (f32[3,1152]{1,0:T(4,128)S(1)}, f32[3,1152]{1,0:T(4,128)}, u32[]{:S(2)}) copy-start(f32[3,1152]{1,0:T(4,128)} %param.10) | copy-start | bytes 41476
  98.7 27.9 %all-to-all-start.3 = ((bf16[256,2,360]{2,1,0:T(2,128)(2,1)}), bf16[256,2,360]{2,1,0:T(2,128)(2,1)S(1)}, u32[]{:S(2)}, u32[]{:S(2)}) async-start(bf16[256,2,360]{2,1,0:T(2,128)(2,1)} %reshape.79), calls=%async_computation.3 | async-start | bytes 786432 | tf_op jit(solution)/shard_map/all_to_all | solution.py:262
Sparse Core Ops, SparseCore 0:
  36.8 79.1 all-gather.1

commit v6 on v5

--- a/solution.py
+++ b/solution.py
@@ -47,7 +47,6 @@
         out_shape=jax.ShapeDtypeStruct((4, 4, 40, D), BF16),
         in_specs=[VMEM] * 2,
         out_specs=VMEM,
-        compiler_params=pltpu.CompilerParams(vmem_limit_bytes=12 * 2**20),
         cost_estimate=pl.CostEstimate(flops=4_000_000, bytes_accessed=2_000_000, transcendentals=0),
     )(mod, rows)
 

time: 160 us -> 158 us (0.988)
    ppermute x1, waiting for transfers between devices: 4.97 us -> 3.2 us  [per_device(): w_far = lax.ppermute(w_x, 'zh', other)]
    unnamed x23 -> x21, local copies, waits for them, and re-layouts: 8.63 us -> 7.66 us
  transfers between devices with their start and end apart: 13 -> 13, of which waited for: 8 -> 8; matrix products, arithmetic and copies ran while one was open for 8% -> 8% of each run, Pallas kernels for 6% -> 7%
where the time goes in v6:
time: 158 us
  waiting for transfers between devices  48.5 us (31%)
  starting transfers between devices  42.9 us (27%)
  Pallas kernels  19 us (12%)
  local copies, waits for them, and re-layouts  16.2 us (10%)
  blocking collectives  14 us (9%)
  between operations  13.7 us (9%)
  other arithmetic  3.22 us (2%)
    all_to_all x1, waiting for transfers between devices, per_device(): lax.all_to_all(att, everyone, split_axis=0, concat_axis=0, tiled=True)  17.1 us
    ppermute x3, waiting for transfers between devices, per_device(): lax.ppermute(w_z, 'y', [((i + k) % 4, i) for i in range(4)])  14.9 us
    all_to_all x1, blocking collectives, per_device(): lax.all_to_all(mixed, ('zl', 'core'), split_axis=0, concat_axis=0, tiled=...  14 us
    all_to_all x1, starting transfers between devices, per_device(): lax.all_to_all(att, everyone, split_axis=0, concat_axis=0, tiled=True)  9.24 us
    pallas_call x1, Pallas kernels, temporal(): pl.pallas_call(temporal_kernel, out_shape=jax.ShapeDtypeStruct((8, 5, 4,...  8.68 us
    ppermute x1, starting transfers between devices, per_device(): moved = lax.ppermute(leave, ('core', 'zh'), [(i, 3 - i) for i in range(4)])  8.39 us
    pallas_call x1, Pallas kernels, spatial(): pl.pallas_call(spatial_kernel, out_shape=jax.ShapeDtypeStruct((32, 40, PA...  7.9 us
    unnamed x21, local copies, waits for them, and re-layouts  7.66 us
  transfers between devices with their start and end apart: 13, of which 8 were waited for; matrix products, arithmetic and copies ran while one was open for 8% of the time, Pallas kernels for 7%

profile of v6, /device:TPU:1, one launch (start us, length us, event | category | flops | bytes accessed | tf_op | source)
XLA Modules:
  0.0 157.6 jit_solution(11483802182584806516)
XLA Ops:
  7.5 8.4 %collective-permute-start = (bf16[2,40,1152]{2,1,0:T(8,128)(2,1)S(1)}, bf16[2,40,1152]{2,1,0:T(8,128)(2,1)S(1)}, u32[]{:S(2)}, u32[]{:S(2)}) collective-permute-start(bf16[2,40,1152]{2,1,0:T(8,128)(2,1)S(1)} %dynamic-slice_bitcast_fusion), channel_id=1, source_target_pairs={{0,33},{1,32},{32,1},{33,0},{2,35},{3,34},{34,3},{35,2},{4,37},{5,... | collective-permute-start | bytes 552968 | tf_op jit(solution)/shard_map/ppermute | solution.py:220
  16.7 1.1 maximum_select_fusion
  18.1 1.6 reshape.67
  21.1 3.8 %all-to-all-start = ((bf16[4,36,432]{2,1,0:T(8,128)(2,1)}), bf16[4,36,432]{2,1,0:T(8,128)(2,1)S(1)}, u32[]{:S(2)}, u32[]{:S(2)}) async-start(bf16[4,36,432]{2,1,0:T(8,128)(2,1)} %reshape.78), calls=%async_computation | async-start | bytes 327680 | tf_op jit(solution)/shard_map/all_to_all | solution.py:230
  25.0 5.3 %all-to-all-done = bf16[4,36,432]{2,1,0:T(8,128)(2,1)S(1)} async-done(((bf16[4,36,432]{2,1,0:T(8,128)(2,1)}), bf16[4,36,432]{2,1,0:T(8,128)(2,1)S(1)}, u32[]{:S(2)}, u32[]{:S(2)}) %all-to-all-start) | async-done | bytes 124448 | tf_op jit(solution)/shard_map/all_to_all | solution.py:230
  30.3 5.5 %collective-permute-done.1 = bf16[36,2944]{1,0:T(8,128)(2,1)S(1)} collective-permute-done((bf16[36,2944]{1,0:T(8,128)(2,1)S(1)}, bf16[36,2944]{1,0:T(8,128)(2,1)S(1)}, u32[]{:S(2)}, u32[]{:S(2)}) %collective-permute-start.1) | collective-permute-done | bytes 212000 | tf_op jit(solution)/shard_map/ppermute | solution.py:225
  37.6 5.7 %all-to-all-start.1 = ((bf16[4,40,1152]{2,1,0:T(8,128)(2,1)}), bf16[4,40,1152]{2,1,0:T(8,128)(2,1)S(1)}, u32[]{:S(2)}, u32[]{:S(2)}) async-start(bf16[4,40,1152]{2,1,0:T(8,128)(2,1)} %pad_maximum_fusion.1), calls=%async_computation.1 | async-start | bytes 737280 | tf_op jit(solution)/shard_map/all_to_all | solution.py:236
  43.2 3.1 %collective-permute-start.2 = (bf16[4,36,432]{2,1,0:T(8,128)(2,1)S(1)}, bf16[4,36,432]{2,1,0:T(8,128)(2,1)S(1)}, u32[]{:S(2)}, u32[]{:S(2)}) collective-permute-start(bf16[4,36,432]{2,1,0:T(8,128)(2,1)S(1)} %all-to-all-done), channel_id=1, source_target_pairs={{0,1},{1,0},{2,3},{3,2},{4,5},{5,4},{6,7},{7,6},{8,9},{9,8},{10,11... | collective-permute-start | bytes 373256 | tf_op jit(solution)/shard_map/ppermute | solution.py:232
  47.2 2.5 %all-to-all-done.1.rows = bf16[4,40,1152]{2,1,0:T(8,128)(2,1)S(1)} async-done(((bf16[4,40,1152]{2,1,0:T(8,128)(2,1)}), bf16[4,40,1152]{2,1,0:T(8,128)(2,1)S(1)}, u32[]{:S(2)}, u32[]{:S(2)}) %all-to-all-start.1) | async-done | bytes 368672 | tf_op jit(solution)/shard_map/all_to_all | solution.py:236
  50.5 2.5 %shard_map.82 = bf16[4,4,40,1152]{3,2,1,0:T(8,128)(2,1)} custom-call(f32[3,1152]{1,0:T(4,128)} %mod.1, bf16[4,40,1152]{2,1,0:T(8,128)(2,1)} %copy-done.5), custom_call_target="tpu_custom_call" | custom-call | flops 4000000 | bytes 2000000 | tf_op jit(solution)/shard_map/pallas_call | solution.py:45
  52.9 3.2 %collective-permute-done.2 = bf16[4,36,432]{2,1,0:T(8,128)(2,1)S(1)} collective-permute-done((bf16[4,36,432]{2,1,0:T(8,128)(2,1)S(1)}, bf16[4,36,432]{2,1,0:T(8,128)(2,1)S(1)}, u32[]{:S(2)}, u32[]{:S(2)}) %collective-permute-start.2) | collective-permute-done | bytes 124448 | tf_op jit(solution)/shard_map/ppermute | solution.py:232
  56.1 3.6 %all-to-all-start.2 = ((bf16[4,160,1152]{2,1,0:T(8,128)(2,1)}), bf16[4,160,1152]{2,1,0:T(8,128)(2,1)S(1)}, u32[]{:S(2)}, u32[]{:S(2)}) async-start(bf16[4,160,1152]{2,1,0:T(8,128)(2,1)} %bitcast.37), calls=%async_computation.2 | async-start | bytes 2949120 | tf_op jit(solution)/shard_map/all_to_all | solution.py:249
  59.9 2.9 %collective-permute-start.3 = (bf16[288,432]{1,0:T(8,128)(2,1)S(1)}, bf16[288,432]{1,0:T(8,128)(2,1)S(1)}, u32[]{:S(2)}, u32[]{:S(2)}) collective-permute-start(bf16[288,432]{1,0:T(8,128)(2,1)S(1)} %reshape.71.w0), channel_id=1, source_target_pairs={{8,0},{16,8},{24,16},{0,24},{9,1},{17,9},{25,17},{1,25},{10,2},{18... | collective-permute-start | bytes 746504 | tf_op jit(solution)/shard_map/ppermute | solution.py:246
  64.0 5.4 %collective-permute-done.3.w1 = bf16[288,432]{1,0:T(8,128)(2,1)S(1)} collective-permute-done((bf16[288,432]{1,0:T(8,128)(2,1)S(1)}, bf16[288,432]{1,0:T(8,128)(2,1)S(1)}, u32[]{:S(2)}, u32[]{:S(2)}) %collective-permute-start.3) | collective-permute-done | bytes 248864 | tf_op jit(solution)/shard_map/ppermute | solution.py:246
  69.4 2.3 %collective-permute-done.4.w2 = bf16[288,432]{1,0:T(8,128)(2,1)S(1)} collective-permute-done((bf16[288,432]{1,0:T(8,128)(2,1)S(1)}, bf16[288,432]{1,0:T(8,128)(2,1)S(1)}, u32[]{:S(2)}, u32[]{:S(2)}) %collective-permute-start.4) | collective-permute-done | bytes 248864 | tf_op jit(solution)/shard_map/ppermute | solution.py:246
  72.3 7.2 %collective-permute-done.5.w3 = bf16[288,432]{1,0:T(8,128)(2,1)S(1)} collective-permute-done((bf16[288,432]{1,0:T(8,128)(2,1)S(1)}, bf16[288,432]{1,0:T(8,128)(2,1)S(1)}, u32[]{:S(2)}, u32[]{:S(2)}) %collective-permute-start.5) | collective-permute-done | bytes 248864 | tf_op jit(solution)/shard_map/ppermute | solution.py:246
  80.8 4.2 %all-to-all-start.4 = ((bf16[8,5,4,1152]{3,2,1,0:T(4,128)(2,1)}), bf16[8,5,4,1152]{3,2,1,0:T(4,128)(2,1)}, u32[]{:S(2)}, u32[]{:S(2)}) async-start(bf16[8,5,4,1152]{3,2,1,0:T(4,128)(2,1)} %bitcast.41), calls=%async_computation.4 | async-start | bytes 737280 | tf_op jit(solution)/shard_map/all_to_all | solution.py:253
  87.2 7.9 %shard_map.83 = bf16[32,40,144]{2,1,0:T(8,128)(2,1)S(1)} custom-call(s32[2]{0:T(128)S(1)} %pad_add_fusion.place, f32[2,256]{1,0:T(2,128)S(1)} %pad.4.gain, bf16[640,1152]{1,0:T(8,128)(2,1)S(1)} %bitcast.36, bf16[640,1152]{1,0:T(8,128)(2,1)S(1)} %collective-permute-done.6.tok_theirs, bf16[288,432]{1,0:T(8,128)(2,1)S(1)} %reshape.71.w0, ...), custom_call_target="tpu_custom_call" | custom-call | flops 5000000000 | bytes 5000000 | tf_op jit(solution)/shard_map/pallas_call | solution.py:106
  95.9 1.7 %reshape.79 = bf16[256,2,360]{2,1,0:T(2,128)(2,1)} reshape(bf16[256,5,144]{2,1,0:T(8,128)(2,1)S(1)} %bitcast.38) | data formatting | bytes 737280
  97.7 9.2 %all-to-all-start.3 = ((bf16[256,2,360]{2,1,0:T(2,128)(2,1)}), bf16[256,2,360]{2,1,0:T(2,128)(2,1)S(1)}, u32[]{:S(2)}, u32[]{:S(2)}) async-start(bf16[256,2,360]{2,1,0:T(2,128)(2,1)} %reshape.79), calls=%async_computation.3 | async-start | bytes 786432 | tf_op jit(solution)/shard_map/all_to_all | solution.py:261
  107.3 1.1 copy.31
  108.5 17.1 %all-to-all-done.3 = bf16[256,2,360]{2,1,0:T(2,128)(2,1)S(1)} async-done(((bf16[256,2,360]{2,1,0:T(2,128)(2,1)}), bf16[256,2,360]{2,1,0:T(2,128)(2,1)S(1)}, u32[]{:S(2)}, u32[]{:S(2)}) %all-to-all-start.3) | async-done | bytes 368672 | tf_op jit(solution)/shard_map/all_to_all | solution.py:261
  127.3 8.7 %shard_map.84 = bf16[8,5,4,1152]{3,2,1,0:T(4,128)(2,1)S(1)} custom-call(f32[6,1152]{1,0:T(8,128)S(1)} %pad_maximum_fusion.3.mods, f32[2,1152]{1,0:T(2,128)S(1)} %tile.9.gain, bf16[1152,128]{1,0:T(8,128)(2,1)S(1)} %fusion.seg, bf16[160,1152]{1,0:T(8,128)(2,1)S(1)} %reshape.75.back, bf16[160,1152]{1,0:T(8,128)(2,1)S(1)} %reshape.76.res, ...), custom_call_target="tpu_custom_call" | custom-call | flops 1800000000 | bytes 15000000 | tf_op jit(solution)/shard_map/pallas_call | solution.py:185
  136.0 14.0 %all_to_all.30 = bf16[8,5,4,1152]{3,2,1,0:T(4,128)(2,1)S(1)} all-to-all(bf16[8,5,4,1152]{3,2,1,0:T(4,128)(2,1)S(1)} %shard_map.84), channel_id=1, replica_groups=mesh['zl'=4,'core'=2,'y'=4,'x'=4,'zh'=2] {'zl','core'}, dimensions={0} | all-to-all | bytes 737280 | tf_op jit(solution)/shard_map/all_to_all | solution.py:267
  (63 shorter events, 15.9 us)
Async XLA Ops:
  7.5 22.8 %collective-permute-start = (bf16[2,40,1152]{2,1,0:T(8,128)(2,1)S(1)}, bf16[2,40,1152]{2,1,0:T(8,128)(2,1)S(1)}, u32[]{:S(2)}, u32[]{:S(2)}) collective-permute-start(bf16[2,40,1152]{2,1,0:T(8,128)(2,1)S(1)} %dynamic-slice_bitcast_fusion), channel_id=1, source_target_pairs={{0,33},{1,32},{32,1},{33,0},{2,35},{3,34},{34,3},{35,2},{4,37},{5,... | collective-permute-start | bytes 552968 | tf_op jit(solution)/shard_map/ppermute | solution.py:220
  17.8 18.0 %collective-permute-start.1 = (bf16[36,2944]{1,0:T(8,128)(2,1)S(1)}, bf16[36,2944]{1,0:T(8,128)(2,1)S(1)}, u32[]{:S(2)}, u32[]{:S(2)}) collective-permute-start(bf16[36,2944]{1,0:T(8,128)(2,1)S(1)} %maximum_select_fusion), channel_id=1, source_target_pairs={{0,1},{1,0},{2,3},{3,2},{4,5},{5,4},{6,7},{7,6},{8,9},{9,8},{10,11... | collective-permute-start | bytes 635912 | tf_op jit(solution)/shard_map/ppermute | solution.py:225
  20.3 16.5 %copy-start.4 = (bf16[4,1,40,1152]{3,2,1,0:T(8,128)(2,1)S(1)}, bf16[4,1,40,1152]{3,2,1,0:T(8,128)(2,1)}, u32[]{:S(2)}) copy-start(bf16[4,1,40,1152]{3,2,1,0:T(8,128)(2,1)} %param.8) | copy-start | bytes 1105924
  21.1 9.1 %all-to-all-start = ((bf16[4,36,432]{2,1,0:T(8,128)(2,1)}), bf16[4,36,432]{2,1,0:T(8,128)(2,1)S(1)}, u32[]{:S(2)}, u32[]{:S(2)}) async-start(bf16[4,36,432]{2,1,0:T(8,128)(2,1)} %reshape.78), calls=%async_computation | async-start | bytes 327680 | tf_op jit(solution)/shard_map/all_to_all | solution.py:230
  25.0 102.3 %all-gather.2.cloned.1.call-start = ((), (), s32[]{:S(2)}) async-start(), calls=%async_computation.6 | async-start | bytes 13989888 | tf_op jit(solution)/shard_map/all_gather | solution.py:241
  37.6 12.2 %all-to-all-start.1 = ((bf16[4,40,1152]{2,1,0:T(8,128)(2,1)}), bf16[4,40,1152]{2,1,0:T(8,128)(2,1)S(1)}, u32[]{:S(2)}, u32[]{:S(2)}) async-start(bf16[4,40,1152]{2,1,0:T(8,128)(2,1)} %pad_maximum_fusion.1), calls=%async_computation.1 | async-start | bytes 737280 | tf_op jit(solution)/shard_map/all_to_all | solution.py:236
  43.2 12.9 %collective-permute-start.2 = (bf16[4,36,432]{2,1,0:T(8,128)(2,1)S(1)}, bf16[4,36,432]{2,1,0:T(8,128)(2,1)S(1)}, u32[]{:S(2)}, u32[]{:S(2)}) collective-permute-start(bf16[4,36,432]{2,1,0:T(8,128)(2,1)S(1)} %all-to-all-done), channel_id=1, source_target_pairs={{0,1},{1,0},{2,3},{3,2},{4,5},{5,4},{6,7},{7,6},{8,9},{9,8},{10,11... | collective-permute-start | bytes 373256 | tf_op jit(solution)/shard_map/ppermute | solution.py:232
  49.7 0.7 copy-start.5
  56.1 24.1 %all-to-all-start.2 = ((bf16[4,160,1152]{2,1,0:T(8,128)(2,1)}), bf16[4,160,1152]{2,1,0:T(8,128)(2,1)S(1)}, u32[]{:S(2)}, u32[]{:S(2)}) async-start(bf16[4,160,1152]{2,1,0:T(8,128)(2,1)} %bitcast.37), calls=%async_computation.2 | async-start | bytes 2949120 | tf_op jit(solution)/shard_map/all_to_all | solution.py:249
  59.7 25.3 %copy-start.8 = (f32[4,72]{1,0:T(4,128)S(1)}, f32[4,72]{1,0:T(4,128)}, u32[]{:S(2)}) copy-start(f32[4,72]{1,0:T(4,128)} %param.11) | copy-start | bytes 3460
  59.9 9.4 %collective-permute-start.3 = (bf16[288,432]{1,0:T(8,128)(2,1)S(1)}, bf16[288,432]{1,0:T(8,128)(2,1)S(1)}, u32[]{:S(2)}, u32[]{:S(2)}) collective-permute-start(bf16[288,432]{1,0:T(8,128)(2,1)S(1)} %reshape.71.w0), channel_id=1, source_target_pairs={{8,0},{16,8},{24,16},{0,24},{9,1},{17,9},{25,17},{1,25},{10,2},{18... | collective-permute-start | bytes 746504 | tf_op jit(solution)/shard_map/ppermute | solution.py:246
  62.8 8.8 %collective-permute-start.4 = (bf16[288,432]{1,0:T(8,128)(2,1)S(1)}, bf16[288,432]{1,0:T(8,128)(2,1)S(1)}, u32[]{:S(2)}, u32[]{:S(2)}) collective-permute-start(bf16[288,432]{1,0:T(8,128)(2,1)S(1)} %reshape.71.w0), channel_id=1, source_target_pairs={{16,0},{24,8},{0,16},{8,24},{17,1},{25,9},{1,17},{9,25},{18,2},{26... | collective-permute-start | bytes 746504 | tf_op jit(solution)/shard_map/ppermute | solution.py:246
  63.4 16.2 %collective-permute-start.5 = (bf16[288,432]{1,0:T(8,128)(2,1)S(1)}, bf16[288,432]{1,0:T(8,128)(2,1)S(1)}, u32[]{:S(2)}, u32[]{:S(2)}) collective-permute-start(bf16[288,432]{1,0:T(8,128)(2,1)S(1)} %reshape.71.w0), channel_id=1, source_target_pairs={{24,0},{0,8},{8,16},{16,24},{25,1},{1,9},{9,17},{17,25},{26,2},{2,... | collective-permute-start | bytes 746504 | tf_op jit(solution)/shard_map/ppermute | solution.py:246
  71.6 0.7 copy-start
  79.6 0.7 copy-start.2
  80.3 5.0 %collective-permute-start.6 = (bf16[640,1152]{1,0:T(8,128)(2,1)S(1)}, bf16[640,1152]{1,0:T(8,128)(2,1)S(1)}, u32[]{:S(2)}, u32[]{:S(2)}) collective-permute-start(bf16[640,1152]{1,0:T(8,128)(2,1)S(1)} %bitcast.35), channel_id=1, source_target_pairs={{0,32},{32,0},{1,33},{33,1},{2,34},{34,2},{3,35},{35,3},{4,36},{36... | collective-permute-start | bytes 4423688 | tf_op jit(solution)/shard_map/ppermute | solution.py:251
  80.8 16.8 %all-to-all-start.4 = ((bf16[8,5,4,1152]{3,2,1,0:T(4,128)(2,1)}), bf16[8,5,4,1152]{3,2,1,0:T(4,128)(2,1)}, u32[]{:S(2)}, u32[]{:S(2)}) async-start(bf16[8,5,4,1152]{3,2,1,0:T(4,128)(2,1)} %bitcast.41), calls=%async_computation.4 | async-start | bytes 737280 | tf_op jit(solution)/shard_map/all_to_all | solution.py:253
  85.3 1.0 copy-start.1
  86.3 1.0 copy-start.3
  95.9 11.1 %copy-start.6 = (f32[3,1152]{1,0:T(4,128)S(1)}, f32[3,1152]{1,0:T(4,128)}, u32[]{:S(2)}) copy-start(f32[3,1152]{1,0:T(4,128)} %mod.1) | copy-start | bytes 41476
  95.9 11.1 %copy-start.7 = (f32[3,1152]{1,0:T(4,128)S(1)}, f32[3,1152]{1,0:T(4,128)}, u32[]{:S(2)}) copy-start(f32[3,1152]{1,0:T(4,128)} %param.10) | copy-start | bytes 41476
  97.7 27.9 %all-to-all-start.3 = ((bf16[256,2,360]{2,1,0:T(2,128)(2,1)}), bf16[256,2,360]{2,1,0:T(2,128)(2,1)S(1)}, u32[]{:S(2)}, u32[]{:S(2)}) async-start(bf16[256,2,360]{2,1,0:T(2,128)(2,1)} %reshape.79), calls=%async_computation.3 | async-start | bytes 786432 | tf_op jit(solution)/shard_map/all_to_all | solution.py:261
Sparse Core Ops, SparseCore 0:
  36.8 79.7 all-gather.1

commit v7 on v6

--- a/solution.py
+++ b/solution.py
@@ -63,8 +63,11 @@
     wall[...] = jnp.zeros_like(wall)
     for k, w in enumerate((w0, w1, w2, w3)):
         rows = pl.ds(pl.multiple_of(lax.rem(y + k, 4) * quarter, quarter), quarter)
-        for part in range(3):
-            wall[rows, 256 * part : 256 * part + PAIR] = w[:, PAIR * part : PAIR * (part + 1)]
+        for part in range(2):
+            lo = 256 * part
+            wall[rows, lo : lo + PAIR] = w[:, PAIR * part : PAIR * (part + 1)]
+            head = 2 * PAIR + HDIM * part
+            wall[rows, lo + PAIR : lo + PAIR + HDIM] = w[:, head : head + HDIM]
     lane = lax.broadcasted_iota(jnp.int32, (1, 256), 1)
     first = lane < HDIM
     second = (lane >= HDIM) & (lane < PAIR)
@@ -72,7 +75,7 @@
     def head_norm(heads, g):
         square = heads * heads
         s0 = jnp.sum(jnp.where(first, square, 0.0), -1, keepdims=True)
-        s1 = jnp.sum(jnp.where(first, 0.0, square), -1, keepdims=True)
+        s1 = jnp.sum(jnp.where(second, square, 0.0), -1, keepdims=True)
         r0 = lax.rsqrt(s0 * (1.0 / HDIM) + 1e-06)
         r1 = lax.rsqrt(s1 * (1.0 / HDIM) + 1e-06)
         return heads * jnp.where(first, r0, r1) * g
@@ -85,7 +88,9 @@
         q0[at] = jnp.where(first, q, 0.0).astype(BF16)
         q1[at] = jnp.where(second, q, 0.0).astype(BF16)
         k0[at] = head_norm(qkv[:, 256:512], gain[1:2]).astype(BF16)
-        v0[at] = jnp.where(lane == PAIR, 1.0, qkv[:, 512:]).astype(BF16)
+        v = jnp.where(first, pltpu.roll(qkv[:, :256], 112, 1), pltpu.roll(qkv[:, 256:], 184, 1))
+        v = jnp.where(lane < PAIR, v, jnp.where(lane == PAIR, 1.0, 0.0))
+        v0[at] = v.astype(BF16)
 
     def attend(queries):
         scores = dot_t(queries, k0[...])
@@ -108,7 +113,7 @@
         out_shape=jax.ShapeDtypeStruct((32, 40, PAIR), BF16),
         in_specs=[SMEM] + [VMEM] * 7,
         out_specs=VMEM,
-        scratch_shapes=[pltpu.VMEM((D, 768), BF16)] + [pltpu.VMEM((1280, 256), BF16)] * 4,
+        scratch_shapes=[pltpu.VMEM((D, 512), BF16)] + [pltpu.VMEM((1280, 256), BF16)] * 4,
         compiler_params=pltpu.CompilerParams(vmem_limit_bytes=48 * 2**20),
         cost_estimate=pl.CostEstimate(
             flops=5_000_000_000, bytes_accessed=5_000_000, transcendentals=3_300_000

time: 158 us -> 158 us (level)
  transfers between devices with their start and end apart: 13 -> 13, of which waited for: 8 -> 8; matrix products, arithmetic and copies ran while one was open for 8% -> 8% of each run, Pallas kernels for 7% -> 6%
where the time goes in v7:
time: 158 us; the launch traced here: 157 us
  waiting for transfers between devices  48.4 us (31%)
  starting transfers between devices  42.9 us (27%)
  Pallas kernels  18.3 us (12%)
  local copies, waits for them, and re-layouts  16.3 us (10%)
  blocking collectives  14.1 us (9%)
  between operations  13.7 us (9%)
  other arithmetic  3.22 us (2%)
    all_to_all x1, waiting for transfers between devices, per_device(): lax.all_to_all(att, everyone, split_axis=0, concat_axis=0, tiled=True)  17 us
    ppermute x3, waiting for transfers between devices, per_device(): lax.ppermute(w_z, 'y', [((i + k) % 4, i) for i in range(4)])  14.9 us
    all_to_all x1, blocking collectives, per_device(): lax.all_to_all(mixed, ('zl', 'core'), split_axis=0, concat_axis=0, tiled=...  14.1 us
    all_to_all x1, starting transfers between devices, per_device(): lax.all_to_all(att, everyone, split_axis=0, concat_axis=0, tiled=True)  9.24 us
    pallas_call x1, Pallas kernels, temporal(): pl.pallas_call(temporal_kernel, out_shape=jax.ShapeDtypeStruct((8, 5, 4,...  8.67 us
    ppermute x1, starting transfers between devices, per_device(): moved = lax.ppermute(leave, ('core', 'zh'), [(i, 3 - i) for i in range(4)])  8.39 us
    unnamed x21, local copies, waits for them, and re-layouts  7.66 us
    pallas_call x1, Pallas kernels, spatial(): pl.pallas_call(spatial_kernel, out_shape=jax.ShapeDtypeStruct((32, 40, PA...  7.17 us
  transfers between devices with their start and end apart: 13, of which 8 were waited for; matrix products, arithmetic and copies ran while one was open for 8% of the time, Pallas kernels for 6%

profile of v7, /device:TPU:1, one launch (start us, length us, event | category | flops | bytes accessed | tf_op | source)
XLA Modules:
  0.0 156.9 jit_solution(8236316667427846392)
XLA Ops:
  7.5 8.4 %collective-permute-start = (bf16[2,40,1152]{2,1,0:T(8,128)(2,1)S(1)}, bf16[2,40,1152]{2,1,0:T(8,128)(2,1)S(1)}, u32[]{:S(2)}, u32[]{:S(2)}) collective-permute-start(bf16[2,40,1152]{2,1,0:T(8,128)(2,1)S(1)} %dynamic-slice_bitcast_fusion), channel_id=1, source_target_pairs={{0,33},{1,32},{32,1},{33,0},{2,35},{3,34},{34,3},{35,2},{4,37},{5,... | collective-permute-start | bytes 552968 | tf_op jit(solution)/shard_map/ppermute | solution.py:225
  16.7 1.1 maximum_select_fusion
  18.1 1.6 reshape.67
  21.1 3.8 %all-to-all-start = ((bf16[4,36,432]{2,1,0:T(8,128)(2,1)}), bf16[4,36,432]{2,1,0:T(8,128)(2,1)S(1)}, u32[]{:S(2)}, u32[]{:S(2)}) async-start(bf16[4,36,432]{2,1,0:T(8,128)(2,1)} %reshape.78), calls=%async_computation | async-start | bytes 327680 | tf_op jit(solution)/shard_map/all_to_all | solution.py:235
  25.0 5.3 %all-to-all-done = bf16[4,36,432]{2,1,0:T(8,128)(2,1)S(1)} async-done(((bf16[4,36,432]{2,1,0:T(8,128)(2,1)}), bf16[4,36,432]{2,1,0:T(8,128)(2,1)S(1)}, u32[]{:S(2)}, u32[]{:S(2)}) %all-to-all-start) | async-done | bytes 124448 | tf_op jit(solution)/shard_map/all_to_all | solution.py:235
  30.3 5.5 %collective-permute-done.1 = bf16[36,2944]{1,0:T(8,128)(2,1)S(1)} collective-permute-done((bf16[36,2944]{1,0:T(8,128)(2,1)S(1)}, bf16[36,2944]{1,0:T(8,128)(2,1)S(1)}, u32[]{:S(2)}, u32[]{:S(2)}) %collective-permute-start.1) | collective-permute-done | bytes 212000 | tf_op jit(solution)/shard_map/ppermute | solution.py:230
  37.6 5.7 %all-to-all-start.1 = ((bf16[4,40,1152]{2,1,0:T(8,128)(2,1)}), bf16[4,40,1152]{2,1,0:T(8,128)(2,1)S(1)}, u32[]{:S(2)}, u32[]{:S(2)}) async-start(bf16[4,40,1152]{2,1,0:T(8,128)(2,1)} %pad_maximum_fusion.1), calls=%async_computation.1 | async-start | bytes 737280 | tf_op jit(solution)/shard_map/all_to_all | solution.py:241
  43.2 3.1 %collective-permute-start.2 = (bf16[4,36,432]{2,1,0:T(8,128)(2,1)S(1)}, bf16[4,36,432]{2,1,0:T(8,128)(2,1)S(1)}, u32[]{:S(2)}, u32[]{:S(2)}) collective-permute-start(bf16[4,36,432]{2,1,0:T(8,128)(2,1)S(1)} %all-to-all-done), channel_id=1, source_target_pairs={{0,1},{1,0},{2,3},{3,2},{4,5},{5,4},{6,7},{7,6},{8,9},{9,8},{10,11... | collective-permute-start | bytes 373256 | tf_op jit(solution)/shard_map/ppermute | solution.py:237
  47.2 2.5 %all-to-all-done.1.rows = bf16[4,40,1152]{2,1,0:T(8,128)(2,1)S(1)} async-done(((bf16[4,40,1152]{2,1,0:T(8,128)(2,1)}), bf16[4,40,1152]{2,1,0:T(8,128)(2,1)S(1)}, u32[]{:S(2)}, u32[]{:S(2)}) %all-to-all-start.1) | async-done | bytes 368672 | tf_op jit(solution)/shard_map/all_to_all | solution.py:241
  50.5 2.5 %shard_map.82 = bf16[4,4,40,1152]{3,2,1,0:T(8,128)(2,1)} custom-call(f32[3,1152]{1,0:T(4,128)} %mod.1, bf16[4,40,1152]{2,1,0:T(8,128)(2,1)} %copy-done.5), custom_call_target="tpu_custom_call" | custom-call | flops 4000000 | bytes 2000000 | tf_op jit(solution)/shard_map/pallas_call | solution.py:45
  52.9 3.2 %collective-permute-done.2 = bf16[4,36,432]{2,1,0:T(8,128)(2,1)S(1)} collective-permute-done((bf16[4,36,432]{2,1,0:T(8,128)(2,1)S(1)}, bf16[4,36,432]{2,1,0:T(8,128)(2,1)S(1)}, u32[]{:S(2)}, u32[]{:S(2)}) %collective-permute-start.2) | collective-permute-done | bytes 124448 | tf_op jit(solution)/shard_map/ppermute | solution.py:237
  56.1 3.6 %all-to-all-start.2 = ((bf16[4,160,1152]{2,1,0:T(8,128)(2,1)}), bf16[4,160,1152]{2,1,0:T(8,128)(2,1)S(1)}, u32[]{:S(2)}, u32[]{:S(2)}) async-start(bf16[4,160,1152]{2,1,0:T(8,128)(2,1)} %bitcast.37), calls=%async_computation.2 | async-start | bytes 2949120 | tf_op jit(solution)/shard_map/all_to_all | solution.py:254
  59.9 2.9 %collective-permute-start.3 = (bf16[288,432]{1,0:T(8,128)(2,1)S(1)}, bf16[288,432]{1,0:T(8,128)(2,1)S(1)}, u32[]{:S(2)}, u32[]{:S(2)}) collective-permute-start(bf16[288,432]{1,0:T(8,128)(2,1)S(1)} %reshape.71.w0), channel_id=1, source_target_pairs={{8,0},{16,8},{24,16},{0,24},{9,1},{17,9},{25,17},{1,25},{10,2},{18... | collective-permute-start | bytes 746504 | tf_op jit(solution)/shard_map/ppermute | solution.py:251
  64.0 5.4 %collective-permute-done.3.w1 = bf16[288,432]{1,0:T(8,128)(2,1)S(1)} collective-permute-done((bf16[288,432]{1,0:T(8,128)(2,1)S(1)}, bf16[288,432]{1,0:T(8,128)(2,1)S(1)}, u32[]{:S(2)}, u32[]{:S(2)}) %collective-permute-start.3) | collective-permute-done | bytes 248864 | tf_op jit(solution)/shard_map/ppermute | solution.py:251
  69.4 2.3 %collective-permute-done.4.w2 = bf16[288,432]{1,0:T(8,128)(2,1)S(1)} collective-permute-done((bf16[288,432]{1,0:T(8,128)(2,1)S(1)}, bf16[288,432]{1,0:T(8,128)(2,1)S(1)}, u32[]{:S(2)}, u32[]{:S(2)}) %collective-permute-start.4) | collective-permute-done | bytes 248864 | tf_op jit(solution)/shard_map/ppermute | solution.py:251
  72.3 7.2 %collective-permute-done.5.w3 = bf16[288,432]{1,0:T(8,128)(2,1)S(1)} collective-permute-done((bf16[288,432]{1,0:T(8,128)(2,1)S(1)}, bf16[288,432]{1,0:T(8,128)(2,1)S(1)}, u32[]{:S(2)}, u32[]{:S(2)}) %collective-permute-start.5) | collective-permute-done | bytes 248864 | tf_op jit(solution)/shard_map/ppermute | solution.py:251
  80.8 4.2 %all-to-all-start.4 = ((bf16[8,5,4,1152]{3,2,1,0:T(4,128)(2,1)}), bf16[8,5,4,1152]{3,2,1,0:T(4,128)(2,1)}, u32[]{:S(2)}, u32[]{:S(2)}) async-start(bf16[8,5,4,1152]{3,2,1,0:T(4,128)(2,1)} %bitcast.41), calls=%async_computation.4 | async-start | bytes 737280 | tf_op jit(solution)/shard_map/all_to_all | solution.py:258
  87.2 7.2 %shard_map.83 = bf16[32,40,144]{2,1,0:T(8,128)(2,1)S(1)} custom-call(s32[2]{0:T(128)S(1)} %pad_add_fusion.place, f32[2,256]{1,0:T(2,128)S(1)} %pad.4.gain, bf16[640,1152]{1,0:T(8,128)(2,1)S(1)} %bitcast.36, bf16[640,1152]{1,0:T(8,128)(2,1)S(1)} %collective-permute-done.6.tok_theirs, bf16[288,432]{1,0:T(8,128)(2,1)S(1)} %reshape.71.w0, ...), custom_call_target="tpu_custom_call" | custom-call | flops 5000000000 | bytes 5000000 | tf_op jit(solution)/shard_map/pallas_call | solution.py:111
  95.2 1.7 %reshape.79 = bf16[256,2,360]{2,1,0:T(2,128)(2,1)} reshape(bf16[256,5,144]{2,1,0:T(8,128)(2,1)S(1)} %bitcast.38) | data formatting | bytes 737280
  96.9 9.2 %all-to-all-start.3 = ((bf16[256,2,360]{2,1,0:T(2,128)(2,1)}), bf16[256,2,360]{2,1,0:T(2,128)(2,1)S(1)}, u32[]{:S(2)}, u32[]{:S(2)}) async-start(bf16[256,2,360]{2,1,0:T(2,128)(2,1)} %reshape.79), calls=%async_computation.3 | async-start | bytes 786432 | tf_op jit(solution)/shard_map/all_to_all | solution.py:266
  106.6 1.2 copy.31
  107.9 17.0 %all-to-all-done.3 = bf16[256,2,360]{2,1,0:T(2,128)(2,1)S(1)} async-done(((bf16[256,2,360]{2,1,0:T(2,128)(2,1)}), bf16[256,2,360]{2,1,0:T(2,128)(2,1)S(1)}, u32[]{:S(2)}, u32[]{:S(2)}) %all-to-all-start.3) | async-done | bytes 368672 | tf_op jit(solution)/shard_map/all_to_all | solution.py:266
  126.6 8.7 %shard_map.84 = bf16[8,5,4,1152]{3,2,1,0:T(4,128)(2,1)S(1)} custom-call(f32[6,1152]{1,0:T(8,128)S(1)} %pad_maximum_fusion.3.mods, f32[2,1152]{1,0:T(2,128)S(1)} %tile.9.gain, bf16[1152,128]{1,0:T(8,128)(2,1)S(1)} %fusion.seg, bf16[160,1152]{1,0:T(8,128)(2,1)S(1)} %reshape.75.back, bf16[160,1152]{1,0:T(8,128)(2,1)S(1)} %reshape.76.res, ...), custom_call_target="tpu_custom_call" | custom-call | flops 1800000000 | bytes 15000000 | tf_op jit(solution)/shard_map/pallas_call | solution.py:190
  135.2 14.1 %all_to_all.30 = bf16[8,5,4,1152]{3,2,1,0:T(4,128)(2,1)S(1)} all-to-all(bf16[8,5,4,1152]{3,2,1,0:T(4,128)(2,1)S(1)} %shard_map.84), channel_id=1, replica_groups=mesh['zl'=4,'core'=2,'y'=4,'x'=4,'zh'=2] {'zl','core'}, dimensions={0} | all-to-all | bytes 737280 | tf_op jit(solution)/shard_map/all_to_all | solution.py:272
  (63 shorter events, 15.9 us)
Async XLA Ops:
  7.5 22.8 %collective-permute-start = (bf16[2,40,1152]{2,1,0:T(8,128)(2,1)S(1)}, bf16[2,40,1152]{2,1,0:T(8,128)(2,1)S(1)}, u32[]{:S(2)}, u32[]{:S(2)}) collective-permute-start(bf16[2,40,1152]{2,1,0:T(8,128)(2,1)S(1)} %dynamic-slice_bitcast_fusion), channel_id=1, source_target_pairs={{0,33},{1,32},{32,1},{33,0},{2,35},{3,34},{34,3},{35,2},{4,37},{5,... | collective-permute-start | bytes 552968 | tf_op jit(solution)/shard_map/ppermute | solution.py:225
  17.8 18.0 %collective-permute-start.1 = (bf16[36,2944]{1,0:T(8,128)(2,1)S(1)}, bf16[36,2944]{1,0:T(8,128)(2,1)S(1)}, u32[]{:S(2)}, u32[]{:S(2)}) collective-permute-start(bf16[36,2944]{1,0:T(8,128)(2,1)S(1)} %maximum_select_fusion), channel_id=1, source_target_pairs={{0,1},{1,0},{2,3},{3,2},{4,5},{5,4},{6,7},{7,6},{8,9},{9,8},{10,11... | collective-permute-start | bytes 635912 | tf_op jit(solution)/shard_map/ppermute | solution.py:230
  20.3 16.5 %copy-start.4 = (bf16[4,1,40,1152]{3,2,1,0:T(8,128)(2,1)S(1)}, bf16[4,1,40,1152]{3,2,1,0:T(8,128)(2,1)}, u32[]{:S(2)}) copy-start(bf16[4,1,40,1152]{3,2,1,0:T(8,128)(2,1)} %param.8) | copy-start | bytes 1105924
  21.1 9.1 %all-to-all-start = ((bf16[4,36,432]{2,1,0:T(8,128)(2,1)}), bf16[4,36,432]{2,1,0:T(8,128)(2,1)S(1)}, u32[]{:S(2)}, u32[]{:S(2)}) async-start(bf16[4,36,432]{2,1,0:T(8,128)(2,1)} %reshape.78), calls=%async_computation | async-start | bytes 327680 | tf_op jit(solution)/shard_map/all_to_all | solution.py:235
  25.0 101.6 %all-gather.2.cloned.1.call-start = ((), (), s32[]{:S(2)}) async-start(), calls=%async_computation.6 | async-start | bytes 13989888 | tf_op jit(solution)/shard_map/all_gather | solution.py:246
  37.6 12.2 %all-to-all-start.1 = ((bf16[4,40,1152]{2,1,0:T(8,128)(2,1)}), bf16[4,40,1152]{2,1,0:T(8,128)(2,1)S(1)}, u32[]{:S(2)}, u32[]{:S(2)}) async-start(bf16[4,40,1152]{2,1,0:T(8,128)(2,1)} %pad_maximum_fusion.1), calls=%async_computation.1 | async-start | bytes 737280 | tf_op jit(solution)/shard_map/all_to_all | solution.py:241
  43.2 12.9 %collective-permute-start.2 = (bf16[4,36,432]{2,1,0:T(8,128)(2,1)S(1)}, bf16[4,36,432]{2,1,0:T(8,128)(2,1)S(1)}, u32[]{:S(2)}, u32[]{:S(2)}) collective-permute-start(bf16[4,36,432]{2,1,0:T(8,128)(2,1)S(1)} %all-to-all-done), channel_id=1, source_target_pairs={{0,1},{1,0},{2,3},{3,2},{4,5},{5,4},{6,7},{7,6},{8,9},{9,8},{10,11... | collective-permute-start | bytes 373256 | tf_op jit(solution)/shard_map/ppermute | solution.py:237
  49.7 0.7 copy-start.5
  56.1 24.1 %all-to-all-start.2 = ((bf16[4,160,1152]{2,1,0:T(8,128)(2,1)}), bf16[4,160,1152]{2,1,0:T(8,128)(2,1)S(1)}, u32[]{:S(2)}, u32[]{:S(2)}) async-start(bf16[4,160,1152]{2,1,0:T(8,128)(2,1)} %bitcast.37), calls=%async_computation.2 | async-start | bytes 2949120 | tf_op jit(solution)/shard_map/all_to_all | solution.py:254
  59.7 25.3 %copy-start.8 = (f32[4,72]{1,0:T(4,128)S(1)}, f32[4,72]{1,0:T(4,128)}, u32[]{:S(2)}) copy-start(f32[4,72]{1,0:T(4,128)} %param.11) | copy-start | bytes 3460
  59.9 9.4 %collective-permute-start.3 = (bf16[288,432]{1,0:T(8,128)(2,1)S(1)}, bf16[288,432]{1,0:T(8,128)(2,1)S(1)}, u32[]{:S(2)}, u32[]{:S(2)}) collective-permute-start(bf16[288,432]{1,0:T(8,128)(2,1)S(1)} %reshape.71.w0), channel_id=1, source_target_pairs={{8,0},{16,8},{24,16},{0,24},{9,1},{17,9},{25,17},{1,25},{10,2},{18... | collective-permute-start | bytes 746504 | tf_op jit(solution)/shard_map/ppermute | solution.py:251
  62.8 8.8 %collective-permute-start.4 = (bf16[288,432]{1,0:T(8,128)(2,1)S(1)}, bf16[288,432]{1,0:T(8,128)(2,1)S(1)}, u32[]{:S(2)}, u32[]{:S(2)}) collective-permute-start(bf16[288,432]{1,0:T(8,128)(2,1)S(1)} %reshape.71.w0), channel_id=1, source_target_pairs={{16,0},{24,8},{0,16},{8,24},{17,1},{25,9},{1,17},{9,25},{18,2},{26... | collective-permute-start | bytes 746504 | tf_op jit(solution)/shard_map/ppermute | solution.py:251
  63.4 16.2 %collective-permute-start.5 = (bf16[288,432]{1,0:T(8,128)(2,1)S(1)}, bf16[288,432]{1,0:T(8,128)(2,1)S(1)}, u32[]{:S(2)}, u32[]{:S(2)}) collective-permute-start(bf16[288,432]{1,0:T(8,128)(2,1)S(1)} %reshape.71.w0), channel_id=1, source_target_pairs={{24,0},{0,8},{8,16},{16,24},{25,1},{1,9},{9,17},{17,25},{26,2},{2,... | collective-permute-start | bytes 746504 | tf_op jit(solution)/shard_map/ppermute | solution.py:251
  71.6 0.7 copy-start
  79.6 0.7 copy-start.2
  80.3 5.0 %collective-permute-start.6 = (bf16[640,1152]{1,0:T(8,128)(2,1)S(1)}, bf16[640,1152]{1,0:T(8,128)(2,1)S(1)}, u32[]{:S(2)}, u32[]{:S(2)}) collective-permute-start(bf16[640,1152]{1,0:T(8,128)(2,1)S(1)} %bitcast.35), channel_id=1, source_target_pairs={{0,32},{32,0},{1,33},{33,1},{2,34},{34,2},{3,35},{35,3},{4,36},{36... | collective-permute-start | bytes 4423688 | tf_op jit(solution)/shard_map/ppermute | solution.py:256
  80.8 16.1 %all-to-all-start.4 = ((bf16[8,5,4,1152]{3,2,1,0:T(4,128)(2,1)}), bf16[8,5,4,1152]{3,2,1,0:T(4,128)(2,1)}, u32[]{:S(2)}, u32[]{:S(2)}) async-start(bf16[8,5,4,1152]{3,2,1,0:T(4,128)(2,1)} %bitcast.41), calls=%async_computation.4 | async-start | bytes 737280 | tf_op jit(solution)/shard_map/all_to_all | solution.py:258
  85.3 1.0 copy-start.1
  86.3 1.0 copy-start.3
  95.2 11.1 %copy-start.6 = (f32[3,1152]{1,0:T(4,128)S(1)}, f32[3,1152]{1,0:T(4,128)}, u32[]{:S(2)}) copy-start(f32[3,1152]{1,0:T(4,128)} %mod.1) | copy-start | bytes 41476
  95.2 11.1 %copy-start.7 = (f32[3,1152]{1,0:T(4,128)S(1)}, f32[3,1152]{1,0:T(4,128)}, u32[]{:S(2)}) copy-start(f32[3,1152]{1,0:T(4,128)} %param.10) | copy-start | bytes 41476
  96.9 27.9 %all-to-all-start.3 = ((bf16[256,2,360]{2,1,0:T(2,128)(2,1)}), bf16[256,2,360]{2,1,0:T(2,128)(2,1)S(1)}, u32[]{:S(2)}, u32[]{:S(2)}) async-start(bf16[256,2,360]{2,1,0:T(2,128)(2,1)} %reshape.79), calls=%async_computation.3 | async-start | bytes 786432 | tf_op jit(solution)/shard_map/all_to_all | solution.py:266
Sparse Core Ops, SparseCore 0:
  36.8 80.4 all-gather.1
